TPU v7x, 32 devices: a whole 2x2x4 slice. The times are simulated.
32 devices in a mesh: dp: 8 (over y, x, core), ctx: 4 (over z).
Axes of the slice: x: 2, y: 2, z: 4, core: 2. Of those that a mesh axis runs over, the one named last changes fastest.
Arguments:
- tokens: bfloat16 [8, 1024, 2048], P('dp', 'ctx'), may hold values from -6 to 6
- cotangent: bfloat16 [8, 1024, 2048], P('dp', 'ctx'), may hold values from -6 to 6
- qkv_weight: bfloat16 [2048, 6144], P(('dp', 'ctx')), may hold values from -0.125 to 0.125
- out_weight: bfloat16 [2048, 2048], P(('dp', 'ctx')), may hold values from -0.375 to 0.375
- up_weight: bfloat16 [2048, 8192], P(('dp', 'ctx')), may hold values from -0.125 to 0.125
- down_weight: bfloat16 [8192, 2048], P(('dp', 'ctx')), may hold values from -0.0625 to 0.0625
- vectors: bfloat16 [12, 2048], P(None, ('dp', 'ctx')), may hold values from -0.5 to 1.65, as said below
- qkv_moments: float32 [2, 2048, 6144], P(None, ('dp', 'ctx')), may hold values from -0.02 to 0.02, as said below
- out_moments: float32 [2, 2048, 2048], P(None, ('dp', 'ctx')), may hold values from -0.02 to 0.02, as said below
- up_moments: float32 [2, 2048, 8192], P(None, ('dp', 'ctx')), may hold values from -0.02 to 0.02, as said below
- down_moments: float32 [2, 8192, 2048], P(None, ('dp', 'ctx')), may hold values from -0.02 to 0.02, as said below
- vector_moments: float32 [2, 12, 2048], P(None, None, ('dp', 'ctx')), may hold values from -0.02 to 0.02, as said below
- step: int32 [], replicated, may hold values from 1 to 20
- hyper: float32 [5], replicated, may hold values from 0.002 to 200, as said below
Outputs:
- activations: bfloat16 [8, 1024, 2048], P('dp', 'ctx')
- input_grad: bfloat16 [8, 1024, 2048], P('dp', 'ctx')
- grad_norm: float32 [], replicated
- new_qkv_weight: bfloat16 [2048, 6144], P(('dp', 'ctx'))
- out_step: float32 [2048, 2048], P(('dp', 'ctx'))
- new_up_weight: bfloat16 [2048, 8192], P(('dp', 'ctx'))
- new_down_weight: bfloat16 [8192, 2048], P(('dp', 'ctx'))
- vector_step: float32 [12, 2048], P(None, ('dp', 'ctx'))
- new_qkv_moments: float32 [2, 2048, 6144], P(None, ('dp', 'ctx'))
- new_out_moments: float32 [2, 2048, 2048], P(None, ('dp', 'ctx'))
- new_up_moments: float32 [2, 2048, 8192], P(None, ('dp', 'ctx'))
- new_down_moments: float32 [2, 8192, 2048], P(None, ('dp', 'ctx'))
- new_vector_moments: float32 [2, 12, 2048], P(None, None, ('dp', 'ctx'))
Inputs may be any that keep to these rules, and one draw needn't show every extreme that they name: `vectors`: rows 0 and 5 are positive gains, the others biases. `qkv_moments`: entry 0 of the first dimension is a first moment, entry 1 a positive second moment. `out_moments`: entry 0 of the first dimension is a first moment, entry 1 a positive second moment. `up_moments`: entry 0 of the first dimension is a first moment, entry 1 a positive second moment. `down_moments`: entry 0 of the first dimension is a first moment, entry 1 a positive second moment. `vector_moments`: entry 0 of the first dimension is a first moment, entry 1 a positive second moment. `hyper`: rate in 0.002 to 0.004, decay 0.05 to 0.2, first decay 0.85 to 0.95, second 0.95 to 0.999, clip maximum 50 to 200.
All inputs are finite; a program needn't handle non-finite values.
Results may differ from a plain program's by a relative error of at most 0.0095.
Values may be sent and summed in bfloat16 or wider, within the bound.
No kernel may reach another device: no remote copies, remote signals or barrier semaphores. Data moves between devices by JAX's collectives and lax.ppermute only.
A program may use at most 576 MiB of HBM per device.

v0:
```python
from functools import partial

import jax
import jax.numpy as jnp
from jax import lax
from jax.sharding import PartitionSpec as P

HEADS = 16
HEAD_DIM = 128


EPS_NORM = 1e-05
EPS_ADAM = 1e-08
MASKED = -1e30


def norm_forward(values, gain, shift):
    centre = values - jnp.mean(values, axis=-1, keepdims=True)
    factor = lax.rsqrt(jnp.mean(centre * centre, axis=-1, keepdims=True) + EPS_NORM)
    normed = centre * factor
    return (normed * gain + shift, normed, factor)


def norm_backward(incoming, normed, factor, gain):
    scaled = incoming * gain
    input_grad = factor * (
        scaled
        - jnp.mean(scaled, axis=-1, keepdims=True)
        - normed * jnp.mean(scaled * normed, axis=-1, keepdims=True)
    )
    return (input_grad, jnp.sum(incoming * normed, axis=0), jnp.sum(incoming, axis=0))


def position_bias(head_count, block, length, ctx_id):
    query_pos = ctx_id * block + jnp.arange(block, dtype=jnp.int32)
    key_pos = jnp.arange(length, dtype=jnp.int32)
    distance = jnp.abs(query_pos[:, None] - key_pos[None, :]).astype(jnp.float32)
    slopes = jnp.exp2(-8.0 * (jnp.arange(head_count).astype(jnp.float32) + 1.0) / head_count)
    allowed = key_pos[None, :] < (ctx_id + 1) * block
    return (-slopes[:, None, None] * distance[None], allowed)


def adam_update(weight, moments, grad, clip_factor, step, hyper):
    step_float = step.astype(jnp.float32)
    scaled = grad * clip_factor
    first_moment = hyper[2] * moments[0] + (1.0 - hyper[2]) * scaled
    second_moment = hyper[3] * moments[1] + (1.0 - hyper[3]) * scaled * scaled
    fix_first = 1.0 - hyper[2] ** step_float
    fix_second = 1.0 - hyper[3] ** step_float
    current = weight.astype(jnp.float32)
    change = -hyper[0] * (
        first_moment / fix_first / (jnp.sqrt(second_moment / fix_second) + EPS_ADAM)
        + hyper[1] * current
    )
    updated = current + change
    return (updated.astype(jnp.bfloat16), change, jnp.stack([first_moment, second_moment]))


def finish(owned, shards, moments, step, hyper):
    local_squares = jnp.float32(0.0)
    for grad in owned:
        local_squares = local_squares + jnp.sum(grad * grad)
    grad_norm = jnp.sqrt(lax.psum(local_squares, ("dp", "ctx")))
    clip_factor = jnp.minimum(1.0, hyper[4] / (grad_norm + 1e-06))
    news = [
        adam_update(w, m, g, clip_factor, step, hyper) for w, m, g in zip(shards, moments, owned)
    ]
    return (grad_norm, news)


def assemble(activations, input_grad, grad_norm, news):
    return (
        activations,
        input_grad,
        grad_norm,
        news[0][0],
        news[1][1],
        news[2][0],
        news[3][0],
        news[4][1],
        news[0][2],
        news[1][2],
        news[2][2],
        news[3][2],
        news[4][2],
    )


def body(
    tokens,
    cotangent,
    qkv_weight,
    out_weight,
    up_weight,
    down_weight,
    vectors,
    qkv_moments,
    out_moments,
    up_moments,
    down_moments,
    vector_moments,
    step,
    hyper,
):
    shards = (qkv_weight, out_weight, up_weight, down_weight, vectors)
    moments = (qkv_moments, out_moments, up_moments, down_moments, vector_moments)
    seq_count, block, model_width = tokens.shape
    row_count = seq_count * block
    score_scale = HEAD_DIM ** (-0.5)
    w_qkv, w_out, w_up, w_down, vec_low = (
        lax.all_gather(qkv_weight, ("dp", "ctx"), axis=0, tiled=True),
        lax.all_gather(out_weight, ("dp", "ctx"), axis=0, tiled=True),
        lax.all_gather(up_weight, ("dp", "ctx"), axis=0, tiled=True),
        lax.all_gather(down_weight, ("dp", "ctx"), axis=0, tiled=True),
        lax.all_gather(vectors, ("dp", "ctx"), axis=1, tiled=True),
    )
    vecs = vec_low.astype(jnp.float32)
    ctx_id = lax.axis_index("ctx")
    length = block * lax.axis_size("ctx")
    rows_in = tokens.reshape(row_count, model_width).astype(jnp.float32)
    normed_a, hat_one, factor_one = norm_forward(rows_in, vecs[0], vecs[1])
    normed_a = normed_a.astype(jnp.bfloat16)
    qkv = jnp.dot(normed_a, w_qkv, preferred_element_type=jnp.float32)
    query_low = (qkv[:, :model_width] + vecs[2]).astype(jnp.bfloat16)
    key_low = qkv[:, model_width : 2 * model_width].astype(jnp.bfloat16)
    value_low = (qkv[:, 2 * model_width :] + vecs[3]).astype(jnp.bfloat16)
    paired = jnp.stack([key_low, value_low], axis=1).reshape(seq_count, block, 2, model_width)
    gathered = lax.all_gather(paired, "ctx", axis=1, tiled=True)
    keys = gathered[:, :, 0].reshape(seq_count, length, HEADS, HEAD_DIM)
    values = gathered[:, :, 1].reshape(seq_count, length, HEADS, HEAD_DIM)
    queries = query_low.reshape(seq_count, block, HEADS, HEAD_DIM)
    bias_table, allowed = position_bias(HEADS, block, length, ctx_id)

    def scores_of():
        raw = (
            jnp.einsum("sbhe,slhe->shbl", queries, keys, preferred_element_type=jnp.float32)
            * score_scale
            + bias_table
        )
        return jnp.where(allowed, raw, MASKED)

    scores = scores_of()
    row_max = jnp.max(scores, axis=-1, keepdims=True)
    expo = jnp.exp(scores - row_max)
    denominator = jnp.sum(expo, axis=-1, keepdims=True)
    probs = expo / denominator
    log_total = row_max + jnp.log(denominator)
    context = jnp.einsum(
        "shbl,slhe->sbhe", probs.astype(jnp.bfloat16), values, preferred_element_type=jnp.float32
    )
    context = context.reshape(row_count, model_width).astype(jnp.bfloat16)
    residual = rows_in + jnp.dot(context, w_out, preferred_element_type=jnp.float32) + vecs[4]
    normed_b, hat_two, factor_two = norm_forward(residual, vecs[5], vecs[6])
    normed_b = normed_b.astype(jnp.bfloat16)
    up_bias = vecs[8:12].reshape(-1)
    pre_act = jnp.dot(normed_b, w_up, preferred_element_type=jnp.float32) + up_bias
    hidden = jax.nn.gelu(pre_act, approximate=True).astype(jnp.bfloat16)
    result = residual + jnp.dot(hidden, w_down, preferred_element_type=jnp.float32) + vecs[7]
    activations = result.astype(jnp.bfloat16).reshape(seq_count, block, model_width)
    grad_top = cotangent.reshape(row_count, model_width).astype(jnp.float32)
    grad_mlp = cotangent.reshape(row_count, model_width)
    down_bias_grad = jnp.sum(grad_top, axis=0)
    grad_down = jnp.dot(hidden.T, grad_mlp, preferred_element_type=jnp.float32)
    grad_hidden = jnp.dot(grad_mlp, w_down.T, preferred_element_type=jnp.float32)
    _, gelu_pull = jax.vjp(partial(jax.nn.gelu, approximate=True), pre_act)
    grad_pre = gelu_pull(grad_hidden)[0].astype(jnp.bfloat16)
    up_bias_grad = jnp.sum(grad_pre.astype(jnp.float32), axis=0)
    grad_up = jnp.dot(normed_b.T, grad_pre, preferred_element_type=jnp.float32)
    grad_normed_b = jnp.dot(grad_pre, w_up.T, preferred_element_type=jnp.float32)
    through_two, gain_two_grad, shift_two_grad = norm_backward(
        grad_normed_b, hat_two, factor_two, vecs[5]
    )
    grad_residual = grad_top + through_two
    owned_up, owned_down = (
        lax.psum_scatter(grad_up, ("dp", "ctx"), scatter_dimension=0, tiled=True),
        lax.psum_scatter(grad_down, ("dp", "ctx"), scatter_dimension=0, tiled=True),
    )
    grad_attn = grad_residual.astype(jnp.bfloat16)
    out_bias_grad = jnp.sum(grad_attn.astype(jnp.float32), axis=0)
    grad_out = jnp.dot(context.T, grad_attn, preferred_element_type=jnp.float32)
    grad_context = jnp.dot(grad_attn, w_out.T, preferred_element_type=jnp.float32).astype(
        jnp.bfloat16
    )
    grad_context = grad_context.reshape(seq_count, block, HEADS, HEAD_DIM)
    scores = scores_of()
    probs = jnp.exp(scores - log_total)
    grad_values_all = jnp.einsum(
        "shbl,sbhe->slhe",
        probs.astype(jnp.bfloat16),
        grad_context,
        preferred_element_type=jnp.float32,
    )
    grad_probs = jnp.einsum(
        "sbhe,slhe->shbl", grad_context, values, preferred_element_type=jnp.float32
    )
    grad_scores = (
        probs * (grad_probs - jnp.sum(probs * grad_probs, axis=-1, keepdims=True))
    ).astype(jnp.bfloat16)
    grad_queries = (
        jnp.einsum("shbl,slhe->sbhe", grad_scores, keys, preferred_element_type=jnp.float32)
        * score_scale
    )
    grad_keys_all = (
        jnp.einsum("shbl,sbhe->slhe", grad_scores, queries, preferred_element_type=jnp.float32)
        * score_scale
    )
    pair_terms = jnp.stack(
        [
            grad_keys_all.reshape(seq_count, length, model_width),
            grad_values_all.reshape(seq_count, length, model_width),
        ],
        axis=2,
    )
    pair_owned = lax.psum_scatter(pair_terms, "ctx", scatter_dimension=1, tiled=True)
    grad_key_low = pair_owned[:, :, 0].reshape(row_count, model_width).astype(jnp.bfloat16)
    grad_value_low = pair_owned[:, :, 1].reshape(row_count, model_width).astype(jnp.bfloat16)
    grad_query_low = grad_queries.reshape(row_count, model_width).astype(jnp.bfloat16)
    grad_qkv = jnp.concatenate([grad_query_low, grad_key_low, grad_value_low], axis=1)
    grad_qkv_weight = jnp.dot(normed_a.T, grad_qkv, preferred_element_type=jnp.float32)
    grad_normed_a = jnp.dot(grad_qkv, w_qkv.T, preferred_element_type=jnp.float32)
    through_one, gain_one_grad, shift_one_grad = norm_backward(
        grad_normed_a, hat_one, factor_one, vecs[0]
    )
    input_grad = (
        (grad_residual + through_one).astype(jnp.bfloat16).reshape(seq_count, block, model_width)
    )
    head_rows = jnp.stack(
        [
            gain_one_grad,
            shift_one_grad,
            jnp.sum(grad_query_low.astype(jnp.float32), axis=0),
            jnp.sum(grad_value_low.astype(jnp.float32), axis=0),
            out_bias_grad,
            gain_two_grad,
            shift_two_grad,
            down_bias_grad,
        ]
    )
    vector_grad = jnp.concatenate([head_rows, up_bias_grad.reshape(4, model_width)], axis=0)
    owned_qkv, owned_out, owned_vec = (
        lax.psum_scatter(grad_qkv_weight, ("dp", "ctx"), scatter_dimension=0, tiled=True),
        lax.psum_scatter(grad_out, ("dp", "ctx"), scatter_dimension=0, tiled=True),
        lax.psum_scatter(vector_grad, ("dp", "ctx"), scatter_dimension=1, tiled=True),
    )
    owned = (owned_qkv, owned_out, owned_up, owned_down, owned_vec)
    grad_norm, news = finish(owned, shards, moments, step, hyper)
    return assemble(activations, input_grad, grad_norm, news)


def solution(mesh):
    return jax.shard_map(
        body,
        mesh=mesh,
        in_specs=(
            P("dp", "ctx", None),
            P("dp", "ctx", None),
            P(("dp", "ctx"), None),
            P(("dp", "ctx"), None),
            P(("dp", "ctx"), None),
            P(("dp", "ctx"), None),
            P(None, ("dp", "ctx")),
            P(None, ("dp", "ctx"), None),
            P(None, ("dp", "ctx"), None),
            P(None, ("dp", "ctx"), None),
            P(None, ("dp", "ctx"), None),
            P(None, None, ("dp", "ctx")),
            P(),
            P(),
        ),
        out_specs=(
            P("dp", "ctx", None),
            P("dp", "ctx", None),
            P(),
            P(("dp", "ctx"), None),
            P(("dp", "ctx"), None),
            P(("dp", "ctx"), None),
            P(("dp", "ctx"), None),
            P(None, ("dp", "ctx")),
            P(None, ("dp", "ctx"), None),
            P(None, ("dp", "ctx"), None),
            P(None, ("dp", "ctx"), None),
            P(None, ("dp", "ctx"), None),
            P(None, None, ("dp", "ctx")),
        ),
        check_vma=False,
    )
```

profile of v0, /device:TPU:0, one launch (start us, length us, event | category | flops | bytes accessed | tf_op | source)
XLA Modules:
  0.0 5037.9 jit_solution(6201582707057280063)
XLA Ops:
  8.0 72.8 %all-gather.1 = bf16[32,64,12]{1,2,0:T(8,128)(2,1)S(1)} all-gather(bf16[1,64,12]{1,2,0:T(8,128)(2,1)} %bitcast.273), channel_id=1, replica_groups=mesh['dp'=8,'ctx'=4] {'dp','ctx'}, dimensions={0}, use_global_device_ids=true | all-gather | bytes 50688 | tf_op jit(solution)/shard_map/all_gather | solution.py:115
  82.3 87.1 %all-gather.8.cloned.1.call-done = bf16[2048,6144]{1,0:T(8,128)(2,1)} async-done(((bf16[64,6144]{1,0:T(8,128)(2,1)}), bf16[2048,6144]{1,0:T(8,128)(2,1)}) %all-gather.8.cloned.1.call-update) | async-done | bytes 25165840 | tf_op jit(solution)/shard_map/all_gather | solution.py:111
  169.4 11.7 fusion.86
  187.3 144.0 %all-gather.16.cloned.1.call-done = bf16[1024,2,2048]{2,0,1:T(8,128)(2,1)} async-done(((bf16[256,2,2048]{2,0,1:T(8,128)(2,1)}), bf16[1024,2,2048]{2,0,1:T(8,128)(2,1)}) %all-gather.16.cloned.1.call-update) | async-done | bytes 8388624 | tf_op jit(solution)/shard_map/all_gather | solution.py:128
  331.3 6.1 slice_bitcast_fusion
  337.4 6.4 copy.79
  343.9 5.8 copy.81
  349.6 4.5 fusion.92
  354.1 3.6 fusion
  357.7 3.5 copy-done
  361.2 9.5 fusion.51
  370.8 39.1 all-gather.10.cloned.1.call-done
  409.8 6.2 fusion.93
  416.4 189.6 %all-gather.12.cloned.1.call-done = bf16[2048,8192]{1,0:T(8,128)(2,1)} async-done(((bf16[64,8192]{1,0:T(8,128)(2,1)}), bf16[2048,8192]{1,0:T(8,128)(2,1)}) %all-gather.12.cloned.1.call-update) | async-done | bytes 33554448 | tf_op jit(solution)/shard_map/all_gather | solution.py:113
  606.1 18.4 convolution_add_fusion
  624.4 177.4 %all-gather.14.cloned.1.call-done = bf16[8192,2048]{1,0:T(8,128)(2,1)} async-done(((bf16[256,2048]{1,0:T(8,128)(2,1)}), bf16[8192,2048]{1,0:T(8,128)(2,1)}) %all-gather.14.cloned.1.call-update) | async-done | bytes 33554448 | tf_op jit(solution)/shard_map/all_gather | solution.py:114
  801.9 21.1 convert_reduce_fusion
  822.9 17.9 multiply_reduce_fusion.1
  840.9 3.0 convert_reduce_fusion.3
  845.2 6.7 convolution_convert_fusion
  854.2 12.4 fusion.9
  866.6 15.1 multiply_reduce_fusion
  881.7 12.3 multiply_convert_fusion
  895.6 2.6 copy-done.1
  900.4 6.3 pad_maximum_fusion
  906.7 10.1 fusion.82
  916.9 8.6 convert_reduce_fusion.5
  925.5 259.8 %reduce-scatter.9.cloned.1.call-done = f32[1,256,2,2048]{1,3,2,0:T(8,128)} async-done(((f32[1,1024,2,2048]{1,3,2,0:T(8,128)}), f32[1,256,2,2048]{1,3,2,0:T(8,128)}) %reduce-scatter.9.cloned.1.call-update) | async-done | bytes 4194320 | tf_op jit(solution)/shard_map/reduce_scatter | solution.py:214
  1189.6 13.4 fusion.35
  1204.6 19.9 fusion.54
  1225.2 25.8 fusion.88
  1251.1 27.8 fusion.59
  1284.0 19.7 fusion.27
  1303.8 248.9 %reduce-scatter.13.cloned.1.call-done = f32[64,2048]{1,0:T(8,128)} async-done(((f32[2048,2048]{1,0:T(8,128)}), f32[64,2048]{1,0:T(8,128)}) %reduce-scatter.13.cloned.1.call-update) | async-done | bytes 524304 | tf_op jit(solution)/shard_map/reduce_scatter | solution.py:242
  1554.5 134.8 %reduce-scatter.19.cloned.1.call-done = f32[64,12]{1,0:T(8,128)} async-done(((f32[2048,12]{1,0:T(8,128)}), f32[64,12]{1,0:T(8,128)}) %reduce-scatter.19.cloned.1.call-update) | async-done | bytes 3088
  1690.7 432.8 %reduce-scatter.11.cloned.1.call-done = f32[64,6144]{1,0:T(8,128)} async-done(((f32[2048,6144]{1,0:T(8,128)}), f32[64,6144]{1,0:T(8,128)}) %reduce-scatter.11.cloned.1.call-update) | async-done | bytes 1572880 | tf_op jit(solution)/shard_map/reduce_scatter | solution.py:241
  2127.3 1408.1 %reduce-scatter.15.cloned.1.call-done = f32[64,8192]{1,0:T(8,128)} async-done(((f32[2048,8192]{1,0:T(8,128)}), f32[64,8192]{1,0:T(8,128)}) %reduce-scatter.15.cloned.1.call-update) | async-done | bytes 2097168 | tf_op jit(solution)/shard_map/reduce_scatter | solution.py:175
  3535.4 2.7 multiply_reduce_fusion.3
  3538.8 1409.6 %reduce-scatter.17.cloned.1.call-done = f32[256,2048]{1,0:T(8,128)} async-done(((f32[8192,2048]{1,0:T(8,128)}), f32[256,2048]{1,0:T(8,128)}) %reduce-scatter.17.cloned.1.call-update) | async-done | bytes 2097168 | tf_op jit(solution)/shard_map/reduce_scatter | solution.py:176
  4948.4 2.7 multiply_reduce_fusion.2
  4952.5 3.4 fusion.58
  4955.8 39.7 psum.7
  4996.9 2.5 fusion.78
  5000.0 6.6 fusion.68
  5008.6 4.2 fusion.72
  5013.9 4.6 fusion.66
  5018.5 2.4 pad_maximum_fusion.1
  5023.1 4.6 fusion.67
  (139 shorter events, 37.6 us)
Async XLA Ops:
  7.2 73.8 %copy-start.3 = (bf16[1,256,2048]{2,1,0:T(8,128)(2,1)S(1)}, bf16[1,256,2048]{2,1,0:T(8,128)(2,1)}, u32[]{:S(2)}) copy-start(bf16[1,256,2048]{2,1,0:T(8,128)(2,1)} %param.14) | copy-start | bytes 3145732
  7.2 162.2 %all-gather.8.cloned.1.call-start = ((), (), s32[]{:S(2)}) async-start(), calls=%async_computation.6 | async-start | bytes 25952256 | tf_op jit(solution)/shard_map/all_gather | solution.py:111
  7.9 323.4 %all-gather.16.cloned.1.call-start = ((), (), s32[]{:S(2)}) async-start(), calls=%async_computation.15 | async-start | bytes 10485760 | tf_op jit(solution)/shard_map/all_gather | solution.py:128
  81.2 99.9 %copy-start.30 = (f32[256]{0:T(256)}, f32[256]{0:T(256)S(1)}, u32[]{:S(2)}) copy-start(f32[256]{0:T(256)S(1)} %broadcast_multiply_fusion.6) | copy-start | bytes 3076
  81.6 99.5 %copy-start.32 = (f32[256]{0:T(256)}, f32[256]{0:T(256)S(1)}, u32[]{:S(2)}) copy-start(f32[256]{0:T(256)S(1)} %add_rsqrt_fusion.1) | copy-start | bytes 3076
  82.3 98.9 %copy-start.24 = (f32[1,2048]{1,0:T(1,128)}, f32[1,2048]{1,0:T(1,128)S(1)}, u32[]{:S(2)}) copy-start(f32[1,2048]{1,0:T(1,128)S(1)} %get-tuple-element.88) | copy-start | bytes 24580
  82.3 98.9 %copy-start.26 = (f32[1,2048]{1,0:T(1,128)}, f32[1,2048]{1,0:T(1,128)S(1)}, u32[]{:S(2)}) copy-start(f32[1,2048]{1,0:T(1,128)S(1)} %get-tuple-element.87) | copy-start | bytes 24580
  82.3 523.8 %copy-start.28 = (f32[1,2048]{1,0:T(1,128)}, f32[1,2048]{1,0:T(1,128)S(1)}, u32[]{:S(2)}) copy-start(f32[1,2048]{1,0:T(1,128)S(1)} %get-tuple-element.83) | copy-start | bytes 24580
  183.3 226.5 %all-gather.10.cloned.1.call-start = ((), (), s32[]{:S(2)}) async-start(), calls=%async_computation.7 | async-start | bytes 8650752 | tf_op jit(solution)/shard_map/all_gather | solution.py:112
  184.1 422.0 %all-gather.12.cloned.1.call-start = ((), (), s32[]{:S(2)}) async-start(), calls=%async_computation.8 | async-start | bytes 34603008 | tf_op jit(solution)/shard_map/all_gather | solution.py:113
  184.6 617.3 %all-gather.14.cloned.1.call-start = ((), (), s32[]{:S(2)}) async-start(), calls=%async_computation.9 | async-start | bytes 34603008 | tf_op jit(solution)/shard_map/all_gather | solution.py:114
  185.2 1000.1 %reduce-scatter.9.cloned.1.call-start = ((), (), s32[]{:S(2)}) async-start(), calls=%async_computation.10 | async-start | bytes 20971520 | tf_op jit(solution)/shard_map/reduce_scatter | solution.py:214
  187.3 162.4 %copy-start.11 = (bf16[256,2048]{0,1:T(8,128)(2,1)}, bf16[256,2048]{0,1:T(8,128)(2,1)S(1)}, u32[]{:S(2)}) copy-start(bf16[256,2048]{0,1:T(8,128)(2,1)S(1)} %copy.78) | copy-start | bytes 3145732
  343.9 5.8 copy-start.6
  343.9 5.8 copy-start.23
  354.1 7.1 copy-start
  354.1 7.1 copy-start.7
  843.9 1.3 copy-start.4
  854.2 12.4 copy-start.8
  881.7 12.3 copy-start.12
  893.9 4.3 copy-start.1
  894.0 6.4 copy-start.2
  906.7 646.0 %reduce-scatter.13.cloned.1.call-start = ((), (), s32[]{:S(2)}) async-start(), calls=%async_computation.12 | async-start | bytes 17301504 | tf_op jit(solution)/shard_map/reduce_scatter | solution.py:242
  916.8 772.5 %reduce-scatter.19.cloned.1.call-start = ((), (), s32[]{:S(2)}) async-start(), calls=%async_computation.16 | async-start | bytes 1081344
  1188.1 1.5 copy-start.15
  1188.1 1.5 copy-start.25
  1188.1 1.5 copy-start.31
  1188.1 1.5 copy-start.33
  1188.3 14.7 copy-start.18
  1188.3 14.7 copy-start.19
  1203.0 1.6 copy-start.27
  1204.5 919.1 %reduce-scatter.11.cloned.1.call-start = ((), (), s32[]{:S(2)}) async-start(), calls=%async_computation.11 | async-start | bytes 51904512 | tf_op jit(solution)/shard_map/reduce_scatter | solution.py:241
  1224.5 0.7 copy-start.29
  1224.5 2310.9 %reduce-scatter.15.cloned.1.call-start = ((), (), s32[]{:S(2)}) async-start(), calls=%async_computation.13 | async-start | bytes 69206016 | tf_op jit(solution)/shard_map/reduce_scatter | solution.py:175
  1251.0 3697.4 %reduce-scatter.17.cloned.1.call-start = ((), (), s32[]{:S(2)}) async-start(), calls=%async_computation.14 | async-start | bytes 69206016 | tf_op jit(solution)/shard_map/reduce_scatter | solution.py:176
  1278.9 5.1 copy-start.36
  1278.9 5.2 copy-start.37
  2127.3 2825.2 %copy-start.5 = (f32[256,2048]{1,0:T(8,128)S(1)}, f32[256,2048]{1,0:T(8,128)}, u32[]{:S(2)}) copy-start(f32[256,2048]{1,0:T(8,128)} %copy-done.4) | copy-start | bytes 6291460
  4952.5 44.5 copy-start.34
  5006.6 2.0 copy-start.20
  5006.6 2.0 copy-start.21
  5006.6 2.0 copy-start.22
  5006.6 7.3 copy-start.13
  5008.6 5.3 copy-start.9
  5008.6 5.3 copy-start.16
  5018.5 2.4 copy-start.10
  5018.5 4.3 copy-start.14
  5018.5 4.6 copy-start.17
  (1 other events, 0.7 us)
Sparse Core Ops, SparseCore 0:
  10.9 158.4 all-gather.7
  183.4 147.7 all-gather.15
  334.2 75.5 all-gather.9
  412.6 193.3 all-gather.11
  608.8 193.0 all-gather.13
  906.8 278.4 reduce-scatter.8
  1187.7 364.9 reduce-scatter.12
  1555.6 133.6 reduce-scatter.18
  1695.7 427.7 reduce-scatter.10
  2125.8 1409.5 reduce-scatter.14
  3537.8 1410.6 reduce-scatter.16
where the time goes:
time: 5040 us
  waiting for transfers between devices  4530 us (90%)
  matrix products  250 us (5%)
  blocking collectives  113 us (2%)
  other arithmetic  76.1 us (2%)
    reduce_scatter x1, waiting for transfers between devices, body(): lax.psum_scatter(grad_down, ('dp', 'ctx'), scatter_dimension=0, tiled=True)  1410 us
    reduce_scatter x1, waiting for transfers between devices, body(): lax.psum_scatter(grad_up, ('dp', 'ctx'), scatter_dimension=0, tiled=True)  1410 us
    reduce_scatter x1, waiting for transfers between devices, body(): lax.psum_scatter(grad_qkv_weight, ('dp', 'ctx'), scatter_dimension=0, til...  433 us
    reduce_scatter x1, waiting for transfers between devices, body(): lax.psum_scatter(pair_terms, 'ctx', scatter_dimension=1, tiled=True)  260 us
    reduce_scatter x1, waiting for transfers between devices, body(): lax.psum_scatter(grad_out, ('dp', 'ctx'), scatter_dimension=0, tiled=True)  249 us
    all_gather x1, waiting for transfers between devices, body(): lax.all_gather(up_weight, ('dp', 'ctx'), axis=0, tiled=True)  190 us
    all_gather x1, waiting for transfers between devices, body(): lax.all_gather(down_weight, ('dp', 'ctx'), axis=0, tiled=True)  177 us
    all_gather x1, waiting for transfers between devices, body(): gathered = lax.all_gather(paired, 'ctx', axis=1, tiled=True)  144 us
  transfers between devices with their start and end apart: 11, of which 11 were waited for; matrix products, arithmetic and copies ran while one was open for 4% of the time, Pallas kernels for 0%

commit v1 on v0

v1 whole, which is shorter than its diff:
```python
from functools import partial

import jax
import jax.numpy as jnp
import numpy as np
from jax import lax
from jax.experimental import pallas as pl
from jax.experimental.pallas import tpu as pltpu
from jax.sharding import Mesh
from jax.sharding import PartitionSpec as P

HEADS = 16
HEAD_DIM = 128
GROUP = 8
CHIPS = GROUP // 2

EPS_NORM = 1e-05
EPS_ADAM = 1e-08
F32 = jnp.float32
BF16 = jnp.bfloat16
AXES = ("o", "p", "z")
VMEM_LIMIT = 56 * 1024 * 1024


def dot(a, b):
    return jnp.dot(a, b, preferred_element_type=F32)


def dot_nt(a, b):
    return lax.dot_general(a, b, (((1,), (1,)), ((), ())), preferred_element_type=F32)


def dot_tn(a, b):
    return lax.dot_general(a, b, (((0,), (0,)), ((), ())), preferred_element_type=F32)


def permute(value, target):
    sizes = [lax.axis_size(a) for a in AXES]
    pairs = []
    for o in range(sizes[0]):
        for p in range(sizes[1]):
            for z in range(sizes[2]):
                to = target(o, p, z)
                flat = lambda c: (c[0] * sizes[1] + c[1]) * sizes[2] + c[2]
                pairs.append((flat((o, p, z)), flat(to)))
    return lax.ppermute(value, AXES, pairs)


def swap_p(value, k):
    return permute(value, lambda o, p, z: (o, p ^ k, z))


def swap_z(value, k):
    return permute(value, lambda o, p, z: (o, p, z ^ k))


def swap_o(value, k):
    return permute(value, lambda o, p, z: (o ^ k, p, z))


def sum_all(value):
    for swap, size in ((swap_p, GROUP), (swap_z, lax.axis_size("z")), (swap_o, lax.axis_size("o"))):
        k = 1
        while k < size:
            value = value + swap(value, k)
            k *= 2
    return value


def pick(stacked, index):
    return lax.dynamic_index_in_dim(stacked, index, 0, keepdims=False)


def spread(block, chip, z):
    rows = block.shape[0] // CHIPS
    parts = block.reshape(CHIPS, rows, block.shape[1])
    held = [pick(parts, chip)]
    for k in range(1, CHIPS):
        held.append(swap_p(pick(parts, chip ^ k), 2 * k))
    held = jnp.stack(held)
    arrived = [pick(held, chip ^ z)]
    for j in range(1, CHIPS):
        arrived.append(swap_z(pick(held, chip ^ z ^ j), j))
    return jnp.concatenate(arrived, axis=0)


def unspread(block, chip, z):
    rows = block.shape[0] // CHIPS
    parts = block.reshape(CHIPS, rows, block.shape[1])
    held = [parts[0]]
    for j in range(1, CHIPS):
        held.append(swap_z(parts[j], j))
    held = jnp.stack(held)
    arrived = [pick(held, chip ^ z)]
    for k in range(1, CHIPS):
        arrived.append(swap_p(pick(held, chip ^ k ^ z), 2 * k))
    arrived = jnp.stack(arrived)
    return jnp.concatenate([pick(arrived, q ^ chip) for q in range(CHIPS)], axis=0)


def plane_gather(block):
    own = [block] + [swap_p(block, 2 * k) for k in range(1, CHIPS)]
    other = [swap_p(v, 1) for v in own]
    return [jnp.concatenate(own, axis=0), jnp.concatenate(other, axis=0)]


def plane_reduce(own_terms, other_terms):
    rows = own_terms.shape[0] // CHIPS
    total = None
    for k in range(CHIPS):
        span = slice(k * rows, (k + 1) * rows)
        part = own_terms[span].astype(F32) + swap_p(other_terms[span], 1).astype(F32)
        if k:
            part = swap_p(part.astype(BF16), 2 * k).astype(F32)
        total = part if total is None else total + part
    return total


def gather_columns(weight, groups):
    rows, cols = weight.shape
    width = cols // (groups * GROUP)
    parts = weight.reshape(rows, groups, GROUP, width).transpose(2, 0, 1, 3)
    parts = parts.reshape(GROUP, rows, groups * width)
    parts = lax.all_to_all(parts, "p", 0, 0, tiled=True)
    full = lax.all_gather(parts, ("o", "z"), axis=0, tiled=False)
    o_size, z_size = lax.axis_size("o"), lax.axis_size("z")
    full = full.reshape(o_size, z_size, GROUP, rows, groups * width).transpose(0, 2, 1, 3, 4)
    return full.reshape(-1, groups * width)


def scatter_columns(grad, groups, rows):
    o_size, z_size = lax.axis_size("o"), lax.axis_size("z")
    width = grad.shape[1] // groups
    parts = grad.reshape(o_size, GROUP, z_size, rows, -1).transpose(0, 2, 1, 3, 4)
    parts = parts.reshape(-1, groups * width)
    mine = lax.psum_scatter(parts, ("o", "z"), scatter_dimension=0, tiled=True)
    mine = lax.all_to_all(mine, "p", 0, 0, tiled=True)
    mine = mine.reshape(GROUP, rows, groups, width).transpose(1, 2, 0, 3)
    return mine.reshape(rows, -1).astype(F32)


def gather_rows(weight, p):
    if lax.axis_size("o") == 1:
        return lax.all_gather(weight, "z", axis=0, tiled=True)
    full = lax.all_gather(weight, AXES, axis=0, tiled=True)
    return pick(full.reshape(GROUP, -1, weight.shape[1]), p)


def scatter_rows(grad, p):
    if lax.axis_size("o") == 1:
        return lax.psum_scatter(grad, "z", scatter_dimension=0, tiled=True).astype(F32)
    full = jnp.zeros((GROUP,) + grad.shape, grad.dtype)
    full = lax.dynamic_update_index_in_dim(full, grad, p, 0)
    full = full.reshape(-1, grad.shape[1])
    return lax.psum_scatter(full, AXES, scatter_dimension=0, tiled=True).astype(F32)


def order_rows(pos_ref, blocks, rows):
    out = []
    for b in range(blocks):
        for q in range(CHIPS):
            held = ((q ^ pos_ref[0]) * blocks + (b ^ pos_ref[1])) * rows
            out.append(((b * CHIPS + q) * rows, pl.multiple_of(held, rows)))
    return out


def block_probs(q, keys, slope, start, scale):
    scores = dot_nt(q, keys) * scale
    row = lax.broadcasted_iota(jnp.int32, scores.shape, 0) + start
    col = lax.broadcasted_iota(jnp.int32, scores.shape, 1)
    scores = scores - slope * jnp.abs(row - col).astype(F32)
    expo = jnp.exp(scores - jnp.max(scores, axis=-1, keepdims=True))
    return expo * (1.0 / jnp.sum(expo, axis=-1, keepdims=True))


def attend_kernel(blocks, scale, pos_ref, slope_ref, q_ref, k_ref, v_ref, ctx_ref, qs, ks, vs):
    rows = q_ref.shape[0] // (blocks * CHIPS)
    block = rows * CHIPS
    slope = slope_ref[pl.program_id(0)]
    order = order_rows(pos_ref, blocks, rows)
    for nat, held in order:
        qs[nat : nat + rows] = q_ref[pl.ds(held, rows), :]
        ks[nat : nat + rows] = k_ref[pl.ds(held, rows), :]
        vs[nat : nat + rows] = v_ref[pl.ds(held, rows), :]
    for b in range(blocks):
        end = (b + 1) * block
        probs = block_probs(qs[b * block : end], ks[:end], slope, b * block, scale)
        ctx = dot(probs.astype(BF16), vs[:end]).astype(BF16)
        for q in range(CHIPS):
            held = order[b * CHIPS + q][1]
            ctx_ref[pl.ds(held, rows), :] = ctx[q * rows : (q + 1) * rows]


def attend_back_kernel(
    blocks, scale, pos_ref, slope_ref, q_ref, k_ref, v_ref, g_ref, gq_ref, gk_ref, gv_ref,
    qs, ks, vs, gs, gks, gvs,
):
    rows = q_ref.shape[0] // (blocks * CHIPS)
    block = rows * CHIPS
    slope = slope_ref[pl.program_id(0)]
    order = order_rows(pos_ref, blocks, rows)
    for nat, held in order:
        qs[nat : nat + rows] = q_ref[pl.ds(held, rows), :]
        ks[nat : nat + rows] = k_ref[pl.ds(held, rows), :]
        vs[nat : nat + rows] = v_ref[pl.ds(held, rows), :]
        gs[nat : nat + rows] = g_ref[pl.ds(held, rows), :]
    for b in reversed(range(blocks)):
        start, end = b * block, (b + 1) * block
        q, g = qs[start:end], gs[start:end]
        keys, values = ks[:end], vs[:end]
        probs = block_probs(q, keys, slope, start, scale)
        grad_values = dot_tn(probs.astype(BF16), g)
        grad_probs = dot_nt(g, values)
        inner = jnp.sum(probs * grad_probs, axis=-1, keepdims=True)
        grad_scores = (probs * (grad_probs - inner)).astype(BF16)
        grad_q = (dot(grad_scores, keys) * scale).astype(BF16)
        grad_keys = dot_tn(grad_scores, q)
        if b == blocks - 1:
            gks[...] = grad_keys
            gvs[...] = grad_values
        else:
            gks[:end] += grad_keys
            gvs[:end] += grad_values
        for c in range(CHIPS):
            held = order[b * CHIPS + c][1]
            gq_ref[pl.ds(held, rows), :] = grad_q[c * rows : (c + 1) * rows]
    for nat, held in order:
        gk_ref[pl.ds(held, rows), :] = (gks[nat : nat + rows] * scale).astype(BF16)
        gv_ref[pl.ds(held, rows), :] = gvs[nat : nat + rows].astype(BF16)


def attend(qkv, place, slopes):
    length, heads = qkv.shape[0], qkv.shape[1] // (3 * HEAD_DIM)
    blocks = lax.axis_size("z")
    smem = pl.BlockSpec(memory_space=pltpu.SMEM)
    column = lambda first: pl.BlockSpec((length, HEAD_DIM), lambda h: (0, first + h))
    held = pltpu.VMEM((length, HEAD_DIM), BF16)
    return pl.pallas_call(
        partial(attend_kernel, blocks, HEAD_DIM**-0.5),
        grid=(heads,),
        in_specs=[smem, smem, column(0), column(heads), column(2 * heads)],
        out_specs=column(0),
        out_shape=jax.ShapeDtypeStruct((length, heads * HEAD_DIM), BF16),
        scratch_shapes=[held] * 3,
        compiler_params=pltpu.CompilerParams(vmem_limit_bytes=VMEM_LIMIT),
        cost_estimate=pl.CostEstimate(
            flops=3 * length * length * HEAD_DIM * heads,
            bytes_accessed=8 * length * heads * HEAD_DIM,
            transcendentals=length * length * heads,
        ),
    )(place, slopes, qkv, qkv, qkv)


def attend_back(qkv, grad_ctx, place, slopes):
    length, heads = qkv.shape[0], qkv.shape[1] // (3 * HEAD_DIM)
    blocks = lax.axis_size("z")
    smem = pl.BlockSpec(memory_space=pltpu.SMEM)
    column = lambda first: pl.BlockSpec((length, HEAD_DIM), lambda h: (0, first + h))
    held = pltpu.VMEM((length, HEAD_DIM), BF16)
    wide = pltpu.VMEM((length, HEAD_DIM), F32)
    return pl.pallas_call(
        partial(attend_back_kernel, blocks, HEAD_DIM**-0.5),
        grid=(heads,),
        in_specs=[smem, smem, column(0), column(heads), column(2 * heads), column(0)],
        out_specs=[column(0)] * 3,
        out_shape=[jax.ShapeDtypeStruct((length, heads * HEAD_DIM), BF16)] * 3,
        scratch_shapes=[held] * 4 + [wide] * 2,
        compiler_params=pltpu.CompilerParams(vmem_limit_bytes=VMEM_LIMIT),
        cost_estimate=pl.CostEstimate(
            flops=8 * length * length * HEAD_DIM * heads,
            bytes_accessed=14 * length * heads * HEAD_DIM,
            transcendentals=length * length * heads,
        ),
    )(place, slopes, qkv, qkv, qkv, grad_ctx)


def norm_forward(values, gain, shift):
    centre = values - jnp.mean(values, axis=-1, keepdims=True)
    factor = lax.rsqrt(jnp.mean(centre * centre, axis=-1, keepdims=True) + EPS_NORM)
    normed = centre * factor
    return (normed * gain + shift, normed, factor)


def norm_backward(incoming, normed, factor, gain):
    scaled = incoming * gain
    input_grad = factor * (
        scaled
        - jnp.mean(scaled, axis=-1, keepdims=True)
        - normed * jnp.mean(scaled * normed, axis=-1, keepdims=True)
    )
    return (input_grad, jnp.sum(incoming * normed, axis=0), jnp.sum(incoming, axis=0))


def adam_update(weight, moments, grad, clip_factor, step, hyper):
    step_float = step.astype(F32)
    scaled = grad * clip_factor
    first_moment = hyper[2] * moments[0] + (1.0 - hyper[2]) * scaled
    second_moment = hyper[3] * moments[1] + (1.0 - hyper[3]) * scaled * scaled
    fix_first = 1.0 - hyper[2] ** step_float
    fix_second = 1.0 - hyper[3] ** step_float
    current = weight.astype(F32)
    change = -hyper[0] * (
        first_moment / fix_first / (jnp.sqrt(second_moment / fix_second) + EPS_ADAM)
        + hyper[1] * current
    )
    updated = current + change
    return (updated.astype(BF16), change, jnp.stack([first_moment, second_moment]))


def column_sum(values):
    return jnp.sum(values.astype(F32), axis=0)


def body(
    tokens,
    cotangent,
    qkv_weight,
    out_weight,
    up_weight,
    down_weight,
    vectors,
    qkv_moments,
    out_moments,
    up_moments,
    down_moments,
    vector_moments,
    step,
    hyper,
):
    o, p, z = (lax.axis_index(a) for a in AXES)
    chip = p >> 1
    width = tokens.shape[2]
    place = jnp.stack([chip, z]).astype(jnp.int32)
    heads = HEADS // GROUP
    head_ids = (p * heads + jnp.arange(heads)).astype(F32)
    slopes = jnp.exp2(-8.0 * (head_ids + 1.0) / HEADS)
    tokens_given, top_given = tokens[0], cotangent[0]

    w_qkv = gather_columns(qkv_weight, 3)
    rows_low = spread(tokens_given, chip, z)
    flat = (o * GROUP + p) * lax.axis_size("z") + z
    vec_cols = vectors.shape[1]
    vec_low = lax.dynamic_update_slice(
        jnp.zeros((vectors.shape[0], width), BF16), vectors, (0, flat * vec_cols)
    )
    vecs = sum_all(vec_low).astype(F32)
    w_out = gather_rows(out_weight, p)
    w_up = gather_columns(up_weight, 1)
    w_down = gather_rows(down_weight, p)
    top_low = spread(top_given, chip, z)

    rows_in = rows_low.astype(F32)
    normed, hat_one, factor_one = norm_forward(rows_in, vecs[0], vecs[1])
    normed_a = plane_gather(normed.astype(BF16))
    part = width // GROUP
    bias_q = lax.dynamic_slice(vecs[2], (p * part,), (part,))
    bias_v = lax.dynamic_slice(vecs[3], (p * part,), (part,))
    bias_qkv = jnp.concatenate([bias_q, jnp.zeros_like(bias_q), bias_v])
    qkv = [(dot(v, w_qkv) + bias_qkv).astype(BF16) for v in normed_a]
    context = [attend(v, place, slopes) for v in qkv]
    attn = plane_reduce(*[dot(v, w_out).astype(BF16) for v in context])
    residual = rows_in + attn + vecs[4]
    normed, hat_two, factor_two = norm_forward(residual, vecs[5], vecs[6])
    normed_b = plane_gather(normed.astype(BF16))
    hidden_part = w_up.shape[1]
    bias_up = lax.dynamic_slice(vecs[8:].reshape(-1), (p * hidden_part,), (hidden_part,))
    pre_act = [dot(v, w_up) + bias_up for v in normed_b]
    hidden = [jax.nn.gelu(v, approximate=True).astype(BF16) for v in pre_act]
    mlp = plane_reduce(*[dot(v, w_down).astype(BF16) for v in hidden])
    activations = unspread((residual + mlp + vecs[7]).astype(BF16), chip, z)

    grad_top = top_low.astype(F32)
    grad_mlp = plane_gather(top_low)
    grad_down = dot_tn(hidden[0], grad_mlp[0]) + dot_tn(hidden[1], grad_mlp[1])
    owned_down = scatter_rows(grad_down.astype(BF16), p)
    grad_pre = []
    for v, g in zip(pre_act, grad_mlp):
        _, pull = jax.vjp(partial(jax.nn.gelu, approximate=True), v)
        grad_pre.append(pull(dot_nt(g, w_down))[0].astype(BF16))
    grad_up = dot_tn(normed_b[0], grad_pre[0]) + dot_tn(normed_b[1], grad_pre[1])
    owned_up = scatter_columns(grad_up.astype(BF16), 1, up_weight.shape[0])
    grad_normed = plane_reduce(*[dot_nt(g, w_up).astype(BF16) for g in grad_pre])
    through, gain_two_grad, shift_two_grad = norm_backward(grad_normed, hat_two, factor_two, vecs[5])
    grad_residual = grad_top + through
    grad_attn_own = grad_residual.astype(BF16)
    grad_attn = plane_gather(grad_attn_own)
    grad_context = [dot_nt(g, w_out).astype(BF16) for g in grad_attn]
    grad_out = dot_tn(context[0], grad_attn[0]) + dot_tn(context[1], grad_attn[1])
    owned_out = scatter_rows(grad_out.astype(BF16), p)
    grads = [attend_back(v, g, place, slopes) for v, g in zip(qkv, grad_context)]
    grad_qkv = [jnp.concatenate(g, axis=1) for g in grads]
    grad_qkv_weight = dot_tn(normed_a[0], grad_qkv[0]) + dot_tn(normed_a[1], grad_qkv[1])
    owned_qkv = scatter_columns(grad_qkv_weight.astype(BF16), 3, qkv_weight.shape[0])
    grad_normed = plane_reduce(*[dot_nt(g, w_qkv).astype(BF16) for g in grad_qkv])
    through, gain_one_grad, shift_one_grad = norm_backward(grad_normed, hat_one, factor_one, vecs[0])
    input_grad = unspread((grad_residual + through).astype(BF16), chip, z)

    bias_grads = column_sum(grad_qkv[0]) + column_sum(grad_qkv[1])
    up_bias_grad = column_sum(grad_pre[0]) + column_sum(grad_pre[1])
    wide = lambda v: lax.dynamic_update_slice(jnp.zeros((width,), F32), v, (p * part,))
    up_wide = lax.dynamic_update_slice(
        jnp.zeros((GROUP * hidden_part,), F32), up_bias_grad, (p * hidden_part,)
    )
    vector_grad = jnp.concatenate(
        [
            jnp.stack(
                [
                    gain_one_grad,
                    shift_one_grad,
                    wide(bias_grads[:part]),
                    wide(bias_grads[2 * part :]),
                    column_sum(grad_attn_own),
                    gain_two_grad,
                    shift_two_grad,
                    column_sum(top_given),
                ]
            ),
            up_wide.reshape(-1, width),
        ],
        axis=0,
    )
    owned_vec = lax.dynamic_slice(
        sum_all(vector_grad), (0, flat * vec_cols), (vectors.shape[0], vec_cols)
    )

    owned = (owned_qkv, owned_out, owned_up, owned_down, owned_vec)
    squares = sum(jnp.sum(g * g) for g in owned)
    grad_norm = jnp.sqrt(sum_all(squares.reshape(1, 1))[0, 0])
    clip_factor = jnp.minimum(1.0, hyper[4] / (grad_norm + 1e-06))
    shards = (qkv_weight, out_weight, up_weight, down_weight, vectors)
    moments = (qkv_moments, out_moments, up_moments, down_moments, vector_moments)
    news = [
        adam_update(w, m, g, clip_factor, step, hyper) for w, m, g in zip(shards, moments, owned)
    ]
    return (
        activations[None],
        input_grad[None],
        grad_norm,
        news[0][0],
        news[1][1],
        news[2][0],
        news[3][0],
        news[4][1],
        news[0][2],
        news[1][2],
        news[2][2],
        news[3][2],
        news[4][2],
    )


def solution(mesh):
    devices = np.asarray(mesh.devices)
    planes = Mesh(devices.reshape(-1, GROUP, devices.shape[1]), AXES)
    rows = P(AXES, None)
    seqs = P(("o", "p"), "z", None)
    pair = P(None, AXES, None)
    cols = P(None, AXES)
    return jax.shard_map(
        body,
        mesh=planes,
        in_specs=(seqs, seqs, rows, rows, rows, rows, cols)
        + (pair, pair, pair, pair, P(None, None, AXES), P(), P()),
        out_specs=(seqs, seqs, P(), rows, rows, rows, rows, cols)
        + (pair, pair, pair, pair, P(None, None, AXES)),
        check_vma=False,
    )
```

time: 5040 us -> 944 us (0.19)
  waiting for transfers between devices: 4530 us -> 440 us
  starting transfers between devices: 0.65 us -> 105 us
  matrix products: 250 us -> 153 us
  blocking collectives: 113 us -> 17.8 us
    reduce_scatter x5 -> x4, waiting for transfers between devices: 3760 us -> 0.04 us  [the longest x2 0.04 us: scatter_columns(): mine = lax.psum_scatter(parts, ('o', 'z'), scatter_dimension=0, tiled=True)]
    all_gather x5 -> x4, waiting for transfers between devices: 637 us -> 16.3 us  [the longest x2 16.3 us: gather_columns(): full = lax.all_gather(parts, ('o', 'z'), axis=0, tiled=False)]
    ppermute x0 -> x95, waiting for transfers between devices: none -> 414 us  [permute(): return lax.ppermute(value, AXES, pairs)]
    unnamed x12 -> x8, waiting for transfers between devices: 137 us -> 1.48 us
    dot_general x18 -> x24, matrix products: 250 us -> 153 us  [the longest x8 56.2 us: dot_tn(): lax.dot_general(a, b, (((0,), (0,)), ((), ())), preferred_element_type=F32)]
    ppermute x0 -> x95, starting transfers between devices: none -> 93.4 us  [permute(): return lax.ppermute(value, AXES, pairs)]
    all_gather x1 -> x0, blocking collectives: 72.8 us -> none  [body(): lax.all_gather(vectors, ('dp', 'ctx'), axis=1, tiled=True)]
  transfers between devices with their start and end apart: 11 -> 106, of which waited for: 11 -> 41; matrix products, arithmetic and copies ran while one was open for 4% -> 24% of each run, Pallas kernels for 0% -> 3%
where the time goes in v1:
time: 944 us; the launch traced here: 936 us
  waiting for transfers between devices  440 us (47%)
  matrix products  153 us (16%)
  starting transfers between devices  105 us (11%)
  local copies, waits for them, and re-layouts  82.8 us (9%)
  other arithmetic  78.9 us (8%)
  Pallas kernels  30.6 us (3%)
  between operations  27.7 us (3%)
  blocking collectives  17.8 us (2%)
    ppermute x95, waiting for transfers between devices, permute(): return lax.ppermute(value, AXES, pairs)  414 us
    ppermute x95, starting transfers between devices, permute(): return lax.ppermute(value, AXES, pairs)  93.4 us
    dot_general x8, matrix products, dot_tn(): lax.dot_general(a, b, (((0,), (0,)), ((), ())), preferred_element_type=F32)  56.2 us
    dot_general x8, matrix products, dot_nt(): lax.dot_general(a, b, (((1,), (1,)), ((), ())), preferred_element_type=F32)  52.6 us
    dot_general x8, matrix products, dot(): return jnp.dot(a, b, preferred_element_type=F32)  44.5 us
    unnamed x185, local copies, waits for them, and re-layouts  38.5 us
  transfers between devices with their start and end apart: 106, of which 41 were waited for; matrix products, arithmetic and copies ran while one was open for 24% of the time, Pallas kernels for 3%

profile of v1, /device:TPU:0, one launch (start us, length us, event | category | flops | bytes accessed | tf_op | source)
XLA Modules:
  0.0 935.9 jit_solution(6925642461123673988)
XLA Ops:
  9.9 17.8 %all_to_all.28 = bf16[8,64,768]{2,1,0:T(8,128)(2,1)} all-to-all(bf16[8,64,768]{2,1,0:T(8,128)(2,1)S(1)} %reshape.249), channel_id=1, replica_groups=mesh['dp'=8,'ctx'=4] {'dp'}, dimensions={0} | all-to-all | bytes 1572864 | tf_op jit(solution)/shard_map/all_to_all | solution.py:124
  45.5 8.8 collective-permute-done.8
  56.7 7.3 collective-permute-done.9
  66.3 8.9 collective-permute-done.10
  76.8 5.6 collective-permute-start.45
  90.7 9.0 collective-permute-done.5
  99.7 15.7 %collective-permute-done.4 = bf16[64,2048]{1,0:T(8,128)(2,1)S(1)} collective-permute-done((bf16[64,2048]{1,0:T(8,128)(2,1)S(1)}, bf16[64,2048]{1,0:T(8,128)(2,1)S(1)}, u32[]{:S(2)}, u32[]{:S(2)}) %collective-permute-start.4) | collective-permute-done | bytes 262176 | tf_op jit(solution)/shard_map/ppermute | solution.py:46
  124.1 14.4 %collective-permute-done.48 = bf16[64,2048]{1,0:T(8,128)(2,1)S(1)} collective-permute-done((bf16[64,2048]{1,0:T(8,128)(2,1)S(1)}, bf16[64,2048]{1,0:T(8,128)(2,1)S(1)}, u32[]{:S(2)}, u32[]{:S(2)}) %collective-permute-start.48) | collective-permute-done | bytes 262176 | tf_op jit(solution)/shard_map/ppermute | solution.py:46
  141.8 12.5 %collective-permute-done.49 = bf16[64,2048]{1,0:T(8,128)(2,1)S(1)} collective-permute-done((bf16[64,2048]{1,0:T(8,128)(2,1)S(1)}, bf16[64,2048]{1,0:T(8,128)(2,1)S(1)}, u32[]{:S(2)}, u32[]{:S(2)}) %collective-permute-start.49) | collective-permute-done | bytes 262176 | tf_op jit(solution)/shard_map/ppermute | solution.py:46
  156.7 7.8 collective-permute-done.12
  173.2 13.3 %collective-permute-done.51 = bf16[256,2048]{1,0:T(8,128)(2,1)} collective-permute-done((bf16[256,2048]{1,0:T(8,128)(2,1)}, bf16[256,2048]{1,0:T(8,128)(2,1)}, u32[]{:S(2)}, u32[]{:S(2)}) %collective-permute-start.51) | collective-permute-done | bytes 1048608 | tf_op jit(solution)/shard_map/ppermute | solution.py:46
  201.8 6.8 add_convert_fusion.3.q_ref.k_ref.v_ref
  208.6 6.5 shard_map.238
  222.9 6.4 add_convert_fusion.4.q_ref.k_ref.v_ref
  229.9 6.6 shard_map.237
  249.6 18.1 %collective-permute-done.24 = bf16[256,2048]{1,0:T(8,128)(2,1)S(1)} collective-permute-done((bf16[256,2048]{1,0:T(8,128)(2,1)S(1)}, bf16[256,2048]{1,0:T(8,128)(2,1)S(1)}, u32[]{:S(2)}, u32[]{:S(2)}) %collective-permute-start.24) | collective-permute-done | bytes 1048608 | tf_op jit(solution)/shard_map/ppermute | solution.py:46
  267.8 21.1 %collective-permute-done.22 = bf16[256,2048]{1,0:T(8,128)(2,1)S(1)} collective-permute-done((bf16[256,2048]{1,0:T(8,128)(2,1)S(1)}, bf16[256,2048]{1,0:T(8,128)(2,1)S(1)}, u32[]{:S(2)}, u32[]{:S(2)}) %collective-permute-start.22) | collective-permute-done | bytes 1048608 | tf_op jit(solution)/shard_map/ppermute | solution.py:46
  295.3 10.0 %fusion.103 = f32[1024,1024]{1,0:T(8,128)} fusion(bf16[1024,2048]{1,0:T(8,128)(2,1)} %constant_dynamic-update-slice_fusion.8, bf16[1024,2048]{1,0:T(8,128)(2,1)} %all-gather.9.cloned.1.call-done), kind=kOutput, calls=%fused_computation.290 | convolution fusion | flops 4294967296 | bytes 12582912 | tf_op jit(solution)/shard_map/dot_general | solution.py:30
  305.3 16.3 %all-gather.13.cloned.1.call-done = bf16[32,64,1024]{2,1,0:T(8,128)(2,1)} async-done(((bf16[8,64,1024]{2,1,0:T(8,128)(2,1)}), bf16[32,64,1024]{2,1,0:T(8,128)(2,1)}) %all-gather.13.cloned.1.call-update) | async-done | bytes 4194320 | tf_op jit(solution)/shard_map/all_gather | solution.py:125
  324.3 16.2 %collective-permute-done.25 = bf16[256,2048]{1,0:T(8,128)(2,1)} collective-permute-done((bf16[256,2048]{1,0:T(8,128)(2,1)}, bf16[256,2048]{1,0:T(8,128)(2,1)}, u32[]{:S(2)}, u32[]{:S(2)}) %collective-permute-start.25) | collective-permute-done | bytes 1048608 | tf_op jit(solution)/shard_map/ppermute | solution.py:46
  341.1 9.1 fusion.64
  350.7 6.1 fusion.102
  356.8 13.5 %convert_reduce_fusion.1 = (f32[1024]{0:T(1024)S(1)}, bf16[1024,1024]{1,0:T(8,128)(2,1)}, f32[1024]{0:T(1024)S(1)}, bf16[1024,1024]{1,0:T(8,128)(2,1)}) fusion(f32[1024,1024]{1,0:T(8,128)} %fusion.103, f32[1024,1024]{1,0:T(8,128)S(1)} %copy-done.72, f32[1024]{0:T(1024)S(1)} %dynamic_slice.125, f32[1024,1024]{1,0:T(8,128)} %fusion.102, ...), kind=kOutput, calls=%fused_computation.27 | convolution fusion | flops 4343199744 | bytes 25178112 | tf_op jit(solution)/shard_map/dot_general | solution.py:30
  370.3 6.4 convolution_convert_fusion.4
  380.5 5.4 convolution_convert_fusion.6
  388.8 10.2 %fusion.63 = f32[2048,1024]{1,0:T(8,128)} fusion(bf16[1024,1024]{1,0:T(8,128)(2,1)S(1)} %copy-done.77, bf16[256,2048]{1,0:T(8,128)(2,1)} %collective-permute-done.27, bf16[256,2048]{1,0:T(8,128)(2,1)} %collective-permute-done.26, bf16[256,2048]{1,0:T(8,128)(2,1)} %collective-permute-done.25, bf16[256,2048]{1,0:T(8,128)(2,1)} %add_convert_fusion.15), kind=kOutput, calls=%fused_computation.161 | convolution fusion | flops 4311744512 | bytes 14680064 | tf_op jit(solution)/shard_map/dot_general | solution.py:34
  399.1 7.1 add_convert_fusion.1
  406.2 6.2 convolution_convert_fusion.5
  423.5 5.6 convolution_convert_fusion.7
  433.3 13.7 %collective-permute-done.64 = bf16[256,2048]{1,0:T(8,128)(2,1)S(1)} collective-permute-done((bf16[256,2048]{1,0:T(8,128)(2,1)S(1)}, bf16[256,2048]{1,0:T(8,128)(2,1)S(1)}, u32[]{:S(2)}, u32[]{:S(2)}) %collective-permute-start.64) | collective-permute-done | bytes 1048608 | tf_op jit(solution)/shard_map/ppermute | solution.py:46
  448.3 21.1 %collective-permute-done.62 = bf16[256,2048]{1,0:T(8,128)(2,1)S(1)} collective-permute-done((bf16[256,2048]{1,0:T(8,128)(2,1)S(1)}, bf16[256,2048]{1,0:T(8,128)(2,1)S(1)}, u32[]{:S(2)}, u32[]{:S(2)}) %collective-permute-start.62) | collective-permute-done | bytes 1048608 | tf_op jit(solution)/shard_map/ppermute | solution.py:46
  473.7 18.2 %collective-permute-done.38 = bf16[256,2048]{1,0:T(8,128)(2,1)S(1)} collective-permute-done((bf16[256,2048]{1,0:T(8,128)(2,1)S(1)}, bf16[256,2048]{1,0:T(8,128)(2,1)S(1)}, u32[]{:S(2)}, u32[]{:S(2)}) %collective-permute-start.38) | collective-permute-done | bytes 1048608 | tf_op jit(solution)/shard_map/ppermute | solution.py:46
  491.9 22.1 %collective-permute-done.36 = bf16[256,2048]{1,0:T(8,128)(2,1)S(1)} collective-permute-done((bf16[256,2048]{1,0:T(8,128)(2,1)S(1)}, bf16[256,2048]{1,0:T(8,128)(2,1)S(1)}, u32[]{:S(2)}, u32[]{:S(2)}) %collective-permute-start.36) | collective-permute-done | bytes 1048608 | tf_op jit(solution)/shard_map/ppermute | solution.py:46
  521.6 22.6 %collective-permute-done.65 = bf16[256,2048]{1,0:T(8,128)(2,1)} collective-permute-done((bf16[256,2048]{1,0:T(8,128)(2,1)S(1)}, bf16[256,2048]{1,0:T(8,128)(2,1)}, u32[]{:S(2)}, u32[]{:S(2)}) %collective-permute-start.65) | collective-permute-done | bytes 1048608 | tf_op jit(solution)/shard_map/ppermute | solution.py:46
  544.2 21.9 %collective-permute-done.66 = bf16[256,2048]{1,0:T(8,128)(2,1)} collective-permute-done((bf16[256,2048]{1,0:T(8,128)(2,1)S(1)}, bf16[256,2048]{1,0:T(8,128)(2,1)}, u32[]{:S(2)}, u32[]{:S(2)}) %collective-permute-start.66) | collective-permute-done | bytes 1048608 | tf_op jit(solution)/shard_map/ppermute | solution.py:46
  570.3 8.8 shard_map.239
  591.7 8.6 fusion.65
  602.4 8.8 shard_map.240
  613.4 8.3 add_convert_fusion.2
  628.5 9.6 %fusion.87 = f32[1024,2048]{1,0:T(8,128)S(1)} fusion(bf16[1024,2048]{1,0:T(8,128)(2,1)} %constant_dynamic-update-slice_fusion.8, f32[1024,1024]{1,0:T(8,128)} %fusion.64, f32[1024]{0:T(1024)S(1)} %dynamic_slice.125), kind=kOutput, calls=%fused_computation.278 | convolution fusion | flops 4305453056 | bytes 16781312 | tf_op jit(solution)/shard_map/dot_general | solution.py:34
  638.1 7.2 add_convert_fusion
  650.6 5.6 convolution_convert_fusion.2
  662.9 36.2 %collective-permute-done.40 = bf16[64,2048]{1,0:T(8,128)(2,1)} collective-permute-done((bf16[64,2048]{1,0:T(8,128)(2,1)}, bf16[64,2048]{1,0:T(8,128)(2,1)}, u32[]{:S(2)}, u32[]{:S(2)}) %collective-permute-start.40) | collective-permute-done | bytes 262176 | tf_op jit(solution)/shard_map/ppermute | solution.py:46
  717.8 18.1 %collective-permute-done.78 = bf16[256,2048]{1,0:T(8,128)(2,1)S(1)} collective-permute-done((bf16[256,2048]{1,0:T(8,128)(2,1)S(1)}, bf16[256,2048]{1,0:T(8,128)(2,1)S(1)}, u32[]{:S(2)}, u32[]{:S(2)}) %collective-permute-start.78) | collective-permute-done | bytes 1048608 | tf_op jit(solution)/shard_map/ppermute | solution.py:46
  737.4 21.0 %collective-permute-done.76 = bf16[256,2048]{1,0:T(8,128)(2,1)S(1)} collective-permute-done((bf16[256,2048]{1,0:T(8,128)(2,1)S(1)}, bf16[256,2048]{1,0:T(8,128)(2,1)S(1)}, u32[]{:S(2)}, u32[]{:S(2)}) %collective-permute-start.76) | collective-permute-done | bytes 1048608 | tf_op jit(solution)/shard_map/ppermute | solution.py:46
  779.8 24.6 %collective-permute-done.80 = bf16[64,2048]{1,0:T(8,128)(2,1)} collective-permute-done((bf16[64,2048]{1,0:T(8,128)(2,1)}, bf16[64,2048]{1,0:T(8,128)(2,1)}, u32[]{:S(2)}, u32[]{:S(2)}) %collective-permute-start.80) | collective-permute-done | bytes 262176 | tf_op jit(solution)/shard_map/ppermute | solution.py:46
  821.8 5.9 collective-permute-done.89
  845.1 7.9 all-to-all-done.2
  (504 shorter events, 319.0 us)
Async XLA Ops:
  7.2 190.8 %all-gather.11.cloned.1.call-start = ((), (), s32[]{:S(2)}) async-start(), calls=%async_computation.14 | async-start | bytes 3932160 | tf_op jit(solution)/shard_map/all_gather | solution.py:125
  27.7 187.4 %all-gather.7.cloned.1.call-start = ((), (), s32[]{:S(2)}) async-start(), calls=%async_computation.8 | async-start | bytes 1310720 | tf_op jit(solution)/shard_map/all_gather | solution.py:144
  28.4 266.9 %all-gather.9.cloned.1.call-start = ((), (), s32[]{:S(2)}) async-start(), calls=%async_computation.9 | async-start | bytes 5242880 | tf_op jit(solution)/shard_map/all_gather | solution.py:144
  32.4 44.3 %collective-permute-start.2 = (bf16[64,2048]{1,0:T(8,128)(2,1)}, bf16[64,2048]{1,0:T(8,128)(2,1)}, u32[]{:S(2)}, u32[]{:S(2)}) collective-permute-start(bf16[64,2048]{1,0:T(8,128)(2,1)} %get-tuple-element.201), channel_id=1, source_target_pairs={{0,24},{1,25},{2,26},{3,27},{4,28},{5,29},{6,30},{7,31},{8,16},{9,... | collective-permute-start | bytes 786440 | tf_op jit(solution)/shard_map/ppermute | solution.py:46
  33.9 48.5 %collective-permute-start.1 = (bf16[64,2048]{1,0:T(8,128)(2,1)}, bf16[64,2048]{1,0:T(8,128)(2,1)}, u32[]{:S(2)}, u32[]{:S(2)}) collective-permute-start(bf16[64,2048]{1,0:T(8,128)(2,1)} %get-tuple-element.202), channel_id=1, source_target_pairs={{0,16},{1,17},{2,18},{3,19},{4,20},{5,21},{6,22},{7,23},{8,24},{9,... | collective-permute-start | bytes 786440 | tf_op jit(solution)/shard_map/ppermute | solution.py:46
  35.4 47.1 %collective-permute-start = (bf16[64,2048]{1,0:T(8,128)(2,1)S(1)}, bf16[64,2048]{1,0:T(8,128)(2,1)}, u32[]{:S(2)}, u32[]{:S(2)}) collective-permute-start(bf16[64,2048]{1,0:T(8,128)(2,1)S(1)} %get-tuple-element.203), channel_id=1, source_target_pairs={{0,8},{1,9},{2,10},{3,11},{4,12},{5,13},{6,14},{7,15},{8,0},{9,1},... | collective-permute-start | bytes 786440 | tf_op jit(solution)/shard_map/ppermute | solution.py:46
  37.4 47.1 %collective-permute-start.47 = (bf16[64,2048]{1,0:T(8,128)(2,1)}, bf16[64,2048]{1,0:T(8,128)(2,1)S(1)}, u32[]{:S(2)}, u32[]{:S(2)}) collective-permute-start(bf16[64,2048]{1,0:T(8,128)(2,1)} %get-tuple-element.181), channel_id=1, source_target_pairs={{0,24},{1,25},{2,26},{3,27},{4,28},{5,29},{6,30},{7,31},{8,16},{9,... | collective-permute-start | bytes 786440 | tf_op jit(solution)/shard_map/ppermute | solution.py:46
  41.9 125.1 %all-to-all-start.1 = ((bf16[8,64,1024]{2,1,0:T(8,128)(2,1)}), bf16[8,64,1024]{2,1,0:T(8,128)(2,1)S(1)}, u32[]{:S(2)}, u32[]{:S(2)}) async-start(bf16[8,64,1024]{2,1,0:T(8,128)(2,1)} %copy.89), calls=%async_computation.1 | async-start | bytes 2097152 | tf_op jit(solution)/shard_map/all_to_all | solution.py:124
  45.5 276.2 %all-gather.13.cloned.1.call-start = ((), (), s32[]{:S(2)}) async-start(), calls=%async_computation.15 | async-start | bytes 5242880 | tf_op jit(solution)/shard_map/all_gather | solution.py:125
  116.6 38.9 %collective-permute-start.11 = (bf16[256,2048]{1,0:T(8,128)(2,1)S(1)}, bf16[256,2048]{1,0:T(8,128)(2,1)}, u32[]{:S(2)}, u32[]{:S(2)}) collective-permute-start(bf16[256,2048]{1,0:T(8,128)(2,1)S(1)} %fusion.23), channel_id=1, source_target_pairs={{0,8},{1,9},{2,10},{3,11},{4,12},{5,13},{6,14},{7,15},{8,0},{9,1},... | collective-permute-start | bytes 3145736 | tf_op jit(solution)/shard_map/ppermute | solution.py:46
  118.3 46.3 %collective-permute-start.12 = (bf16[256,2048]{1,0:T(8,128)(2,1)S(1)}, bf16[256,2048]{1,0:T(8,128)(2,1)}, u32[]{:S(2)}, u32[]{:S(2)}) collective-permute-start(bf16[256,2048]{1,0:T(8,128)(2,1)S(1)} %fusion.23), channel_id=1, source_target_pairs={{0,16},{1,17},{2,18},{3,19},{4,20},{5,21},{6,22},{7,23},{8,24},{9,... | collective-permute-start | bytes 3145736 | tf_op jit(solution)/shard_map/ppermute | solution.py:46
  168.0 637.6 %reduce-scatter.9.cloned.1.call-start = ((), (), s32[]{:S(2)}) async-start(), calls=%async_computation.12 | async-start | bytes 5242880 | tf_op jit(solution)/shard_map/reduce_scatter | solution.py:136
  168.2 51.9 %collective-permute-start.52 = (bf16[256,2048]{1,0:T(8,128)(2,1)}, bf16[256,2048]{1,0:T(8,128)(2,1)}, u32[]{:S(2)}, u32[]{:S(2)}) collective-permute-start(bf16[256,2048]{1,0:T(8,128)(2,1)} %pad_maximum_fusion.11), channel_id=1, source_target_pairs={{0,16},{1,17},{2,18},{3,19},{4,20},{5,21},{6,22},{7,23},{8,24},{9,... | collective-permute-start | bytes 3145736 | tf_op jit(solution)/shard_map/ppermute | solution.py:46
  186.4 42.9 %collective-permute-start.53 = (bf16[256,2048]{1,0:T(8,128)(2,1)}, bf16[256,2048]{1,0:T(8,128)(2,1)}, u32[]{:S(2)}, u32[]{:S(2)}) collective-permute-start(bf16[256,2048]{1,0:T(8,128)(2,1)} %pad_maximum_fusion.11), channel_id=1, source_target_pairs={{0,24},{1,25},{2,26},{3,27},{4,28},{5,29},{6,30},{7,31},{8,16},{9,... | collective-permute-start | bytes 3145736 | tf_op jit(solution)/shard_map/ppermute | solution.py:46
  191.0 49.7 %collective-permute-start.54 = (bf16[256,2048]{1,0:T(8,128)(2,1)}, bf16[256,2048]{1,0:T(8,128)(2,1)}, u32[]{:S(2)}, u32[]{:S(2)}) collective-permute-start(bf16[256,2048]{1,0:T(8,128)(2,1)} %pad_maximum_fusion.11), channel_id=1, source_target_pairs={{0,4},{1,5},{2,6},{3,7},{4,0},{5,1},{6,2},{7,3},{8,12},{9,13},{10,... | collective-permute-start | bytes 3145736 | tf_op jit(solution)/shard_map/ppermute | solution.py:46
  241.5 47.3 %collective-permute-start.22 = (bf16[256,2048]{1,0:T(8,128)(2,1)S(1)}, bf16[256,2048]{1,0:T(8,128)(2,1)S(1)}, u32[]{:S(2)}, u32[]{:S(2)}) collective-permute-start(bf16[256,2048]{1,0:T(8,128)(2,1)S(1)} %get-tuple-element.160), channel_id=1, source_target_pairs={{0,16},{1,17},{2,18},{3,19},{4,20},{5,21},{6,22},{7,23},{8,24},{9,... | collective-permute-start | bytes 3145736 | tf_op jit(solution)/shard_map/ppermute | solution.py:46
  243.0 45.9 %collective-permute-start.20 = (bf16[256,2048]{1,0:T(8,128)(2,1)S(1)}, bf16[256,2048]{1,0:T(8,128)(2,1)S(1)}, u32[]{:S(2)}, u32[]{:S(2)}) collective-permute-start(bf16[256,2048]{1,0:T(8,128)(2,1)S(1)} %get-tuple-element.158), channel_id=1, source_target_pairs={{0,8},{1,9},{2,10},{3,11},{4,12},{5,13},{6,14},{7,15},{8,0},{9,1},... | collective-permute-start | bytes 3145736 | tf_op jit(solution)/shard_map/ppermute | solution.py:46
  291.8 49.2 %collective-permute-start.27 = (bf16[256,2048]{1,0:T(8,128)(2,1)}, bf16[256,2048]{1,0:T(8,128)(2,1)}, u32[]{:S(2)}, u32[]{:S(2)}) collective-permute-start(bf16[256,2048]{1,0:T(8,128)(2,1)} %add_convert_fusion.15), channel_id=1, source_target_pairs={{0,24},{1,25},{2,26},{3,27},{4,28},{5,29},{6,30},{7,31},{8,16},{9,... | collective-permute-start | bytes 3145736 | tf_op jit(solution)/shard_map/ppermute | solution.py:46
  293.1 47.4 %collective-permute-start.26 = (bf16[256,2048]{1,0:T(8,128)(2,1)}, bf16[256,2048]{1,0:T(8,128)(2,1)}, u32[]{:S(2)}, u32[]{:S(2)}) collective-permute-start(bf16[256,2048]{1,0:T(8,128)(2,1)} %add_convert_fusion.15), channel_id=1, source_target_pairs={{0,16},{1,17},{2,18},{3,19},{4,20},{5,21},{6,22},{7,23},{8,24},{9,... | collective-permute-start | bytes 3145736 | tf_op jit(solution)/shard_map/ppermute | solution.py:46
  294.5 46.0 %collective-permute-start.25 = (bf16[256,2048]{1,0:T(8,128)(2,1)}, bf16[256,2048]{1,0:T(8,128)(2,1)}, u32[]{:S(2)}, u32[]{:S(2)}) collective-permute-start(bf16[256,2048]{1,0:T(8,128)(2,1)} %add_convert_fusion.15), channel_id=1, source_target_pairs={{0,8},{1,9},{2,10},{3,11},{4,12},{5,13},{6,14},{7,15},{8,0},{9,1},... | collective-permute-start | bytes 3145736 | tf_op jit(solution)/shard_map/ppermute | solution.py:46
  295.3 54.9 %collective-permute-start.28 = (bf16[256,2048]{1,0:T(8,128)(2,1)}, bf16[256,2048]{1,0:T(8,128)(2,1)S(1)}, u32[]{:S(2)}, u32[]{:S(2)}) collective-permute-start(bf16[256,2048]{1,0:T(8,128)(2,1)} %add_convert_fusion.15), channel_id=1, source_target_pairs={{0,4},{1,5},{2,6},{3,7},{4,0},{5,1},{6,2},{7,3},{8,12},{9,13},{10,... | collective-permute-start | bytes 3145736 | tf_op jit(solution)/shard_map/ppermute | solution.py:46
  379.4 36.0 %collective-permute-start.63 = (bf16[256,2048]{1,0:T(8,128)(2,1)}, bf16[256,2048]{1,0:T(8,128)(2,1)}, u32[]{:S(2)}, u32[]{:S(2)}) collective-permute-start(bf16[256,2048]{1,0:T(8,128)(2,1)} %get-tuple-element.141), channel_id=1, source_target_pairs={{0,4},{1,5},{2,6},{3,7},{4,0},{5,1},{6,2},{7,3},{8,12},{9,13},{10,... | collective-permute-start | bytes 3145736 | tf_op jit(solution)/shard_map/ppermute | solution.py:46
  379.5 36.1 %collective-permute-start.61 = (bf16[256,2048]{1,0:T(8,128)(2,1)}, bf16[256,2048]{1,0:T(8,128)(2,1)}, u32[]{:S(2)}, u32[]{:S(2)}) collective-permute-start(bf16[256,2048]{1,0:T(8,128)(2,1)} %get-tuple-element.142), channel_id=1, source_target_pairs={{0,4},{1,5},{2,6},{3,7},{4,0},{5,1},{6,2},{7,3},{8,12},{9,13},{10,... | collective-permute-start | bytes 3145736 | tf_op jit(solution)/shard_map/ppermute | solution.py:46
  414.8 405.2 %reduce-scatter.7.cloned.1.call-start = ((), (), s32[]{:S(2)}) async-start(), calls=%async_computation.11 | async-start | bytes 1310720 | tf_op jit(solution)/shard_map/reduce_scatter | solution.py:151
  421.4 48.0 %collective-permute-start.62 = (bf16[256,2048]{1,0:T(8,128)(2,1)S(1)}, bf16[256,2048]{1,0:T(8,128)(2,1)S(1)}, u32[]{:S(2)}, u32[]{:S(2)}) collective-permute-start(bf16[256,2048]{1,0:T(8,128)(2,1)S(1)} %get-tuple-element.146), channel_id=1, source_target_pairs={{0,16},{1,17},{2,18},{3,19},{4,20},{5,21},{6,22},{7,23},{8,24},{9,... | collective-permute-start | bytes 3145736 | tf_op jit(solution)/shard_map/ppermute | solution.py:46
  422.8 48.1 %collective-permute-start.60 = (bf16[256,2048]{1,0:T(8,128)(2,1)S(1)}, bf16[256,2048]{1,0:T(8,128)(2,1)S(1)}, u32[]{:S(2)}, u32[]{:S(2)}) collective-permute-start(bf16[256,2048]{1,0:T(8,128)(2,1)S(1)} %get-tuple-element.144), channel_id=1, source_target_pairs={{0,8},{1,9},{2,10},{3,11},{4,12},{5,13},{6,14},{7,15},{8,0},{9,1},... | collective-permute-start | bytes 3145736 | tf_op jit(solution)/shard_map/ppermute | solution.py:46
  429.2 44.5 %collective-permute-start.32 = (bf16[256,2048]{1,0:T(8,128)(2,1)S(1)}, bf16[256,2048]{1,0:T(8,128)(2,1)S(1)}, u32[]{:S(2)}, u32[]{:S(2)}) collective-permute-start(bf16[256,2048]{1,0:T(8,128)(2,1)S(1)} %copy-done.48), channel_id=1, source_target_pairs={{0,4},{1,5},{2,6},{3,7},{4,0},{5,1},{6,2},{7,3},{8,12},{9,13},{10,... | collective-permute-start | bytes 3145736 | tf_op jit(solution)/shard_map/ppermute | solution.py:46
  431.8 60.0 %collective-permute-start.38 = (bf16[256,2048]{1,0:T(8,128)(2,1)S(1)}, bf16[256,2048]{1,0:T(8,128)(2,1)S(1)}, u32[]{:S(2)}, u32[]{:S(2)}) collective-permute-start(bf16[256,2048]{1,0:T(8,128)(2,1)S(1)} %get-tuple-element.152), channel_id=1, source_target_pairs={{0,24},{1,25},{2,26},{3,27},{4,28},{5,29},{6,30},{7,31},{8,16},{9,... | collective-permute-start | bytes 3145736 | tf_op jit(solution)/shard_map/ppermute | solution.py:46
  446.9 67.1 %collective-permute-start.36 = (bf16[256,2048]{1,0:T(8,128)(2,1)S(1)}, bf16[256,2048]{1,0:T(8,128)(2,1)S(1)}, u32[]{:S(2)}, u32[]{:S(2)}) collective-permute-start(bf16[256,2048]{1,0:T(8,128)(2,1)S(1)} %get-tuple-element.153), channel_id=1, source_target_pairs={{0,16},{1,17},{2,18},{3,19},{4,20},{5,21},{6,22},{7,23},{8,24},{9,... | collective-permute-start | bytes 3145736 | tf_op jit(solution)/shard_map/ppermute | solution.py:46
  469.4 44.6 %collective-permute-start.34 = (bf16[256,2048]{1,0:T(8,128)(2,1)S(1)}, bf16[256,2048]{1,0:T(8,128)(2,1)S(1)}, u32[]{:S(2)}, u32[]{:S(2)}) collective-permute-start(bf16[256,2048]{1,0:T(8,128)(2,1)S(1)} %get-tuple-element.151), channel_id=1, source_target_pairs={{0,8},{1,9},{2,10},{3,11},{4,12},{5,13},{6,14},{7,15},{8,0},{9,1},... | collective-permute-start | bytes 3145736 | tf_op jit(solution)/shard_map/ppermute | solution.py:46
  518.7 47.4 %collective-permute-start.66 = (bf16[256,2048]{1,0:T(8,128)(2,1)S(1)}, bf16[256,2048]{1,0:T(8,128)(2,1)}, u32[]{:S(2)}, u32[]{:S(2)}) collective-permute-start(bf16[256,2048]{1,0:T(8,128)(2,1)S(1)} %get-tuple-element.118), channel_id=1, source_target_pairs={{0,16},{1,17},{2,18},{3,19},{4,20},{5,21},{6,22},{7,23},{8,24},{9,... | collective-permute-start | bytes 3145736 | tf_op jit(solution)/shard_map/ppermute | solution.py:46
  519.8 46.3 %collective-permute-start.67 = (bf16[256,2048]{1,0:T(8,128)(2,1)S(1)}, bf16[256,2048]{1,0:T(8,128)(2,1)S(1)}, u32[]{:S(2)}, u32[]{:S(2)}) collective-permute-start(bf16[256,2048]{1,0:T(8,128)(2,1)S(1)} %get-tuple-element.118), channel_id=1, source_target_pairs={{0,24},{1,25},{2,26},{3,27},{4,28},{5,29},{6,30},{7,31},{8,16},{9,... | collective-permute-start | bytes 3145736 | tf_op jit(solution)/shard_map/ppermute | solution.py:46
  521.6 62.4 %collective-permute-start.68 = (bf16[256,2048]{1,0:T(8,128)(2,1)S(1)}, bf16[256,2048]{1,0:T(8,128)(2,1)S(1)}, u32[]{:S(2)}, u32[]{:S(2)}) collective-permute-start(bf16[256,2048]{1,0:T(8,128)(2,1)S(1)} %get-tuple-element.118), channel_id=1, source_target_pairs={{0,4},{1,5},{2,6},{3,7},{4,0},{5,1},{6,2},{7,3},{8,12},{9,13},{10,... | collective-permute-start | bytes 3145736 | tf_op jit(solution)/shard_map/ppermute | solution.py:46
  544.2 42.8 %collective-permute-start.69 = (bf16[256,2048]{1,0:T(8,128)(2,1)}, bf16[256,2048]{1,0:T(8,128)(2,1)S(1)}, u32[]{:S(2)}, u32[]{:S(2)}) collective-permute-start(bf16[256,2048]{1,0:T(8,128)(2,1)} %collective-permute-done.65), channel_id=1, source_target_pairs={{0,4},{1,5},{2,6},{3,7},{4,0},{5,1},{6,2},{7,3},{8,12},{9,13},{10,... | collective-permute-start | bytes 3145736 | tf_op jit(solution)/shard_map/ppermute | solution.py:46
  591.6 245.3 %reduce-scatter.5.cloned.1.call-start = ((), (), s32[]{:S(2)}) async-start(), calls=%async_computation.10 | async-start | bytes 3932160 | tf_op jit(solution)/shard_map/reduce_scatter | solution.py:136
  623.7 217.9 %reduce-scatter.11.cloned.1.call-start = ((), (), s32[]{:S(2)}) async-start(), calls=%async_computation.13 | async-start | bytes 5242880 | tf_op jit(solution)/shard_map/reduce_scatter | solution.py:151
  647.6 51.5 %collective-permute-start.40 = (bf16[64,2048]{1,0:T(8,128)(2,1)}, bf16[64,2048]{1,0:T(8,128)(2,1)}, u32[]{:S(2)}, u32[]{:S(2)}) collective-permute-start(bf16[64,2048]{1,0:T(8,128)(2,1)} %get-tuple-element.194), channel_id=1, source_target_pairs={{0,2},{1,3},{2,0},{3,1},{4,6},{5,7},{6,4},{7,5},{8,10},{9,11},{10,... | collective-permute-start | bytes 786440 | tf_op jit(solution)/shard_map/ppermute | solution.py:46
  648.3 50.8 %collective-permute-start.39 = (bf16[64,2048]{1,0:T(8,128)(2,1)}, bf16[64,2048]{1,0:T(8,128)(2,1)}, u32[]{:S(2)}, u32[]{:S(2)}) collective-permute-start(bf16[64,2048]{1,0:T(8,128)(2,1)} %get-tuple-element.195), channel_id=1, source_target_pairs={{0,1},{1,0},{2,3},{3,2},{4,5},{5,4},{6,7},{7,6},{8,9},{9,8},{10,11... | collective-permute-start | bytes 786440 | tf_op jit(solution)/shard_map/ppermute | solution.py:46
  658.4 47.4 %collective-permute-start.73 = (bf16[256,2048]{1,0:T(8,128)(2,1)}, bf16[256,2048]{1,0:T(8,128)(2,1)}, u32[]{:S(2)}, u32[]{:S(2)}) collective-permute-start(bf16[256,2048]{1,0:T(8,128)(2,1)} %get-tuple-element.136), channel_id=1, source_target_pairs={{0,4},{1,5},{2,6},{3,7},{4,0},{5,1},{6,2},{7,3},{8,12},{9,13},{10,... | collective-permute-start | bytes 3145736 | tf_op jit(solution)/shard_map/ppermute | solution.py:46
  658.4 47.4 %collective-permute-start.77 = (bf16[256,2048]{1,0:T(8,128)(2,1)}, bf16[256,2048]{1,0:T(8,128)(2,1)}, u32[]{:S(2)}, u32[]{:S(2)}) collective-permute-start(bf16[256,2048]{1,0:T(8,128)(2,1)} %get-tuple-element.134), channel_id=1, source_target_pairs={{0,4},{1,5},{2,6},{3,7},{4,0},{5,1},{6,2},{7,3},{8,12},{9,13},{10,... | collective-permute-start | bytes 3145736 | tf_op jit(solution)/shard_map/ppermute | solution.py:46
  662.9 42.9 %collective-permute-start.75 = (bf16[256,2048]{1,0:T(8,128)(2,1)}, bf16[256,2048]{1,0:T(8,128)(2,1)}, u32[]{:S(2)}, u32[]{:S(2)}) collective-permute-start(bf16[256,2048]{1,0:T(8,128)(2,1)} %get-tuple-element.135), channel_id=1, source_target_pairs={{0,4},{1,5},{2,6},{3,7},{4,0},{5,1},{6,2},{7,3},{8,12},{9,13},{10,... | collective-permute-start | bytes 3145736 | tf_op jit(solution)/shard_map/ppermute | solution.py:46
  711.3 47.1 %collective-permute-start.76 = (bf16[256,2048]{1,0:T(8,128)(2,1)S(1)}, bf16[256,2048]{1,0:T(8,128)(2,1)S(1)}, u32[]{:S(2)}, u32[]{:S(2)}) collective-permute-start(bf16[256,2048]{1,0:T(8,128)(2,1)S(1)} %get-tuple-element.139), channel_id=1, source_target_pairs={{0,16},{1,17},{2,18},{3,19},{4,20},{5,21},{6,22},{7,23},{8,24},{9,... | collective-permute-start | bytes 3145736 | tf_op jit(solution)/shard_map/ppermute | solution.py:46
  711.9 46.5 %collective-permute-start.74 = (bf16[256,2048]{1,0:T(8,128)(2,1)S(1)}, bf16[256,2048]{1,0:T(8,128)(2,1)S(1)}, u32[]{:S(2)}, u32[]{:S(2)}) collective-permute-start(bf16[256,2048]{1,0:T(8,128)(2,1)S(1)} %get-tuple-element.137), channel_id=1, source_target_pairs={{0,8},{1,9},{2,10},{3,11},{4,12},{5,13},{6,14},{7,15},{8,0},{9,1},... | collective-permute-start | bytes 3145736 | tf_op jit(solution)/shard_map/ppermute | solution.py:46
  712.6 52.7 %collective-permute-start.44 = (bf16[64,2048]{1,0:T(8,128)(2,1)S(1)}, bf16[64,2048]{1,0:T(8,128)(2,1)S(1)}, u32[]{:S(2)}, u32[]{:S(2)}) collective-permute-start(bf16[64,2048]{1,0:T(8,128)(2,1)S(1)} %get-tuple-element.189), channel_id=1, source_target_pairs={{0,24},{1,25},{2,26},{3,27},{4,28},{5,29},{6,30},{7,31},{8,16},{9,... | collective-permute-start | bytes 786440 | tf_op jit(solution)/shard_map/ppermute | solution.py:46
  717.1 52.0 %collective-permute-start.43 = (bf16[64,2048]{1,0:T(8,128)(2,1)S(1)}, bf16[64,2048]{1,0:T(8,128)(2,1)S(1)}, u32[]{:S(2)}, u32[]{:S(2)}) collective-permute-start(bf16[64,2048]{1,0:T(8,128)(2,1)S(1)} %get-tuple-element.190), channel_id=1, source_target_pairs={{0,16},{1,17},{2,18},{3,19},{4,20},{5,21},{6,22},{7,23},{8,24},{9,... | collective-permute-start | bytes 786440 | tf_op jit(solution)/shard_map/ppermute | solution.py:46
  765.2 39.2 %collective-permute-start.80 = (bf16[64,2048]{1,0:T(8,128)(2,1)}, bf16[64,2048]{1,0:T(8,128)(2,1)}, u32[]{:S(2)}, u32[]{:S(2)}) collective-permute-start(bf16[64,2048]{1,0:T(8,128)(2,1)} %get-tuple-element.175), channel_id=1, source_target_pairs={{0,2},{1,3},{2,0},{3,1},{4,6},{5,7},{6,4},{7,5},{8,10},{9,11},{10,... | collective-permute-start | bytes 786440 | tf_op jit(solution)/shard_map/ppermute | solution.py:46
  765.3 39.1 %collective-permute-start.79 = (bf16[64,2048]{1,0:T(8,128)(2,1)}, bf16[64,2048]{1,0:T(8,128)(2,1)S(1)}, u32[]{:S(2)}, u32[]{:S(2)}) collective-permute-start(bf16[64,2048]{1,0:T(8,128)(2,1)} %get-tuple-element.176), channel_id=1, source_target_pairs={{0,1},{1,0},{2,3},{3,2},{4,5},{5,4},{6,7},{7,6},{8,9},{9,8},{10,11... | collective-permute-start | bytes 786440 | tf_op jit(solution)/shard_map/ppermute | solution.py:46
  776.1 37.6 %collective-permute-start.87 = (f32[12,2048]{1,0:T(8,128)S(1)}, f32[12,2048]{1,0:T(8,128)}, u32[]{:S(2)}, u32[]{:S(2)}) collective-permute-start(f32[12,2048]{1,0:T(8,128)S(1)} %add.552), channel_id=1, source_target_pairs={{0,16},{1,17},{2,18},{3,19},{4,20},{5,21},{6,22},{7,23},{8,24},{9,... | collective-permute-start | bytes 294920 | tf_op jit(solution)/shard_map/ppermute | solution.py:46
  (136 other events, 2989.9 us)
Sparse Core Ops, SparseCore 0:
  27.8 82.3 all-gather.10
  111.8 47.6 all-gather.6
  161.0 79.2 all-gather.8
  242.3 79.2 all-gather.12
  415.0 74.2 reduce-scatter.8
  591.7 24.5 reduce-scatter.6
  623.8 74.4 reduce-scatter.4
  701.1 93.5 reduce-scatter.10

commit v2 on v1

v2 whole, which is shorter than its diff:
```python
from functools import partial

import jax
import jax.numpy as jnp
import numpy as np
from jax import lax
from jax.experimental import pallas as pl
from jax.experimental.pallas import tpu as pltpu
from jax.sharding import Mesh
from jax.sharding import PartitionSpec as P

HEADS = 16
HEAD_DIM = 128
GROUP = 8
CHIPS = GROUP // 2

EPS_NORM = 1e-05
EPS_ADAM = 1e-08
F32 = jnp.float32
BF16 = jnp.bfloat16
PLANE = ("chip", "core")
AXES = ("o",) + PLANE + ("z",)
VMEM_LIMIT = 56 * 1024 * 1024


def after(value, *others):
    return lax.optimization_barrier((value,) + others)[0]


def together(*values):
    return lax.optimization_barrier(values)


def dot(a, b):
    return jnp.dot(a, b, preferred_element_type=F32)


def dot_nt(a, b):
    return lax.dot_general(a, b, (((1,), (1,)), ((), ())), preferred_element_type=F32)


def dot_tn(a, b):
    return lax.dot_general(a, b, (((0,), (0,)), ((), ())), preferred_element_type=F32)


def swap_chips(value, k):
    return lax.ppermute(value, "chip", [(q, q ^ k) for q in range(CHIPS)])


def swap_cores(value):
    return lax.ppermute(value, "core", [(0, 1), (1, 0)])


def swap(value, axis, k):
    return lax.ppermute(value, axis, [(i, i ^ k) for i in range(lax.axis_size(axis))])


def sum_all(value):
    for axis in AXES:
        k = 1
        while k < lax.axis_size(axis):
            value = value + swap(value, axis, k)
            k *= 2
    return value


def trade(value, axes):
    return lax.all_to_all(value, axes, 0, 0, tiled=True)


def pick(stacked, index):
    return lax.dynamic_index_in_dim(stacked, index, 0, keepdims=False)


def plane_order(own):
    return [own] + [swap_chips(own, k) for k in range(1, CHIPS)]


def to_planes(parts):
    z = lax.axis_index("z")
    return [pick(parts, z)] + [swap(pick(parts, z ^ k), "z", k) for k in range(1, CHIPS)]


def in_z_order(natural):
    z = lax.axis_index("z")
    parts = natural.reshape(CHIPS, -1, natural.shape[1])
    return jnp.concatenate([pick(parts, z ^ k) for k in range(CHIPS)], axis=0)


def from_planes(block):
    parts = block.reshape(CHIPS, -1, block.shape[1])
    return [parts[0]] + [swap(parts[k], "z", k) for k in range(1, CHIPS)]


def to_owners(pieces):
    z = lax.axis_index("z")
    held = jnp.stack(pieces)
    return trade(jnp.concatenate([pick(held, z ^ q) for q in range(CHIPS)], axis=0), "chip")


def core_pieces(own_terms, other_terms):
    rows = own_terms.shape[0] // CHIPS
    arrived = swap_cores(other_terms)
    near = own_terms[:rows].astype(F32) + arrived[:rows].astype(F32)
    far = (own_terms[rows:].astype(F32) + arrived[rows:].astype(F32)).astype(BF16)
    return [near] + [far[k * rows : (k + 1) * rows] for k in range(CHIPS - 1)]


def chip_exchange(pieces):
    return pieces[:1] + [swap_chips(v, k) for k, v in enumerate(pieces) if k]


def add_up(pieces):
    return sum(v.astype(F32) for v in pieces)


def sum_parts(parts):
    return jnp.sum(parts.reshape(CHIPS, -1, parts.shape[1]).astype(F32), axis=0)


def chip_trade(pieces, chip):
    parts = jnp.stack([pieces[0].astype(BF16)] + pieces[1:])
    low = jnp.concatenate([pick(parts, chip ^ q) for q in range(CHIPS)], axis=0)
    return trade(low, "chip")


def trade_columns(weight, groups):
    rows, cols = weight.shape
    width = cols // (groups * GROUP)
    parts = weight.reshape(rows, groups, GROUP, width).transpose(2, 0, 1, 3)
    parts = parts.reshape(GROUP, rows, groups * width)
    return trade(parts, PLANE)


def side_by_side(stack, count):
    rows = stack.shape[0] // count
    return stack.reshape(count, rows, -1).transpose(1, 0, 2).reshape(rows, -1)


def stacked(wide, count):
    rows = wide.shape[0]
    return wide.reshape(rows, count, -1).transpose(1, 0, 2).reshape(count * rows, -1)


def in_row_order(full, width):
    o_size, z_size = lax.axis_size("o"), lax.axis_size("z")
    full = full.reshape(o_size, z_size, GROUP, -1, width).transpose(0, 2, 1, 3, 4)
    return full.reshape(-1, width)


def pair_up(parts, rows_weight, beside):
    width = parts.shape[2]
    flat = parts.reshape(-1, width)
    if lax.axis_size("o") > 1:
        return (flat, rows_weight)
    count = GROUP if beside else rows_weight.shape[1] // width
    return (jnp.concatenate([flat, after(stacked(rows_weight, count), ())], axis=1 if beside else 0),)


def gather_pair(pair, parts, rows_weight, p, beside):
    width = parts.shape[2]
    if len(pair) > 1:
        full = lax.all_gather(pair[0], ("o", "z"), axis=0, tiled=True)
        others = lax.all_gather(pair[1], AXES, axis=0, tiled=True)
        return in_row_order(full, width), pick(others.reshape(GROUP, -1, rows_weight.shape[1]), p)
    full = lax.all_gather(pair[0], "z", axis=0, tiled=False)
    first, second = jnp.split(full, [width if beside else parts.size // width], axis=2 if beside else 1)
    count = GROUP if beside else rows_weight.shape[1] // width
    second = [side_by_side(second[i], count) for i in range(full.shape[0])]
    return in_row_order(first, width), jnp.concatenate(second, axis=0)


def scatter_pair(grad_columns, grad_rows, rows, p):
    width = grad_columns.shape[1]
    if lax.axis_size("o") > 1:
        return scatter_columns(grad_columns), scatter_rows(grad_rows, p)
    z_size = lax.axis_size("z")
    beside = grad_rows.reshape(z_size, -1, grad_rows.shape[1])
    beside = after(jnp.concatenate([stacked(beside[i], GROUP) for i in range(z_size)], axis=0), ())
    both = jnp.concatenate([grad_columns, beside], axis=1)
    mine = lax.psum_scatter(both, "z", scatter_dimension=0, tiled=True)
    return mine[:, :width].reshape(GROUP, rows, width), side_by_side(mine[:, width:], GROUP)


def by_owner(grad, rows):
    o_size, z_size = lax.axis_size("o"), lax.axis_size("z")
    parts = grad.reshape(o_size, GROUP, z_size, rows, -1).transpose(0, 2, 1, 3, 4)
    return parts.reshape(grad.shape)


def scatter_columns(parts):
    mine = lax.psum_scatter(parts, ("o", "z"), scatter_dimension=0, tiled=True)
    return mine.reshape(GROUP, -1, parts.shape[1])


def trade_rows(parts):
    return trade(parts, PLANE)


def gather_rows(weight, p):
    if lax.axis_size("o") == 1:
        return lax.all_gather(weight, "z", axis=0, tiled=True)
    full = lax.all_gather(weight, AXES, axis=0, tiled=True)
    return pick(full.reshape(GROUP, -1, weight.shape[1]), p)


def scatter_rows(grad, p):
    if lax.axis_size("o") == 1:
        return lax.psum_scatter(grad, "z", scatter_dimension=0, tiled=True)
    full = jnp.zeros((GROUP,) + grad.shape, grad.dtype)
    full = lax.dynamic_update_index_in_dim(full, grad, p, 0)
    full = full.reshape(-1, grad.shape[1])
    return lax.psum_scatter(full, AXES, scatter_dimension=0, tiled=True)


def order_rows(pos_ref, blocks, rows):
    out = []
    for b in range(blocks):
        for q in range(CHIPS):
            held = ((q ^ pos_ref[0]) * blocks + (b ^ pos_ref[1])) * rows
            out.append(((b * CHIPS + q) * rows, pl.multiple_of(held, rows)))
    return out


def block_probs(q, keys, slope, start, scale):
    scores = dot_nt(q, keys) * scale
    row = lax.broadcasted_iota(jnp.int32, scores.shape, 0) + start
    col = lax.broadcasted_iota(jnp.int32, scores.shape, 1)
    scores = scores - slope * jnp.abs(row - col).astype(F32)
    expo = jnp.exp(scores - jnp.max(scores, axis=-1, keepdims=True))
    return expo * (1.0 / jnp.sum(expo, axis=-1, keepdims=True))


def attend_kernel(blocks, scale, pos_ref, slope_ref, q_ref, k_ref, v_ref, ctx_ref, qs, ks, vs):
    rows = q_ref.shape[0] // (blocks * CHIPS)
    block = rows * CHIPS
    slope = slope_ref[pl.program_id(0)]
    order = order_rows(pos_ref, blocks, rows)
    for nat, held in order:
        qs[nat : nat + rows] = q_ref[pl.ds(held, rows), :]
        ks[nat : nat + rows] = k_ref[pl.ds(held, rows), :]
        vs[nat : nat + rows] = v_ref[pl.ds(held, rows), :]
    for b in range(blocks):
        end = (b + 1) * block
        probs = block_probs(qs[b * block : end], ks[:end], slope, b * block, scale)
        ctx = dot(probs.astype(BF16), vs[:end]).astype(BF16)
        for q in range(CHIPS):
            held = order[b * CHIPS + q][1]
            ctx_ref[pl.ds(held, rows), :] = ctx[q * rows : (q + 1) * rows]


def attend_back_kernel(
    blocks, scale, pos_ref, slope_ref, q_ref, k_ref, v_ref, g_ref, gq_ref, gk_ref, gv_ref,
    qs, ks, vs, gs, gks, gvs,
):
    rows = q_ref.shape[0] // (blocks * CHIPS)
    block = rows * CHIPS
    slope = slope_ref[pl.program_id(0)]
    order = order_rows(pos_ref, blocks, rows)
    for nat, held in order:
        qs[nat : nat + rows] = q_ref[pl.ds(held, rows), :]
        ks[nat : nat + rows] = k_ref[pl.ds(held, rows), :]
        vs[nat : nat + rows] = v_ref[pl.ds(held, rows), :]
        gs[nat : nat + rows] = g_ref[pl.ds(held, rows), :]
    for b in reversed(range(blocks)):
        start, end = b * block, (b + 1) * block
        q, g = qs[start:end], gs[start:end]
        keys, values = ks[:end], vs[:end]
        probs = block_probs(q, keys, slope, start, scale)
        grad_values = dot_tn(probs.astype(BF16), g)
        grad_probs = dot_nt(g, values)
        inner = jnp.sum(probs * grad_probs, axis=-1, keepdims=True)
        grad_scores = (probs * (grad_probs - inner)).astype(BF16)
        grad_q = (dot(grad_scores, keys) * scale).astype(BF16)
        grad_keys = dot_tn(grad_scores, q)
        if b == blocks - 1:
            gks[...] = grad_keys
            gvs[...] = grad_values
        else:
            gks[:end] += grad_keys
            gvs[:end] += grad_values
        for c in range(CHIPS):
            held = order[b * CHIPS + c][1]
            gq_ref[pl.ds(held, rows), :] = grad_q[c * rows : (c + 1) * rows]
    for nat, held in order:
        gk_ref[pl.ds(held, rows), :] = (gks[nat : nat + rows] * scale).astype(BF16)
        gv_ref[pl.ds(held, rows), :] = gvs[nat : nat + rows].astype(BF16)


def attend(qkv, place, slopes):
    length, heads = qkv.shape[0], qkv.shape[1] // (3 * HEAD_DIM)
    blocks = lax.axis_size("z")
    smem = pl.BlockSpec(memory_space=pltpu.SMEM)
    column = lambda first: pl.BlockSpec((length, HEAD_DIM), lambda h: (0, first + h))
    held = pltpu.VMEM((length, HEAD_DIM), BF16)
    return pl.pallas_call(
        partial(attend_kernel, blocks, HEAD_DIM**-0.5),
        grid=(heads,),
        in_specs=[smem, smem, column(0), column(heads), column(2 * heads)],
        out_specs=column(0),
        out_shape=jax.ShapeDtypeStruct((length, heads * HEAD_DIM), BF16),
        scratch_shapes=[held] * 3,
        compiler_params=pltpu.CompilerParams(vmem_limit_bytes=VMEM_LIMIT),
        cost_estimate=pl.CostEstimate(
            flops=6 * length * length * HEAD_DIM * heads,
            bytes_accessed=16 * length * heads * HEAD_DIM,
            transcendentals=2 * length * length * heads,
        ),
    )(place, slopes, qkv, qkv, qkv)


def attend_back(qkv, grad_ctx, place, slopes):
    length, heads = qkv.shape[0], qkv.shape[1] // (3 * HEAD_DIM)
    blocks = lax.axis_size("z")
    smem = pl.BlockSpec(memory_space=pltpu.SMEM)
    column = lambda first: pl.BlockSpec((length, HEAD_DIM), lambda h: (0, first + h))
    held = pltpu.VMEM((length, HEAD_DIM), BF16)
    wide = pltpu.VMEM((length, HEAD_DIM), F32)
    return pl.pallas_call(
        partial(attend_back_kernel, blocks, HEAD_DIM**-0.5),
        grid=(heads,),
        in_specs=[smem, smem, column(0), column(heads), column(2 * heads), column(0)],
        out_specs=[column(0)] * 3,
        out_shape=[jax.ShapeDtypeStruct((length, heads * HEAD_DIM), BF16)] * 3,
        scratch_shapes=[held] * 4 + [wide] * 2,
        compiler_params=pltpu.CompilerParams(vmem_limit_bytes=VMEM_LIMIT),
        cost_estimate=pl.CostEstimate(
            flops=16 * length * length * HEAD_DIM * heads,
            bytes_accessed=28 * length * heads * HEAD_DIM,
            transcendentals=2 * length * length * heads,
        ),
    )(place, slopes, qkv, qkv, qkv, grad_ctx)


def feed_kernel(norm_ref, top_ref, up_ref, down_ref, bias_ref, hidden_ref, grad_ref, term_ref):
    pre = dot(norm_ref[...], up_ref[...]) + bias_ref[...]
    scale = (2.0 / np.pi) ** 0.5
    square = pre * pre
    bend = jnp.tanh(scale * (pre + 0.044715 * (pre * square)))
    cdf = 0.5 + 0.5 * bend
    hidden_ref[...] = (pre * cdf).astype(BF16)
    slope = cdf + (0.5 * scale) * pre * (1.0 - bend * bend) * (1.0 + (3.0 * 0.044715) * square)
    grad = (dot_nt(top_ref[...], down_ref[...]) * slope).astype(BF16)
    grad_ref[...] = grad
    term_ref[...] = dot_nt(grad, up_ref[...]).astype(BF16)


def feed(normed, top, w_up, w_down, bias):
    rows, width = normed.shape
    part = w_up.shape[1]
    tile = min(rows, 256)
    wide = pl.BlockSpec((tile, width), lambda i: (i, 0))
    slim = pl.BlockSpec((tile, part), lambda i: (i, 0))
    whole = lambda v: pl.BlockSpec(v.shape, lambda i: (0, 0))
    bias = bias.reshape(1, part)
    return pl.pallas_call(
        feed_kernel,
        grid=(rows // tile,),
        in_specs=[wide, wide, whole(w_up), whole(w_down), whole(bias)],
        out_specs=[slim, slim, wide],
        out_shape=[
            jax.ShapeDtypeStruct((rows, part), BF16),
            jax.ShapeDtypeStruct((rows, part), BF16),
            jax.ShapeDtypeStruct((rows, width), BF16),
        ],
        compiler_params=pltpu.CompilerParams(vmem_limit_bytes=VMEM_LIMIT),
        cost_estimate=pl.CostEstimate(
            flops=6 * rows * width * part,
            bytes_accessed=6 * rows * width + 4 * rows * part + 4 * width * part,
            transcendentals=rows * part,
        ),
    )(normed, top, w_up, w_down, bias)


def weight_kernel(count, left_0, left_1, *refs):
    rights, out_ref = refs[:-1], refs[-1]
    first = 0
    for i in range(count):
        a, b = rights[2 * i], rights[2 * i + 1]
        cols = a.shape[1]
        out = dot_tn(left_0[...], a[...]) + dot_tn(left_1[...], b[...])
        out_ref[..., first : first + cols] = out.astype(BF16).reshape(out_ref.shape[:-1] + (cols,))
        first += cols


def weight_grad(left, rights, owner_rows=None):
    rows, width = left[0].shape
    cols = sum(r[0].shape[1] for r in rights)
    if owner_rows and lax.axis_size("o") > 1:
        joined = [jnp.concatenate(v, axis=1) for v in zip(*rights)]
        grad = (dot_tn(left[0], joined[0]) + dot_tn(left[1], joined[1])).astype(BF16)
        return by_owner(grad, owner_rows)
    tile = 256
    if owner_rows:
        z_size = lax.axis_size("z")
        tile = z_size * owner_rows
        shape = (z_size, width // tile, owner_rows, cols)
        out_spec = pl.BlockSpec((z_size, 1, owner_rows, cols), lambda i: (0, i, 0, 0))
    else:
        shape = (width, cols)
        out_spec = pl.BlockSpec((tile, cols), lambda i: (i, 0))
    flat = [v for r in rights for v in r]
    out = pl.pallas_call(
        partial(weight_kernel, len(rights)),
        grid=(width // tile,),
        in_specs=[pl.BlockSpec((rows, tile), lambda i: (0, i))] * 2
        + [pl.BlockSpec(v.shape, lambda i: (0, 0)) for v in flat],
        out_specs=out_spec,
        out_shape=jax.ShapeDtypeStruct(shape, BF16),
        compiler_params=pltpu.CompilerParams(vmem_limit_bytes=VMEM_LIMIT),
        cost_estimate=pl.CostEstimate(
            flops=4 * rows * width * cols,
            bytes_accessed=4 * rows * (width + cols) + 2 * width * cols,
            transcendentals=0,
        ),
    )(*left, *flat)
    return out.reshape(width, cols)


def terms_kernel(*refs):
    weight_ref, out_ref = refs[-2:]
    total, first = 0.0, 0
    for ref in refs[:-2]:
        total = total + dot_nt(ref[...], weight_ref[:, first : first + ref.shape[1]])
        first += ref.shape[1]
    out_ref[...] = total.astype(BF16)


def terms(lefts, weight):
    rows, width = lefts[0].shape[0], weight.shape[0]
    tile = min(rows, 256)
    return pl.pallas_call(
        terms_kernel,
        grid=(rows // tile,),
        in_specs=[pl.BlockSpec((tile, v.shape[1]), lambda i: (i, 0)) for v in lefts]
        + [pl.BlockSpec(weight.shape, lambda i: (0, 0))],
        out_specs=pl.BlockSpec((tile, width), lambda i: (i, 0)),
        out_shape=jax.ShapeDtypeStruct((rows, width), BF16),
        compiler_params=pltpu.CompilerParams(vmem_limit_bytes=VMEM_LIMIT),
        cost_estimate=pl.CostEstimate(
            flops=2 * rows * weight.size,
            bytes_accessed=2 * weight.size + 4 * rows * width,
            transcendentals=0,
        ),
    )(*lefts, weight)


def norm_forward(values, gain, shift):
    centre = values - jnp.mean(values, axis=-1, keepdims=True)
    factor = lax.rsqrt(jnp.mean(centre * centre, axis=-1, keepdims=True) + EPS_NORM)
    normed = centre * factor
    return (normed * gain + shift, normed, factor)


def norm_backward(incoming, normed, factor, gain):
    scaled = incoming * gain
    input_grad = factor * (
        scaled
        - jnp.mean(scaled, axis=-1, keepdims=True)
        - normed * jnp.mean(scaled * normed, axis=-1, keepdims=True)
    )
    return (input_grad, jnp.sum(incoming * normed, axis=0), jnp.sum(incoming, axis=0))


def adam_step(weight, first, second, grad, scalars):
    clip, keep_first, keep_second, fix_first, fix_second, rate, decay = scalars
    scaled = grad * clip
    first = keep_first * first + (1.0 - keep_first) * scaled
    second = keep_second * second + (1.0 - keep_second) * scaled * scaled
    change = -rate * (
        first * fix_first / (jnp.sqrt(second * fix_second) + EPS_ADAM) + decay * weight
    )
    return first, second, change


def adam_kernel(as_step, scalar_ref, weight_ref, moment_ref, grad_ref, out_ref, new_ref):
    scalars = [scalar_ref[i] for i in range(7)]
    weight = weight_ref[...].astype(F32)
    grad = grad_ref[...].reshape(weight.shape).astype(F32)
    first, second, change = adam_step(weight, moment_ref[0], moment_ref[1], grad, scalars)
    new_ref[0] = first
    new_ref[1] = second
    out_ref[...] = change if as_step else (weight + change).astype(BF16)


def adam_update(weight, moments, grad, scalars, as_step=False):
    rows, cols = weight.shape
    if grad.ndim == 2:
        high, wide = (16 if cols > 4096 else max(16, rows // 4)), cols
        grid, where, grad_block, grad_where = (rows // high,), (lambda i: (i, 0)), (high, wide), (lambda i: (i, 0))
    else:
        high, wide = rows, grad.shape[2]
        grid, where, grad_block, grad_where = (GROUP,), (lambda i: (0, i)), (1, rows, wide), (lambda i: (i, 0, 0))
    tile = pl.BlockSpec((high, wide), where)
    pair = pl.BlockSpec((2, high, wide), lambda i: (0,) + where(i))
    return pl.pallas_call(
        partial(adam_kernel, as_step),
        grid=grid,
        in_specs=[
            pl.BlockSpec(memory_space=pltpu.SMEM),
            tile,
            pair,
            pl.BlockSpec(grad_block, grad_where),
        ],
        out_specs=[tile, pair],
        out_shape=[
            jax.ShapeDtypeStruct(weight.shape, F32 if as_step else BF16),
            jax.ShapeDtypeStruct(moments.shape, F32),
        ],
        compiler_params=pltpu.CompilerParams(vmem_limit_bytes=VMEM_LIMIT),
        cost_estimate=pl.CostEstimate(
            flops=20 * weight.size, bytes_accessed=22 * weight.size, transcendentals=weight.size
        ),
    )(scalars, weight, moments, grad)


def column_sum(values):
    return jnp.sum(values.astype(F32), axis=0)


def body(
    tokens,
    cotangent,
    qkv_weight,
    out_weight,
    up_weight,
    down_weight,
    vectors,
    qkv_moments,
    out_moments,
    up_moments,
    down_moments,
    vector_moments,
    step,
    hyper,
):
    chip = lax.axis_index("chip")
    p = lax.axis_index(PLANE)
    devices = lax.axis_size(AXES)
    width = tokens.shape[2]
    place = jnp.stack([chip, lax.axis_index("z")]).astype(jnp.int32)
    heads = HEADS // GROUP
    head_ids = (p * heads + jnp.arange(heads)).astype(F32)
    slopes = jnp.exp2(-8.0 * (head_ids + 1.0) / HEADS)
    tokens_given, top_given = tokens[0], cotangent[0]

    flat = lax.axis_index(AXES)
    vecs = lax.dynamic_update_slice(
        jnp.zeros((vectors.shape[0], width), BF16), vectors, (0, flat * vectors.shape[1])
    )
    vecs = sum_all(vecs).astype(F32)
    qkv_parts = trade_columns(qkv_weight, 3)
    pair_qkv = pair_up(qkv_parts, out_weight, True)
    tokens_given, pair_qkv = together(tokens_given, pair_qkv)
    rows_low = trade(trade(tokens_given, "chip"), "z")
    rows_low, pair_qkv = together(rows_low, pair_qkv)
    full_qkv, full_out = gather_pair(pair_qkv, qkv_parts, out_weight, p, True)
    top_given, up_weight, rows_low = together(top_given, up_weight, rows_low)
    held_top = trade(top_given, "chip")
    up_parts = trade_columns(up_weight, 1)
    rows_low, up_parts, held_top = together(rows_low, up_parts, held_top)
    rows_in = in_z_order(rows_low).astype(F32)
    normed, hat_one, factor_one = norm_forward(rows_in, vecs[0], vecs[1])
    normed_low, held_top = together(normed.astype(BF16), held_top)
    own = plane_order(normed_low)
    top_low = trade(held_top, "z")
    own, top_low, up_parts, w_qkv, w_out = together(own, top_low, up_parts, full_qkv, full_out)
    top_low = in_z_order(top_low)
    full_up = lax.all_gather(up_parts, ("o", "z"), axis=0, tiled=True)
    full_down = gather_rows(down_weight, p)
    own = jnp.concatenate(own, axis=0)
    own, top_low = together(own, top_low)
    normed_a = [own, swap_cores(own)]
    top_own = plane_order(top_low)
    part = width // GROUP
    bias_q = lax.dynamic_slice(vecs[2], (p * part,), (part,))
    bias_v = lax.dynamic_slice(vecs[3], (p * part,), (part,))
    bias_qkv = jnp.concatenate([bias_q, jnp.zeros_like(bias_q), bias_v])
    qkv = [(dot(v, w_qkv) + bias_qkv).astype(BF16) for v in normed_a]
    context = [attend(v, place, slopes) for v in qkv]
    context, top_own = together(context, top_own)
    top_own = jnp.concatenate(top_own, axis=0)
    term_other = dot(context[1], w_out).astype(BF16)
    term_own = dot(after(context[0], term_other), w_out).astype(BF16)
    pieces = chip_exchange(core_pieces(term_own, term_other))
    pieces, top_own, full_up = together(pieces, top_own, full_up)
    w_up = in_row_order(full_up, up_parts.shape[2])
    residual = rows_in + add_up(pieces) + vecs[4]
    normed, hat_two, factor_two = norm_forward(residual, vecs[5], vecs[6])
    normed_low = normed.astype(BF16)
    own = plane_order(normed_low)
    grad_mlp = [top_own, swap_cores(top_own)]
    own, grad_mlp, w_down, w_up = together(own, grad_mlp, full_down, w_up)
    own = jnp.concatenate(own, axis=0)
    normed_b = [own, swap_cores(own)]
    hidden_part = w_up.shape[1]
    bias_up = lax.dynamic_slice(vecs[8:].reshape(-1), (p * hidden_part,), (hidden_part,))

    hidden_other, grad_other, term_other = feed(normed_b[1], grad_mlp[1], w_up, w_down, bias_up)
    left, term_other = together(normed_b[0], term_other)
    hidden_own, grad_own, term_own = feed(left, grad_mlp[0], w_up, w_down, bias_up)
    hidden, grad_pre = [hidden_own, hidden_other], [grad_own, grad_other]
    pieces, held = together(core_pieces(term_own, term_other), hidden)
    grad_down = weight_grad(held, [grad_mlp])
    owned_down = scatter_rows(grad_down, p)
    pieces = chip_exchange(pieces)
    held, grad_down = together(grad_pre, grad_down)
    grad_up = weight_grad(normed_b, [held], up_weight.shape[0])
    pieces, grad_up = together(pieces, grad_up)
    grad_normed = add_up(pieces)
    through, gain_two_grad, shift_two_grad = norm_backward(grad_normed, hat_two, factor_two, vecs[5])
    grad_residual = top_low.astype(F32) + through
    grad_attn_own = grad_residual.astype(BF16)

    own = plane_order(grad_attn_own)
    held, grad_attn_own = together(hidden, grad_attn_own)
    mlp_other = dot(held[1], w_down).astype(BF16)
    mlp_own = dot(after(held[0], mlp_other), w_down).astype(BF16)
    reduced_up = scatter_columns(grad_up)
    mlp_sums = core_pieces(mlp_own, mlp_other)
    own, mlp_sums, owned_down = together(own, mlp_sums, owned_down)
    own = jnp.concatenate(own, axis=0)
    own, mlp_sums = together(own, mlp_sums)
    grad_attn = [own, swap_cores(own)]

    mlp_parts = chip_trade(mlp_sums, chip)
    grad_context = [dot_nt(v, w_out).astype(BF16) for v in grad_attn]
    grads = [attend_back(v, g, place, slopes) for v, g in zip(qkv, grad_context)]
    grads, reduced_up = together(grads, reduced_up)
    grad_qkv_weight = weight_grad(normed_a, list(zip(*grads)), qkv_weight.shape[0])
    held, grad_attn, grad_qkv_weight = together(context, grad_attn, grad_qkv_weight)
    grad_out = (dot_tn(held[0], grad_attn[0]) + dot_tn(held[1], grad_attn[1])).astype(BF16)
    grads, grad_out, mlp_parts = together(grads, grad_out, mlp_parts)
    term_other = terms(grads[1], w_qkv)
    owned_up = trade_rows(reduced_up)
    held, term_other, owned_up = together(grads[0], term_other, owned_up)
    term_own = terms(held, w_qkv)
    pieces = core_pieces(term_own, term_other)
    reduced_qkv, owned_out = scatter_pair(
        grad_qkv_weight, grad_out, qkv_weight.shape[0], p
    )
    pieces = chip_exchange(pieces)
    grad_normed = add_up(pieces)
    through, gain_one_grad, shift_one_grad = norm_backward(grad_normed, hat_one, factor_one, vecs[0])
    result = (residual + sum_parts(mlp_parts) + vecs[7]).astype(BF16)
    result, reduced_qkv = together(result, reduced_qkv)
    owned_qkv = trade_rows(reduced_qkv)
    bias_grads = [column_sum(grads[0][i]) + column_sum(grads[1][i]) for i in (0, 2)]
    up_bias_grad = column_sum(grad_own) + column_sum(grad_other)
    wide = lambda v: lax.dynamic_update_slice(jnp.zeros((width,), F32), v, (p * part,))
    up_wide = lax.dynamic_update_slice(
        jnp.zeros((GROUP * hidden_part,), F32), up_bias_grad, (p * hidden_part,)
    )
    vector_grad = jnp.concatenate(
        [
            jnp.stack(
                [
                    gain_one_grad,
                    shift_one_grad,
                    wide(bias_grads[0]),
                    wide(bias_grads[1]),
                    column_sum(grad_attn_own),
                    gain_two_grad,
                    shift_two_grad,
                    column_sum(top_given),
                ]
            ),
            up_wide.reshape(-1, width),
        ],
        axis=0,
    )
    vec_parts = vector_grad.reshape(vectors.shape[0], devices, -1).transpose(1, 0, 2)
    owned_vec = jnp.sum(trade(vec_parts, AXES), axis=0)

    grad_qkv_rows = owned_qkv.reshape(GROUP, -1, 3, part).transpose(1, 2, 0, 3).reshape(qkv_weight.shape)
    squares = [jnp.sum(jnp.square(g.astype(F32))) for g in (owned_qkv, owned_out, owned_up, owned_down, owned_vec)]
    squares = jnp.broadcast_to(sum(squares), (devices, 1))
    grad_norm = jnp.sqrt(jnp.sum(trade(squares, AXES)))
    back = (grad_residual + through).astype(BF16)
    result, back = from_planes(result), from_planes(back)
    result, back, grad_norm = together(result, back, grad_norm)
    both = to_owners([jnp.concatenate(v, axis=1) for v in zip(result, back)])
    clip_factor = jnp.minimum(1.0, hyper[4] / (grad_norm + 1e-06))
    step_float = step.astype(F32)
    fix_first = 1.0 / (1.0 - hyper[2] ** step_float)
    fix_second = 1.0 / (1.0 - hyper[3] ** step_float)
    scalars = [clip_factor, hyper[2], hyper[3], fix_first, fix_second, hyper[0], hyper[1]]
    listed = jnp.stack(scalars)
    new_qkv, new_qkv_moments = adam_update(qkv_weight, qkv_moments, grad_qkv_rows, listed)
    out_step, new_out_moments = adam_update(out_weight, out_moments, owned_out, listed, as_step=True)
    new_up, new_up_moments = adam_update(up_weight, up_moments, owned_up, listed)
    new_down, new_down_moments = adam_update(down_weight, down_moments, owned_down, listed)
    both, new_qkv, out_step, new_up, new_down = together(both, new_qkv, out_step, new_up, new_down)
    activations, input_grad = both[:, :width], both[:, width:]
    first, second, vector_step = adam_step(
        vectors.astype(F32), vector_moments[0], vector_moments[1], owned_vec, scalars
    )
    return (
        activations[None],
        input_grad[None],
        grad_norm,
        new_qkv,
        out_step,
        new_up,
        new_down,
        vector_step,
        new_qkv_moments,
        new_out_moments,
        new_up_moments,
        new_down_moments,
        jnp.stack([first, second]),
    )


def solution(mesh):
    devices = np.asarray(mesh.devices)
    planes = Mesh(devices.reshape(-1, CHIPS, 2, devices.shape[1]), AXES)
    rows = P(AXES, None)
    seqs = P(("o",) + PLANE, "z", None)
    pair = P(None, AXES, None)
    cols = P(None, AXES)
    return jax.shard_map(
        body,
        mesh=planes,
        in_specs=(seqs, seqs, rows, rows, rows, rows, cols)
        + (pair, pair, pair, pair, P(None, None, AXES), P(), P()),
        out_specs=(seqs, seqs, P(), rows, rows, rows, rows, cols)
        + (pair, pair, pair, pair, P(None, None, AXES)),
        check_vma=False,
    )
```

time: 944 us -> 844 us (0.89)
  waiting for transfers between devices: 440 us -> 316 us
  Pallas kernels: 30.6 us -> 149 us
  matrix products: 153 us -> 51.4 us
  blocking collectives: 17.8 us -> 67.8 us
  local copies, waits for them, and re-layouts: 82.8 us -> 52.5 us
  starting transfers between devices: 105 us -> 77 us
  other arithmetic: 78.9 us -> 96 us
    ppermute x95 -> x40, waiting for transfers between devices: 414 us -> 191 us  [the longest x21 151 us: swap_chips(): return lax.ppermute(value, 'chip', [(q, q ^ k) for q in range(CHIPS)])]
    pallas_call x0 -> x11, Pallas kernels: none -> 118 us  [the longest x3 41 us: weight_grad(): pl.pallas_call(partial(weight_kernel, len(rights)), grid=(width // tile,)...]
    ppermute x95 -> x40, starting transfers between devices: 93.4 us -> 37.8 us  [the longest x21 24.7 us: swap_chips(): return lax.ppermute(value, 'chip', [(q, q ^ k) for q in range(CHIPS)])]
    all_to_all x1 -> x3, blocking collectives: 17.8 us -> 67.8 us  [trade(): return lax.all_to_all(value, axes, 0, 0, tiled=True)]
    dot_general x8 -> x2, matrix products: 56.2 us -> 8.13 us  [dot_tn(): lax.dot_general(a, b, (((0,), (0,)), ((), ())), preferred_element_type=F32)]
    dot_general x8 -> x2, matrix products: 52.6 us -> 8.85 us  [dot_nt(): lax.dot_general(a, b, (((1,), (1,)), ((), ())), preferred_element_type=F32)]
    all_gather x2 -> x1, waiting for transfers between devices: 0.01 us -> 40 us  [gather_rows(): return lax.all_gather(weight, 'z', axis=0, tiled=True)]
    all_gather x2, waiting for transfers between devices: 16.3 us -> 46.7 us  [the longest x1 37.8 us: gather_pair(): full = lax.all_gather(pair[0], 'z', axis=0, tiled=False)]
  transfers between devices with their start and end apart: 106 -> 55, of which waited for: 41 -> 29; matrix products, arithmetic and copies ran while one was open for 24% -> 20% of each run, Pallas kernels for 3% -> 14%
where the time goes in v2:
time: 844 us; the launch traced here: 835 us
  waiting for transfers between devices  316 us (37%)
  Pallas kernels  149 us (18%)
  other arithmetic  96 us (11%)
  starting transfers between devices  77 us (9%)
  blocking collectives  67.8 us (8%)
  local copies, waits for them, and re-layouts  52.5 us (6%)
  matrix products  51.4 us (6%)
  between operations  25.1 us (3%)
    ppermute x21, waiting for transfers between devices, swap_chips(): return lax.ppermute(value, 'chip', [(q, q ^ k) for q in range(CHIPS)])  151 us
    all_to_all x3, blocking collectives, trade(): return lax.all_to_all(value, axes, 0, 0, tiled=True)  67.8 us
    pallas_call x3, Pallas kernels, weight_grad(): pl.pallas_call(partial(weight_kernel, len(rights)), grid=(width // tile,)...  41 us
    all_gather x1, waiting for transfers between devices, gather_rows(): return lax.all_gather(weight, 'z', axis=0, tiled=True)  40 us
    all_to_all x9, starting transfers between devices, trade(): return lax.all_to_all(value, axes, 0, 0, tiled=True)  38.7 us
    pallas_call x2, Pallas kernels, feed(): pl.pallas_call(feed_kernel, grid=(rows // tile,), in_specs=[wide, wide, w...  38.3 us
    all_gather x1, waiting for transfers between devices, gather_pair(): full = lax.all_gather(pair[0], 'z', axis=0, tiled=False)  37.8 us
    dot_general x6, matrix products, dot(): return jnp.dot(a, b, preferred_element_type=F32)  34.5 us
  transfers between devices with their start and end apart: 55, of which 29 were waited for; matrix products, arithmetic and copies ran while one was open for 20% of the time, Pallas kernels for 14%

profile of v2, /device:TPU:0, one launch (start us, length us, event | category | flops | bytes accessed | tf_op | source)
XLA Modules:
  0.0 835.0 jit_solution(149583122439730623)
XLA Ops:
  10.6 5.3 all-to-all-start
  16.1 12.4 %all-to-all-done = bf16[8,64,768]{2,1,0:T(8,128)(2,1)S(1)} async-done(((bf16[8,64,768]{2,1,0:T(8,128)(2,1)}), bf16[8,64,768]{2,1,0:T(8,128)(2,1)S(1)}, u32[]{:S(2)}, u32[]{:S(2)}) %all-to-all-start) | async-done | bytes 786464 | tf_op jit(solution)/shard_map/all_to_all | solution.py:68
  29.6 15.9 %all_to_all.97 = bf16[4,64,2048]{2,1,0:T(8,128)(2,1)S(1)} all-to-all(bf16[4,64,2048]{2,1,0:T(8,128)(2,1)S(1)} %bitcast.244), channel_id=1, replica_groups=mesh['o'=1,'chip'=4,'core'=2,'z'=4] {'chip'}, dimensions={0} | all-to-all | bytes 2097152 | tf_op jit(solution)/shard_map/all_to_all | solution.py:68
  45.5 28.2 %all_to_all.98 = bf16[4,64,2048]{2,1,0:T(8,128)(2,1)S(1)} all-to-all(bf16[4,64,2048]{2,1,0:T(8,128)(2,1)S(1)} %all_to_all.97), channel_id=1, replica_groups=mesh['o'=1,'chip'=4,'core'=2,'z'=4] {'z'}, dimensions={0} | all-to-all | bytes 2097152 | tf_op jit(solution)/shard_map/all_to_all | solution.py:68
  79.7 11.1 %collective-permute-done = bf16[12,2048]{1,0:T(8,128)(2,1)S(1)} collective-permute-done((bf16[12,2048]{1,0:T(8,128)(2,1)S(1)}, bf16[12,2048]{1,0:T(8,128)(2,1)S(1)}, u32[]{:S(2)}, u32[]{:S(2)}) %collective-permute-start) | collective-permute-done | bytes 49184 | tf_op jit(solution)/shard_map/ppermute | solution.py:55
  96.8 9.4 %collective-permute-done.3 = bf16[12,2048]{1,0:T(8,128)(2,1)S(1)} collective-permute-done((bf16[12,2048]{1,0:T(8,128)(2,1)S(1)}, bf16[12,2048]{1,0:T(8,128)(2,1)S(1)}, u32[]{:S(2)}, u32[]{:S(2)}) %collective-permute-start.3) | collective-permute-done | bytes 49184 | tf_op jit(solution)/shard_map/ppermute | solution.py:55
  116.7 10.7 %all-to-all-done.3 = bf16[8,64,1024]{2,1,0:T(8,128)(2,1)S(1)} async-done(((bf16[8,64,1024]{2,1,0:T(8,128)(2,1)}), bf16[8,64,1024]{2,1,0:T(8,128)(2,1)S(1)}, u32[]{:S(2)}, u32[]{:S(2)}) %all-to-all-start.3) | async-done | bytes 1048608 | tf_op jit(solution)/shard_map/all_to_all | solution.py:68
  130.6 4.8 all-to-all-start.5
  138.8 37.8 %all-gather.9.cloned.1.call-done = bf16[2048,1024]{1,0:T(8,128)(2,1)} async-done(((bf16[512,1024]{1,0:T(8,128)(2,1)}), bf16[2048,1024]{1,0:T(8,128)(2,1)}) %all-gather.9.cloned.1.call-update) | async-done | bytes 4194320 | tf_op jit(solution)/shard_map/all_gather | solution.py:166
  192.4 7.7 add_convert_fusion.5.q_ref.k_ref.v_ref
  200.1 6.7 shard_map.237
  206.8 6.8 add_convert_fusion.4.q_ref.k_ref.v_ref
  213.6 6.5 shard_map.238
  220.1 16.8 %collective-permute-done.11 = bf16[256,2048]{1,0:T(8,128)(2,1)} collective-permute-done((bf16[256,2048]{1,0:T(8,128)(2,1)S(1)}, bf16[256,2048]{1,0:T(8,128)(2,1)}, u32[]{:S(2)}, u32[]{:S(2)}) %collective-permute-start.11) | collective-permute-done | bytes 1048608 | tf_op jit(solution)/shard_map/ppermute | solution.py:47
  243.6 5.1 collective-permute-done.12
  264.1 8.9 %all-gather.5.cloned.1.call-done = bf16[32,64,1024]{2,1,0:T(8,128)(2,1)} async-done(((bf16[8,64,1024]{2,1,0:T(8,128)(2,1)}), bf16[32,64,1024]{2,1,0:T(8,128)(2,1)}) %all-gather.5.cloned.1.call-update) | async-done | bytes 4194320 | tf_op jit(solution)/shard_map/all_gather | solution.py:569
  273.0 6.9 collective-permute-done.13
  279.9 23.0 %collective-permute-done.14 = bf16[256,2048]{1,0:T(8,128)(2,1)} collective-permute-done((bf16[256,2048]{1,0:T(8,128)(2,1)}, bf16[256,2048]{1,0:T(8,128)(2,1)}, u32[]{:S(2)}, u32[]{:S(2)}) %collective-permute-start.14) | collective-permute-done | bytes 1048608 | tf_op jit(solution)/shard_map/ppermute | solution.py:47
  313.9 40.0 %all-gather.7.cloned.1.call-done.down_ref = bf16[1024,2048]{1,0:T(8,128)(2,1)} async-done(((bf16[256,2048]{1,0:T(8,128)(2,1)}), bf16[1024,2048]{1,0:T(8,128)(2,1)}) %all-gather.7.cloned.1.call-update) | async-done | bytes 4194320 | tf_op jit(solution)/shard_map/all_gather | solution.py:202
  366.5 6.9 collective-permute-done.20.norm_ref.left_1
  373.3 19.1 %shard_map.239 = (bf16[1024,1024]{1,0:T(8,128)(2,1)}, bf16[1024,1024]{1,0:T(8,128)(2,1)}, bf16[1024,2048]{1,0:T(8,128)(2,1)}) custom-call(bf16[1024,2048]{1,0:T(8,128)(2,1)} %collective-permute-done.20.norm_ref.left_1, bf16[1024,2048]{1,0:T(8,128)(2,1)} %collective-permute-done.19.top_ref.refs_1_, bf16[2048,1024]{1,0:T(8,128)(2,1)} %bitcast.225, ...), custom_call_target="tpu_custom_call" | custom-call | flops 12884901888 | bytes 25165824 | tf_op jit(solution)/shard_map/pallas_call | solution.py:356
  392.6 19.1 %shard_map.240 = (bf16[1024,1024]{1,0:T(8,128)(2,1)}, bf16[1024,1024]{1,0:T(8,128)(2,1)}, bf16[1024,2048]{1,0:T(8,128)(2,1)}) custom-call(bf16[1024,2048]{1,0:T(8,128)(2,1)} %constant_dynamic-update-slice_fusion.norm_ref.left_0, bf16[1024,2048]{1,0:T(8,128)(2,1)} %pad_maximum_fusion.1.top_ref.refs_0_, bf16[2048,1024]{1,0:T(8,128)(2,1)} %bitcast.226, ...), custom_call_target="tpu_custom_call" | custom-call | flops 12884901888 | bytes 25165824 | tf_op jit(solution)/shard_map/pallas_call | solution.py:356
  419.7 14.3 %shard_map.241 = bf16[1024,2048]{1,0:T(8,128)(2,1)} custom-call(bf16[1024,1024]{1,0:T(8,128)(2,1)} %get-tuple-element.215.left_0, bf16[1024,1024]{1,0:T(8,128)(2,1)} %get-tuple-element.214.left_1, bf16[1024,2048]{1,0:T(8,128)(2,1)} %pad_maximum_fusion.1.top_ref.refs_0_, bf16[1024,2048]{1,0:T(8,128)(2,1)} %collective-permute-done.19.top_ref.refs_1_), custom_call_target="tpu_custom_call" | custom-call | flops 8589934592 | bytes 16777216 | tf_op jit(solution)/shard_map/pallas_call | solution.py:403
  437.6 14.3 %shard_map.242 = bf16[4,8,64,1024]{3,2,1,0:T(8,128)(2,1)} custom-call(bf16[1024,2048]{1,0:T(8,128)(2,1)} %constant_dynamic-update-slice_fusion.norm_ref.left_0, bf16[1024,2048]{1,0:T(8,128)(2,1)} %collective-permute-done.20.norm_ref.left_1, bf16[1024,1024]{1,0:T(8,128)(2,1)} %get-tuple-element.207.refs_0_, bf16[1024,1024]{1,0:T(8,128)(2,1)} %get-tuple-element.208.refs_1_), custom_call_target="tpu_custom_call" | custom-call | flops 8589934592 | bytes 16777216 | tf_op jit(solution)/shard_map/pallas_call | solution.py:403
  452.0 8.5 %collective-permute-done.22 = bf16[256,2048]{1,0:T(8,128)(2,1)} collective-permute-done((bf16[256,2048]{1,0:T(8,128)(2,1)}, bf16[256,2048]{1,0:T(8,128)(2,1)}, u32[]{:S(2)}, u32[]{:S(2)}) %collective-permute-start.22) | collective-permute-done | bytes 1048608 | tf_op jit(solution)/shard_map/ppermute | solution.py:47
  460.4 23.1 %collective-permute-done.23 = bf16[256,2048]{1,0:T(8,128)(2,1)} collective-permute-done((bf16[256,2048]{1,0:T(8,128)(2,1)}, bf16[256,2048]{1,0:T(8,128)(2,1)}, u32[]{:S(2)}, u32[]{:S(2)}) %collective-permute-start.23) | collective-permute-done | bytes 1048608 | tf_op jit(solution)/shard_map/ppermute | solution.py:47
  491.5 6.0 convolution_convert_fusion.3
  501.1 7.3 convolution_convert_fusion.2
  516.0 7.9 collective-permute-done.25
  524.2 22.1 %collective-permute-done.27 = bf16[256,2048]{1,0:T(8,128)(2,1)} collective-permute-done((bf16[256,2048]{1,0:T(8,128)(2,1)}, bf16[256,2048]{1,0:T(8,128)(2,1)}, u32[]{:S(2)}, u32[]{:S(2)}) %collective-permute-start.27) | collective-permute-done | bytes 1048608 | tf_op jit(solution)/shard_map/ppermute | solution.py:47
  555.4 5.1 all-to-all-start.6
  560.5 4.6 convolution_convert_fusion.5.g_ref
  565.1 9.0 %shard_map.243 = (bf16[1024,256]{1,0:T(8,128)(2,1)}, bf16[1024,256]{1,0:T(8,128)(2,1)}, bf16[1024,256]{1,0:T(8,128)(2,1)}) custom-call(s32[2]{0:T(128)} %pad_add_fusion.pos_ref, f32[2]{0:T(128)} %multiply_exponential_fusion.slope_ref, bf16[1024,768]{1,0:T(8,128)(2,1)} %add_convert_fusion.5.q_ref.k_ref.v_ref, ...), custom_call_target="tpu_custom_call" | custom-call | flops 4294967296 | bytes 7340032 | tf_op jit(solution)/shard_map/pallas_call | solution.py:319
  578.4 8.8 %shard_map.244 = (bf16[1024,256]{1,0:T(8,128)(2,1)}, bf16[1024,256]{1,0:T(8,128)(2,1)}, bf16[1024,256]{1,0:T(8,128)(2,1)}) custom-call(s32[2]{0:T(128)} %pad_add_fusion.pos_ref, f32[2]{0:T(128)} %multiply_exponential_fusion.slope_ref, bf16[1024,768]{1,0:T(8,128)(2,1)} %add_convert_fusion.4.q_ref.k_ref.v_ref, ...), custom_call_target="tpu_custom_call" | custom-call | flops 4294967296 | bytes 7340032 | tf_op jit(solution)/shard_map/pallas_call | solution.py:319
  590.8 12.3 %shard_map.245 = bf16[4,8,64,768]{3,2,1,0:T(8,128)(2,1)} custom-call(bf16[1024,2048]{1,0:T(8,128)(2,1)} %pad_maximum_fusion.left_0, bf16[1024,2048]{1,0:T(8,128)(2,1)} %collective-permute-done.8.left_1, bf16[1024,256]{1,0:T(8,128)(2,1)} %get-tuple-element.257.refs_0_, bf16[1024,256]{1,0:T(8,128)(2,1)} %get-tuple-element.253.refs_1_.refs_0_, ...), custom_call_target="tpu_custom_call" | custom-call | flops 6442450944 | bytes 14680064 | tf_op jit(solution)/shard_map/pallas_call | solution.py:403
  603.1 5.7 all-to-all-done.6
  616.9 4.5 fusion
  621.3 8.1 shard_map.246
  650.7 7.8 shard_map.247
  673.8 16.4 %collective-permute-done.36 = bf16[256,2048]{1,0:T(8,128)(2,1)S(1)} collective-permute-done((bf16[256,2048]{1,0:T(8,128)(2,1)S(1)}, bf16[256,2048]{1,0:T(8,128)(2,1)S(1)}, u32[]{:S(2)}, u32[]{:S(2)}) %collective-permute-start.36) | collective-permute-done | bytes 1048608 | tf_op jit(solution)/shard_map/ppermute | solution.py:47
  690.1 21.8 %collective-permute-done.35 = bf16[256,2048]{1,0:T(8,128)(2,1)S(1)} collective-permute-done((bf16[256,2048]{1,0:T(8,128)(2,1)S(1)}, bf16[256,2048]{1,0:T(8,128)(2,1)S(1)}, u32[]{:S(2)}, u32[]{:S(2)}) %collective-permute-start.35) | collective-permute-done | bytes 1048608 | tf_op jit(solution)/shard_map/ppermute | solution.py:47
  712.2 4.5 fusion.14
  717.9 4.6 all-to-all-start.9
  745.5 4.9 all-to-all-done.8
  754.6 23.6 %all_to_all.99 = f32[32,1,1]{2,1,0:T(1,128)S(1)} all-to-all(f32[32,1,1]{2,1,0:T(1,128)S(1)} %broadcast_in_dim.15), channel_id=1, replica_groups=mesh['o'=1,'chip'=4,'core'=2,'z'=4] {'o','chip','core','z'}, dimensions={0} | all-to-all | bytes 256 | tf_op jit(solution)/shard_map/all_to_all | solution.py:68
  803.3 5.5 shard_map.248
  808.7 7.6 shard_map.250
  816.4 6.4 shard_map.251
  (319 shorter events, 236.0 us)
Async XLA Ops:
  10.6 17.9 %all-to-all-start = ((bf16[8,64,768]{2,1,0:T(8,128)(2,1)}), bf16[8,64,768]{2,1,0:T(8,128)(2,1)S(1)}, u32[]{:S(2)}, u32[]{:S(2)}) async-start(bf16[8,64,768]{2,1,0:T(8,128)(2,1)} %reshape.283), calls=%async_computation | async-start | bytes 1572864 | tf_op jit(solution)/shard_map/all_to_all | solution.py:68
  15.9 160.8 %all-gather.9.cloned.1.call-start = ((), (), s32[]{:S(2)}) async-start(), calls=%async_computation.20 | async-start | bytes 5242880 | tf_op jit(solution)/shard_map/all_gather | solution.py:166
  73.8 34.7 %all-to-all-start.4 = ((bf16[4,64,2048]{2,1,0:T(8,128)(2,1)}), bf16[4,64,2048]{2,1,0:T(8,128)(2,1)S(1)}, u32[]{:S(2)}, u32[]{:S(2)}) async-start(bf16[4,64,2048]{2,1,0:T(8,128)(2,1)} %bitcast.10), calls=%async_computation.4 | async-start | bytes 2097152 | tf_op jit(solution)/shard_map/all_to_all | solution.py:68
  77.7 13.1 %collective-permute-start = (bf16[12,2048]{1,0:T(8,128)(2,1)S(1)}, bf16[12,2048]{1,0:T(8,128)(2,1)S(1)}, u32[]{:S(2)}, u32[]{:S(2)}) collective-permute-start(bf16[12,2048]{1,0:T(8,128)(2,1)S(1)} %dynamic_update_slice.16), channel_id=1, source_target_pairs={{0,8},{8,0},{16,24},{24,16},{1,9},{9,1},{17,25},{25,17},{2,10},{10... | collective-permute-start | bytes 147464 | tf_op jit(solution)/shard_map/ppermute | solution.py:55
  108.5 18.9 %all-to-all-start.3 = ((bf16[8,64,1024]{2,1,0:T(8,128)(2,1)}), bf16[8,64,1024]{2,1,0:T(8,128)(2,1)S(1)}, u32[]{:S(2)}, u32[]{:S(2)}) async-start(bf16[8,64,1024]{2,1,0:T(8,128)(2,1)} %copy.144), calls=%async_computation.3 | async-start | bytes 2097152 | tf_op jit(solution)/shard_map/all_to_all | solution.py:68
  130.6 52.7 %all-to-all-start.5 = ((bf16[4,64,2048]{2,1,0:T(8,128)(2,1)}), bf16[4,64,2048]{2,1,0:T(8,128)(2,1)S(1)}, u32[]{:S(2)}, u32[]{:S(2)}) async-start(bf16[4,64,2048]{2,1,0:T(8,128)(2,1)} %copy-done.9), calls=%async_computation.5 | async-start | bytes 2097152 | tf_op jit(solution)/shard_map/all_to_all | solution.py:68
  135.3 137.6 %all-gather.5.cloned.1.call-start = ((), (), s32[]{:S(2)}) async-start(), calls=%async_computation.15 | async-start | bytes 5242880 | tf_op jit(solution)/shard_map/all_gather | solution.py:569
  135.4 46.9 %collective-permute-start.5 = (bf16[256,2048]{1,0:T(8,128)(2,1)}, bf16[256,2048]{1,0:T(8,128)(2,1)}, u32[]{:S(2)}, u32[]{:S(2)}) collective-permute-start(bf16[256,2048]{1,0:T(8,128)(2,1)} %fusion.8), channel_id=1, source_target_pairs={{0,8},{8,0},{16,24},{24,16},{1,9},{9,1},{17,25},{25,17},{2,10},{10... | collective-permute-start | bytes 3145736 | tf_op jit(solution)/shard_map/ppermute | solution.py:47
  135.9 47.5 %collective-permute-start.6 = (bf16[256,2048]{1,0:T(8,128)(2,1)}, bf16[256,2048]{1,0:T(8,128)(2,1)}, u32[]{:S(2)}, u32[]{:S(2)}) collective-permute-start(bf16[256,2048]{1,0:T(8,128)(2,1)} %fusion.8), channel_id=1, source_target_pairs={{0,16},{8,24},{16,0},{24,8},{1,17},{9,25},{17,1},{25,9},{2,18},{10... | collective-permute-start | bytes 3145736 | tf_op jit(solution)/shard_map/ppermute | solution.py:47
  136.5 46.8 %collective-permute-start.7 = (bf16[256,2048]{1,0:T(8,128)(2,1)}, bf16[256,2048]{1,0:T(8,128)(2,1)}, u32[]{:S(2)}, u32[]{:S(2)}) collective-permute-start(bf16[256,2048]{1,0:T(8,128)(2,1)} %fusion.8), channel_id=1, source_target_pairs={{0,24},{8,16},{16,8},{24,0},{1,25},{9,17},{17,9},{25,1},{2,26},{10... | collective-permute-start | bytes 3145736 | tf_op jit(solution)/shard_map/ppermute | solution.py:47
  187.2 19.6 %collective-permute-start.8 = (bf16[1024,2048]{1,0:T(8,128)(2,1)}, bf16[1024,2048]{1,0:T(8,128)(2,1)}, u32[]{:S(2)}, u32[]{:S(2)}) collective-permute-start(bf16[1024,2048]{1,0:T(8,128)(2,1)} %pad_maximum_fusion.left_0), channel_id=1, source_target_pairs={{0,4},{4,0},{1,5},{5,1},{2,6},{6,2},{3,7},{7,3},{8,12},{12,8},{9,1... | collective-permute-start | bytes 12582920 | tf_op jit(solution)/shard_map/ppermute | solution.py:51
  188.6 31.5 %collective-permute-start.9 = (bf16[256,2048]{1,0:T(8,128)(2,1)S(1)}, bf16[256,2048]{1,0:T(8,128)(2,1)}, u32[]{:S(2)}, u32[]{:S(2)}) collective-permute-start(bf16[256,2048]{1,0:T(8,128)(2,1)S(1)} %pad_maximum_fusion.11), channel_id=1, source_target_pairs={{0,8},{8,0},{16,24},{24,16},{1,9},{9,1},{17,25},{25,17},{2,10},{10... | collective-permute-start | bytes 3145736 | tf_op jit(solution)/shard_map/ppermute | solution.py:47
  189.0 31.1 %collective-permute-start.10 = (bf16[256,2048]{1,0:T(8,128)(2,1)S(1)}, bf16[256,2048]{1,0:T(8,128)(2,1)}, u32[]{:S(2)}, u32[]{:S(2)}) collective-permute-start(bf16[256,2048]{1,0:T(8,128)(2,1)S(1)} %pad_maximum_fusion.11), channel_id=1, source_target_pairs={{0,16},{8,24},{16,0},{24,8},{1,17},{9,25},{17,1},{25,9},{2,18},{10... | collective-permute-start | bytes 3145736 | tf_op jit(solution)/shard_map/ppermute | solution.py:47
  190.4 46.5 %collective-permute-start.11 = (bf16[256,2048]{1,0:T(8,128)(2,1)S(1)}, bf16[256,2048]{1,0:T(8,128)(2,1)}, u32[]{:S(2)}, u32[]{:S(2)}) collective-permute-start(bf16[256,2048]{1,0:T(8,128)(2,1)S(1)} %pad_maximum_fusion.11), channel_id=1, source_target_pairs={{0,24},{8,16},{16,8},{24,0},{1,25},{9,17},{17,9},{25,1},{2,26},{10... | collective-permute-start | bytes 3145736 | tf_op jit(solution)/shard_map/ppermute | solution.py:47
  192.2 161.7 %all-gather.7.cloned.1.call-start = ((), (), s32[]{:S(2)}) async-start(), calls=%async_computation.16 | async-start | bytes 5242880 | tf_op jit(solution)/shard_map/all_gather | solution.py:202
  241.2 305.0 %reduce-scatter.4.cloned.1.call-start = ((), (), s32[]{:S(2)}) async-start(), calls=%async_computation.17 | async-start | bytes 5242880 | tf_op jit(solution)/shard_map/reduce_scatter | solution.py:209
  253.7 26.2 %collective-permute-start.13 = (bf16[256,2048]{1,0:T(8,128)(2,1)}, bf16[256,2048]{1,0:T(8,128)(2,1)S(1)}, u32[]{:S(2)}, u32[]{:S(2)}) collective-permute-start(bf16[256,2048]{1,0:T(8,128)(2,1)} %get-tuple-element.411), channel_id=1, source_target_pairs={{0,8},{8,0},{16,24},{24,16},{1,9},{9,1},{17,25},{25,17},{2,10},{10... | collective-permute-start | bytes 3145736 | tf_op jit(solution)/shard_map/ppermute | solution.py:47
  255.2 47.7 %collective-permute-start.14 = (bf16[256,2048]{1,0:T(8,128)(2,1)}, bf16[256,2048]{1,0:T(8,128)(2,1)}, u32[]{:S(2)}, u32[]{:S(2)}) collective-permute-start(bf16[256,2048]{1,0:T(8,128)(2,1)} %get-tuple-element.410), channel_id=1, source_target_pairs={{0,16},{8,24},{16,0},{24,8},{1,17},{9,25},{17,1},{25,9},{2,18},{10... | collective-permute-start | bytes 3145736 | tf_op jit(solution)/shard_map/ppermute | solution.py:47
  256.0 46.9 %collective-permute-start.15 = (bf16[256,2048]{1,0:T(8,128)(2,1)}, bf16[256,2048]{1,0:T(8,128)(2,1)}, u32[]{:S(2)}, u32[]{:S(2)}) collective-permute-start(bf16[256,2048]{1,0:T(8,128)(2,1)} %get-tuple-element.409), channel_id=1, source_target_pairs={{0,24},{8,16},{16,8},{24,0},{1,25},{9,17},{17,9},{25,1},{2,26},{10... | collective-permute-start | bytes 3145736 | tf_op jit(solution)/shard_map/ppermute | solution.py:47
  302.9 53.7 %collective-permute-start.19 = (bf16[1024,2048]{1,0:T(8,128)(2,1)}, bf16[1024,2048]{1,0:T(8,128)(2,1)}, u32[]{:S(2)}, u32[]{:S(2)}) collective-permute-start(bf16[1024,2048]{1,0:T(8,128)(2,1)} %pad_maximum_fusion.1.top_ref.refs_0_), channel_id=1, source_target_pairs={{0,4},{4,0},{1,5},{5,1},{2,6},{6,2},{3,7},{7,3},{8,12},{12,8},{9,1... | collective-permute-start | bytes 12582920 | tf_op jit(solution)/shard_map/ppermute | solution.py:51
  308.0 45.9 %collective-permute-start.16 = (bf16[256,2048]{1,0:T(8,128)(2,1)}, bf16[256,2048]{1,0:T(8,128)(2,1)}, u32[]{:S(2)}, u32[]{:S(2)}) collective-permute-start(bf16[256,2048]{1,0:T(8,128)(2,1)} %add_convert_fusion.7), channel_id=1, source_target_pairs={{0,8},{8,0},{16,24},{24,16},{1,9},{9,1},{17,25},{25,17},{2,10},{10... | collective-permute-start | bytes 3145736 | tf_op jit(solution)/shard_map/ppermute | solution.py:47
  308.5 45.4 %collective-permute-start.17 = (bf16[256,2048]{1,0:T(8,128)(2,1)}, bf16[256,2048]{1,0:T(8,128)(2,1)}, u32[]{:S(2)}, u32[]{:S(2)}) collective-permute-start(bf16[256,2048]{1,0:T(8,128)(2,1)} %add_convert_fusion.7), channel_id=1, source_target_pairs={{0,16},{8,24},{16,0},{24,8},{1,17},{9,25},{17,1},{25,9},{2,18},{10... | collective-permute-start | bytes 3145736 | tf_op jit(solution)/shard_map/ppermute | solution.py:47
  309.7 46.9 %collective-permute-start.18 = (bf16[256,2048]{1,0:T(8,128)(2,1)}, bf16[256,2048]{1,0:T(8,128)(2,1)}, u32[]{:S(2)}, u32[]{:S(2)}) collective-permute-start(bf16[256,2048]{1,0:T(8,128)(2,1)} %add_convert_fusion.7), channel_id=1, source_target_pairs={{0,24},{8,16},{16,8},{24,0},{1,25},{9,17},{17,9},{25,1},{2,26},{10... | collective-permute-start | bytes 3145736 | tf_op jit(solution)/shard_map/ppermute | solution.py:47
  392.5 19.3 %collective-permute-start.21 = (bf16[1024,2048]{1,0:T(8,128)(2,1)}, bf16[1024,2048]{1,0:T(8,128)(2,1)S(1)}, u32[]{:S(2)}, u32[]{:S(2)}) collective-permute-start(bf16[1024,2048]{1,0:T(8,128)(2,1)} %get-tuple-element.196), channel_id=1, source_target_pairs={{0,4},{4,0},{1,5},{5,1},{2,6},{6,2},{3,7},{7,3},{8,12},{12,8},{9,1... | collective-permute-start | bytes 12582920 | tf_op jit(solution)/shard_map/ppermute | solution.py:51
  434.0 156.7 %reduce-scatter.6.cloned.1.call-start = ((), (), s32[]{:S(2)}) async-start(), calls=%async_computation.18 | async-start | bytes 5242880 | tf_op jit(solution)/shard_map/reduce_scatter | solution.py:192
  434.1 26.4 %collective-permute-start.22 = (bf16[256,2048]{1,0:T(8,128)(2,1)}, bf16[256,2048]{1,0:T(8,128)(2,1)}, u32[]{:S(2)}, u32[]{:S(2)}) collective-permute-start(bf16[256,2048]{1,0:T(8,128)(2,1)} %get-tuple-element.200), channel_id=1, source_target_pairs={{0,8},{8,0},{16,24},{24,16},{1,9},{9,1},{17,25},{25,17},{2,10},{10... | collective-permute-start | bytes 3145736 | tf_op jit(solution)/shard_map/ppermute | solution.py:47
  435.6 47.9 %collective-permute-start.23 = (bf16[256,2048]{1,0:T(8,128)(2,1)}, bf16[256,2048]{1,0:T(8,128)(2,1)}, u32[]{:S(2)}, u32[]{:S(2)}) collective-permute-start(bf16[256,2048]{1,0:T(8,128)(2,1)} %get-tuple-element.201), channel_id=1, source_target_pairs={{0,16},{8,24},{16,0},{24,8},{1,17},{9,25},{17,1},{25,9},{2,18},{10... | collective-permute-start | bytes 3145736 | tf_op jit(solution)/shard_map/ppermute | solution.py:47
  436.5 47.1 %collective-permute-start.24 = (bf16[256,2048]{1,0:T(8,128)(2,1)}, bf16[256,2048]{1,0:T(8,128)(2,1)}, u32[]{:S(2)}, u32[]{:S(2)}) collective-permute-start(bf16[256,2048]{1,0:T(8,128)(2,1)} %get-tuple-element.202), channel_id=1, source_target_pairs={{0,24},{8,16},{16,8},{24,0},{1,25},{9,17},{17,9},{25,1},{2,26},{10... | collective-permute-start | bytes 3145736 | tf_op jit(solution)/shard_map/ppermute | solution.py:47
  497.6 26.3 %collective-permute-start.25 = (bf16[256,2048]{1,0:T(8,128)(2,1)}, bf16[256,2048]{1,0:T(8,128)(2,1)}, u32[]{:S(2)}, u32[]{:S(2)}) collective-permute-start(bf16[256,2048]{1,0:T(8,128)(2,1)} %get-tuple-element.264), channel_id=1, source_target_pairs={{0,8},{8,0},{16,24},{24,16},{1,9},{9,1},{17,25},{25,17},{2,10},{10... | collective-permute-start | bytes 3145736 | tf_op jit(solution)/shard_map/ppermute | solution.py:47
  498.2 26.0 %collective-permute-start.26 = (bf16[256,2048]{1,0:T(8,128)(2,1)}, bf16[256,2048]{1,0:T(8,128)(2,1)}, u32[]{:S(2)}, u32[]{:S(2)}) collective-permute-start(bf16[256,2048]{1,0:T(8,128)(2,1)} %get-tuple-element.264), channel_id=1, source_target_pairs={{0,16},{8,24},{16,0},{24,8},{1,17},{9,25},{17,1},{25,9},{2,18},{10... | collective-permute-start | bytes 3145736 | tf_op jit(solution)/shard_map/ppermute | solution.py:47
  499.4 46.9 %collective-permute-start.27 = (bf16[256,2048]{1,0:T(8,128)(2,1)}, bf16[256,2048]{1,0:T(8,128)(2,1)}, u32[]{:S(2)}, u32[]{:S(2)}) collective-permute-start(bf16[256,2048]{1,0:T(8,128)(2,1)} %get-tuple-element.264), channel_id=1, source_target_pairs={{0,24},{8,16},{16,8},{24,0},{1,25},{9,17},{17,9},{25,1},{2,26},{10... | collective-permute-start | bytes 3145736 | tf_op jit(solution)/shard_map/ppermute | solution.py:47
  550.0 24.1 %collective-permute-start.29 = (bf16[1024,2048]{1,0:T(8,128)(2,1)}, bf16[1024,2048]{1,0:T(8,128)(2,1)}, u32[]{:S(2)}, u32[]{:S(2)}) collective-permute-start(bf16[1024,2048]{1,0:T(8,128)(2,1)} %pad_maximum_fusion.2), channel_id=1, source_target_pairs={{0,4},{4,0},{1,5},{5,1},{2,6},{6,2},{3,7},{7,3},{8,12},{12,8},{9,1... | collective-permute-start | bytes 12582920 | tf_op jit(solution)/shard_map/ppermute | solution.py:51
  555.4 53.5 %all-to-all-start.6 = ((bf16[4,256,2048]{2,1,0:T(8,128)(2,1)}), bf16[4,256,2048]{2,1,0:T(8,128)(2,1)}, u32[]{:S(2)}, u32[]{:S(2)}) async-start(bf16[4,256,2048]{2,1,0:T(8,128)(2,1)} %bitcast.214), calls=%async_computation.8 | async-start | bytes 8388608 | tf_op jit(solution)/shard_map/all_to_all | solution.py:68
  608.9 20.5 %all-to-all-start.7 = ((bf16[8,64,1024]{2,1,0:T(8,128)(2,1)}), bf16[8,64,1024]{2,1,0:T(8,128)(2,1)}, u32[]{:S(2)}, u32[]{:S(2)}) async-start(bf16[8,64,1024]{2,1,0:T(8,128)(2,1)} %bitcast.245), calls=%async_computation.10 | async-start | bytes 2097152 | tf_op jit(solution)/shard_map/all_to_all | solution.py:68
  613.1 118.9 %reduce-scatter.8.cloned.1.call-start = ((), (), s32[]{:S(2)}) async-start(), calls=%async_computation.19 | async-start | bytes 5242880 | tf_op jit(solution)/shard_map/reduce_scatter | solution.py:181
  629.4 29.1 %collective-permute-start.33 = (bf16[1024,2048]{1,0:T(8,128)(2,1)}, bf16[1024,2048]{1,0:T(8,128)(2,1)}, u32[]{:S(2)}, u32[]{:S(2)}) collective-permute-start(bf16[1024,2048]{1,0:T(8,128)(2,1)} %shard_map.246), channel_id=1, source_target_pairs={{0,4},{4,0},{1,5},{5,1},{2,6},{6,2},{3,7},{7,3},{8,12},{12,8},{9,1... | collective-permute-start | bytes 12582920 | tf_op jit(solution)/shard_map/ppermute | solution.py:51
  663.1 27.0 %collective-permute-start.36 = (bf16[256,2048]{1,0:T(8,128)(2,1)S(1)}, bf16[256,2048]{1,0:T(8,128)(2,1)S(1)}, u32[]{:S(2)}, u32[]{:S(2)}) collective-permute-start(bf16[256,2048]{1,0:T(8,128)(2,1)S(1)} %get-tuple-element.401), channel_id=1, source_target_pairs={{0,24},{8,16},{16,8},{24,0},{1,25},{9,17},{17,9},{25,1},{2,26},{10... | collective-permute-start | bytes 3145736 | tf_op jit(solution)/shard_map/ppermute | solution.py:47
  665.8 46.1 %collective-permute-start.35 = (bf16[256,2048]{1,0:T(8,128)(2,1)S(1)}, bf16[256,2048]{1,0:T(8,128)(2,1)S(1)}, u32[]{:S(2)}, u32[]{:S(2)}) collective-permute-start(bf16[256,2048]{1,0:T(8,128)(2,1)S(1)} %get-tuple-element.402), channel_id=1, source_target_pairs={{0,16},{8,24},{16,0},{24,8},{1,17},{9,25},{17,1},{25,9},{2,18},{10... | collective-permute-start | bytes 3145736 | tf_op jit(solution)/shard_map/ppermute | solution.py:47
  666.3 45.9 %collective-permute-start.34 = (bf16[256,2048]{1,0:T(8,128)(2,1)S(1)}, bf16[256,2048]{1,0:T(8,128)(2,1)S(1)}, u32[]{:S(2)}, u32[]{:S(2)}) collective-permute-start(bf16[256,2048]{1,0:T(8,128)(2,1)S(1)} %get-tuple-element.400), channel_id=1, source_target_pairs={{0,8},{8,0},{16,24},{24,16},{1,9},{9,1},{17,25},{25,17},{2,10},{10... | collective-permute-start | bytes 3145736 | tf_op jit(solution)/shard_map/ppermute | solution.py:47
  717.9 12.6 %all-to-all-start.9 = ((f32[32,1,768]{2,1,0:T(1,128)}), f32[32,1,768]{2,1,0:T(1,128)S(1)}, u32[]{:S(2)}, u32[]{:S(2)}) async-start(f32[32,1,768]{2,1,0:T(1,128)} %reshape.331), calls=%async_computation.12 | async-start | bytes 196608 | tf_op jit(solution)/shard_map/all_to_all | solution.py:68
  725.8 18.4 %collective-permute-start.37 = (bf16[64,2048]{1,0:T(8,128)(2,1)}, bf16[64,2048]{1,0:T(8,128)(2,1)S(1)}, u32[]{:S(2)}, u32[]{:S(2)}) collective-permute-start(bf16[64,2048]{1,0:T(8,128)(2,1)} %get-tuple-element.420), channel_id=1, source_target_pairs={{0,1},{1,0},{2,3},{3,2},{4,5},{5,4},{6,7},{7,6},{8,9},{9,8},{10,11... | collective-permute-start | bytes 786440 | tf_op jit(solution)/shard_map/ppermute | solution.py:55
  727.6 52.0 %collective-permute-start.38 = (bf16[64,2048]{1,0:T(8,128)(2,1)}, bf16[64,2048]{1,0:T(8,128)(2,1)S(1)}, u32[]{:S(2)}, u32[]{:S(2)}) collective-permute-start(bf16[64,2048]{1,0:T(8,128)(2,1)} %get-tuple-element.419), channel_id=1, source_target_pairs={{0,2},{1,3},{2,0},{3,1},{4,6},{5,7},{6,4},{7,5},{8,10},{9,11},{10,... | collective-permute-start | bytes 786440 | tf_op jit(solution)/shard_map/ppermute | solution.py:55
  730.0 49.6 %collective-permute-start.39 = (bf16[64,2048]{1,0:T(8,128)(2,1)}, bf16[64,2048]{1,0:T(8,128)(2,1)}, u32[]{:S(2)}, u32[]{:S(2)}) collective-permute-start(bf16[64,2048]{1,0:T(8,128)(2,1)} %get-tuple-element.418), channel_id=1, source_target_pairs={{0,3},{1,2},{2,1},{3,0},{4,7},{5,6},{6,5},{7,4},{8,11},{9,10},{10,... | collective-permute-start | bytes 786440 | tf_op jit(solution)/shard_map/ppermute | solution.py:55
  734.1 16.3 %all-to-all-start.8 = ((bf16[8,64,768]{2,1,0:T(8,128)(2,1)}), bf16[8,64,768]{2,1,0:T(8,128)(2,1)S(1)}, u32[]{:S(2)}, u32[]{:S(2)}) async-start(bf16[8,64,768]{2,1,0:T(8,128)(2,1)} %bitcast.72), calls=%async_computation.11 | async-start | bytes 1572864 | tf_op jit(solution)/shard_map/all_to_all | solution.py:68
  739.3 40.3 %collective-permute-start.30 = (bf16[64,2048]{1,0:T(8,128)(2,1)}, bf16[64,2048]{1,0:T(8,128)(2,1)S(1)}, u32[]{:S(2)}, u32[]{:S(2)}) collective-permute-start(bf16[64,2048]{1,0:T(8,128)(2,1)} %get-tuple-element.424), channel_id=1, source_target_pairs={{0,1},{1,0},{2,3},{3,2},{4,5},{5,4},{6,7},{7,6},{8,9},{9,8},{10,11... | collective-permute-start | bytes 786440 | tf_op jit(solution)/shard_map/ppermute | solution.py:55
  739.9 39.7 %collective-permute-start.31 = (bf16[64,2048]{1,0:T(8,128)(2,1)}, bf16[64,2048]{1,0:T(8,128)(2,1)S(1)}, u32[]{:S(2)}, u32[]{:S(2)}) collective-permute-start(bf16[64,2048]{1,0:T(8,128)(2,1)} %get-tuple-element.423), channel_id=1, source_target_pairs={{0,2},{1,3},{2,0},{3,1},{4,6},{5,7},{6,4},{7,5},{8,10},{9,11},{10,... | collective-permute-start | bytes 786440 | tf_op jit(solution)/shard_map/ppermute | solution.py:55
  744.2 35.4 %collective-permute-start.32 = (bf16[64,2048]{1,0:T(8,128)(2,1)}, bf16[64,2048]{1,0:T(8,128)(2,1)S(1)}, u32[]{:S(2)}, u32[]{:S(2)}) collective-permute-start(bf16[64,2048]{1,0:T(8,128)(2,1)} %get-tuple-element.422), channel_id=1, source_target_pairs={{0,3},{1,2},{2,1},{3,0},{4,7},{5,6},{6,5},{7,4},{8,11},{9,10},{10,... | collective-permute-start | bytes 786440 | tf_op jit(solution)/shard_map/ppermute | solution.py:55
  782.8 42.6 %all-to-all-start.11 = ((bf16[4,64,4096]{2,1,0:T(8,128)(2,1)}), bf16[4,64,4096]{2,1,0:T(8,128)(2,1)S(1)}, u32[]{:S(2)}, u32[]{:S(2)}) async-start(bf16[4,64,4096]{2,1,0:T(8,128)(2,1)} %bitcast.217), calls=%async_computation.14 | async-start | bytes 4194304 | tf_op jit(solution)/shard_map/all_to_all | solution.py:68
  (37 other events, 565.7 us)
Sparse Core Ops, SparseCore 0:
  73.9 102.7 all-gather.8
  192.3 80.6 all-gather.4
  274.6 79.2 all-gather.6
  434.1 77.0 reduce-scatter.3
  513.5 77.2 reduce-scatter.5
  635.8 77.9 reduce-scatter.7

commit v3 on v2

--- a/solution.py
+++ b/solution.py
@@ -92,10 +92,10 @@
     return [parts[0]] + [swap(parts[k], "z", k) for k in range(1, CHIPS)]
 
 
-def to_owners(pieces):
+def by_chip(pieces):
     z = lax.axis_index("z")
     held = jnp.stack(pieces)
-    return trade(jnp.concatenate([pick(held, z ^ q) for q in range(CHIPS)], axis=0), "chip")
+    return jnp.concatenate([pick(held, z ^ q) for q in range(CHIPS)], axis=0)
 
 
 def core_pieces(own_terms, other_terms):
@@ -549,17 +549,18 @@
         jnp.zeros((vectors.shape[0], width), BF16), vectors, (0, flat * vectors.shape[1])
     )
     vecs = sum_all(vecs).astype(F32)
+    held = trade(tokens_given, "chip").reshape(CHIPS, -1, width)
+    held, qkv_weight = together(held, qkv_weight)
+    pieces = to_planes(held)
     qkv_parts = trade_columns(qkv_weight, 3)
     pair_qkv = pair_up(qkv_parts, out_weight, True)
-    tokens_given, pair_qkv = together(tokens_given, pair_qkv)
-    rows_low = trade(trade(tokens_given, "chip"), "z")
-    rows_low, pair_qkv = together(rows_low, pair_qkv)
+    pieces, pair_qkv = together(pieces, pair_qkv)
     full_qkv, full_out = gather_pair(pair_qkv, qkv_parts, out_weight, p, True)
-    top_given, up_weight, rows_low = together(top_given, up_weight, rows_low)
+    top_given, up_weight, pieces = together(top_given, up_weight, pieces)
     held_top = trade(top_given, "chip")
     up_parts = trade_columns(up_weight, 1)
-    rows_low, up_parts, held_top = together(rows_low, up_parts, held_top)
-    rows_in = in_z_order(rows_low).astype(F32)
+    pieces, up_parts, held_top = together(pieces, up_parts, held_top)
+    rows_in = jnp.concatenate(pieces, axis=0).astype(F32)
     normed, hat_one, factor_one = norm_forward(rows_in, vecs[0], vecs[1])
     normed_low, held_top = together(normed.astype(BF16), held_top)
     own = plane_order(normed_low)
@@ -618,7 +619,6 @@
     mlp_own = dot(after(held[0], mlp_other), w_down).astype(BF16)
     reduced_up = scatter_columns(grad_up)
     mlp_sums = core_pieces(mlp_own, mlp_other)
-    own, mlp_sums, owned_down = together(own, mlp_sums, owned_down)
     own = jnp.concatenate(own, axis=0)
     own, mlp_sums = together(own, mlp_sums)
     grad_attn = [own, swap_cores(own)]
@@ -626,27 +626,30 @@
     mlp_parts = chip_trade(mlp_sums, chip)
     grad_context = [dot_nt(v, w_out).astype(BF16) for v in grad_attn]
     grads = [attend_back(v, g, place, slopes) for v, g in zip(qkv, grad_context)]
-    grads, reduced_up = together(grads, reduced_up)
+    grads, owned_down = together(grads, owned_down)
     grad_qkv_weight = weight_grad(normed_a, list(zip(*grads)), qkv_weight.shape[0])
     held, grad_attn, grad_qkv_weight = together(context, grad_attn, grad_qkv_weight)
     grad_out = (dot_tn(held[0], grad_attn[0]) + dot_tn(held[1], grad_attn[1])).astype(BF16)
     grads, grad_out, mlp_parts = together(grads, grad_out, mlp_parts)
     term_other = terms(grads[1], w_qkv)
+    result = (residual + sum_parts(mlp_parts) + vecs[7]).astype(BF16)
+    held, term_other, reduced_up = together(grads[0], term_other, reduced_up)
     owned_up = trade_rows(reduced_up)
-    held, term_other, owned_up = together(grads[0], term_other, owned_up)
+    owned_up, result = together(owned_up, result)
+    result = trade(in_z_order(result), "z")
     term_own = terms(held, w_qkv)
     pieces = core_pieces(term_own, term_other)
     reduced_qkv, owned_out = scatter_pair(
         grad_qkv_weight, grad_out, qkv_weight.shape[0], p
     )
     pieces = chip_exchange(pieces)
+    grads, grad_pre, pieces[1] = together(grads, grad_pre, pieces[1])
+    pieces, owned_up, reduced_qkv, result = together(pieces, owned_up, reduced_qkv, result)
     grad_normed = add_up(pieces)
     through, gain_one_grad, shift_one_grad = norm_backward(grad_normed, hat_one, factor_one, vecs[0])
-    result = (residual + sum_parts(mlp_parts) + vecs[7]).astype(BF16)
-    result, reduced_qkv = together(result, reduced_qkv)
     owned_qkv = trade_rows(reduced_qkv)
     bias_grads = [column_sum(grads[0][i]) + column_sum(grads[1][i]) for i in (0, 2)]
-    up_bias_grad = column_sum(grad_own) + column_sum(grad_other)
+    up_bias_grad = column_sum(grad_pre[0]) + column_sum(grad_pre[1])
     wide = lambda v: lax.dynamic_update_slice(jnp.zeros((width,), F32), v, (p * part,))
     up_wide = lax.dynamic_update_slice(
         jnp.zeros((GROUP * hidden_part,), F32), up_bias_grad, (p * hidden_part,)
@@ -670,16 +673,18 @@
         axis=0,
     )
     vec_parts = vector_grad.reshape(vectors.shape[0], devices, -1).transpose(1, 0, 2)
+    vec_parts, owned_qkv = together(vec_parts, owned_qkv)
     owned_vec = jnp.sum(trade(vec_parts, AXES), axis=0)
 
     grad_qkv_rows = owned_qkv.reshape(GROUP, -1, 3, part).transpose(1, 2, 0, 3).reshape(qkv_weight.shape)
-    squares = [jnp.sum(jnp.square(g.astype(F32))) for g in (owned_qkv, owned_out, owned_up, owned_down, owned_vec)]
+    squares = [jnp.sum(jnp.square(g.astype(F32))) for g in (grad_qkv_rows, owned_out, owned_up, owned_down, owned_vec)]
     squares = jnp.broadcast_to(sum(squares), (devices, 1))
     grad_norm = jnp.sqrt(jnp.sum(trade(squares, AXES)))
     back = (grad_residual + through).astype(BF16)
-    result, back = from_planes(result), from_planes(back)
-    result, back, grad_norm = together(result, back, grad_norm)
-    both = to_owners([jnp.concatenate(v, axis=1) for v in zip(result, back)])
+    back = from_planes(back)
+    back, grad_norm = together(back, grad_norm)
+    result, back = together(result, by_chip(back))
+    both = trade(jnp.concatenate([result, back], axis=1), "chip")
     clip_factor = jnp.minimum(1.0, hyper[4] / (grad_norm + 1e-06))
     step_float = step.astype(F32)
     fix_first = 1.0 / (1.0 - hyper[2] ** step_float)

time: 844 us -> 827 us (0.980)
  blocking collectives: 67.8 us -> 28.6 us
  waiting for transfers between devices: 316 us -> 331 us
    all_to_all x3 -> x2, blocking collectives: 67.8 us -> 28.6 us  [trade(): return lax.all_to_all(value, axes, 0, 0, tiled=True)]
    reduce_scatter x1, waiting for transfers between devices: 0.02 us -> 15.7 us  [scatter_pair(): mine = lax.psum_scatter(both, 'z', scatter_dimension=0, tiled=True)]
    ppermute x21, waiting for transfers between devices: 151 us -> 140 us  [swap_chips(): return lax.ppermute(value, 'chip', [(q, q ^ k) for q in range(CHIPS)])]
    ppermute x11, waiting for transfers between devices: 28.6 us -> 38.5 us  [swap(): lax.ppermute(value, axis, [(i, i ^ k) for i in range(lax.axis_size(axis))])]
    ppermute x11, starting transfers between devices: 12.6 us -> 21.3 us  [swap(): lax.ppermute(value, axis, [(i, i ^ k) for i in range(lax.axis_size(axis))])]
    all_to_all x9 -> x10, waiting for transfers between devices: 34 us -> 38.4 us  [trade(): return lax.all_to_all(value, axes, 0, 0, tiled=True)]
    all_to_all x9 -> x10, starting transfers between devices: 38.7 us -> 38.1 us  [trade(): return lax.all_to_all(value, axes, 0, 0, tiled=True)]
  transfers between devices with their start and end apart: 55 -> 56, of which waited for: 29 -> 32; matrix products, arithmetic and copies ran while one was open for 20% -> 20% of each run, Pallas kernels for 14% -> 14%
where the time goes in v3:
time: 827 us; the launch traced here: 818 us
  waiting for transfers between devices  331 us (40%)
  Pallas kernels  149 us (18%)
  other arithmetic  96.3 us (12%)
  starting transfers between devices  84.8 us (10%)
  local copies, waits for them, and re-layouts  53.3 us (6%)
  matrix products  49.1 us (6%)
  blocking collectives  28.6 us (3%)
  between operations  25.3 us (3%)
    ppermute x21, waiting for transfers between devices, swap_chips(): return lax.ppermute(value, 'chip', [(q, q ^ k) for q in range(CHIPS)])  140 us
    all_gather x1, waiting for transfers between devices, gather_pair(): full = lax.all_gather(pair[0], 'z', axis=0, tiled=False)  41.5 us
    pallas_call x3, Pallas kernels, weight_grad(): pl.pallas_call(partial(weight_kernel, len(rights)), grid=(width // tile,)...  41.2 us
    ppermute x11, waiting for transfers between devices, swap(): lax.ppermute(value, axis, [(i, i ^ k) for i in range(lax.axis_size(axis))])  38.5 us
    all_to_all x10, waiting for transfers between devices, trade(): return lax.all_to_all(value, axes, 0, 0, tiled=True)  38.4 us
    pallas_call x2, Pallas kernels, feed(): pl.pallas_call(feed_kernel, grid=(rows // tile,), in_specs=[wide, wide, w...  38.3 us
    all_to_all x10, starting transfers between devices, trade(): return lax.all_to_all(value, axes, 0, 0, tiled=True)  38.1 us
    all_gather x1, waiting for transfers between devices, gather_rows(): return lax.all_gather(weight, 'z', axis=0, tiled=True)  37.3 us
  transfers between devices with their start and end apart: 56, of which 32 were waited for; matrix products, arithmetic and copies ran while one was open for 20% of the time, Pallas kernels for 14%

profile of v3, /device:TPU:0, one launch (start us, length us, event | category | flops | bytes accessed | tf_op | source)
XLA Modules:
  0.0 817.8 jit_solution(11668460439314099397)
XLA Ops:
  7.2 19.4 %all_to_all.100 = bf16[4,64,2048]{2,1,0:T(8,128)(2,1)S(1)} all-to-all(bf16[4,64,2048]{2,1,0:T(8,128)(2,1)} %bitcast.252), channel_id=1, replica_groups=mesh['o'=1,'chip'=4,'core'=2,'z'=4] {'chip'}, dimensions={0} | all-to-all | bytes 2097152 | tf_op jit(solution)/shard_map/all_to_all | solution.py:68
  38.1 7.1 all-to-all-done.1
  47.4 9.3 %collective-permute-done.1 = bf16[64,2048]{1,0:T(8,128)(2,1)S(1)} collective-permute-done((bf16[64,2048]{1,0:T(8,128)(2,1)}, bf16[64,2048]{1,0:T(8,128)(2,1)S(1)}, u32[]{:S(2)}, u32[]{:S(2)}) %collective-permute-start.1) | collective-permute-done | bytes 262176 | tf_op jit(solution)/shard_map/ppermute | solution.py:55
  56.8 4.3 all-to-all-start.3
  63.3 11.6 %collective-permute-done.3 = bf16[12,2048]{1,0:T(8,128)(2,1)S(1)} collective-permute-done((bf16[12,2048]{1,0:T(8,128)(2,1)S(1)}, bf16[12,2048]{1,0:T(8,128)(2,1)S(1)}, u32[]{:S(2)}, u32[]{:S(2)}) %collective-permute-start.3) | collective-permute-done | bytes 49184 | tf_op jit(solution)/shard_map/ppermute | solution.py:55
  80.8 6.2 collective-permute-start.6
  87.0 8.1 collective-permute-done.6
  105.8 10.5 %all-to-all-done.2 = bf16[8,64,1024]{2,1,0:T(8,128)(2,1)S(1)} async-done(((bf16[8,64,1024]{2,1,0:T(8,128)(2,1)}), bf16[8,64,1024]{2,1,0:T(8,128)(2,1)S(1)}, u32[]{:S(2)}, u32[]{:S(2)}) %all-to-all-start.2) | async-done | bytes 1048608 | tf_op jit(solution)/shard_map/all_to_all | solution.py:68
  125.2 41.5 %all-gather.9.cloned.1.call-done = bf16[2048,1024]{1,0:T(8,128)(2,1)} async-done(((bf16[512,1024]{1,0:T(8,128)(2,1)}), bf16[2048,1024]{1,0:T(8,128)(2,1)}) %all-gather.9.cloned.1.call-update) | async-done | bytes 4194320 | tf_op jit(solution)/shard_map/all_gather | solution.py:166
  182.1 7.7 add_convert_fusion.5.q_ref.k_ref.v_ref
  189.8 6.7 shard_map.237
  196.5 6.8 add_convert_fusion.4.q_ref.k_ref.v_ref
  203.3 6.5 shard_map.238
  209.8 16.9 %collective-permute-done.13 = bf16[256,2048]{1,0:T(8,128)(2,1)} collective-permute-done((bf16[256,2048]{1,0:T(8,128)(2,1)S(1)}, bf16[256,2048]{1,0:T(8,128)(2,1)}, u32[]{:S(2)}, u32[]{:S(2)}) %collective-permute-start.13) | collective-permute-done | bytes 1048608 | tf_op jit(solution)/shard_map/ppermute | solution.py:47
  227.6 4.3 convolution_convert_fusion.1
  233.3 6.1 collective-permute-done.15
  254.8 6.3 all-gather.5.cloned.1.call-done
  261.1 9.5 %collective-permute-done.16 = bf16[256,2048]{1,0:T(8,128)(2,1)S(1)} collective-permute-done((bf16[256,2048]{1,0:T(8,128)(2,1)}, bf16[256,2048]{1,0:T(8,128)(2,1)S(1)}, u32[]{:S(2)}, u32[]{:S(2)}) %collective-permute-start.16) | collective-permute-done | bytes 1048608 | tf_op jit(solution)/shard_map/ppermute | solution.py:47
  270.6 21.3 %collective-permute-done.17 = bf16[256,2048]{1,0:T(8,128)(2,1)S(1)} collective-permute-done((bf16[256,2048]{1,0:T(8,128)(2,1)}, bf16[256,2048]{1,0:T(8,128)(2,1)S(1)}, u32[]{:S(2)}, u32[]{:S(2)}) %collective-permute-start.17) | collective-permute-done | bytes 1048608 | tf_op jit(solution)/shard_map/ppermute | solution.py:47
  304.7 37.3 %all-gather.7.cloned.1.call-done.down_ref = bf16[1024,2048]{1,0:T(8,128)(2,1)} async-done(((bf16[256,2048]{1,0:T(8,128)(2,1)}), bf16[1024,2048]{1,0:T(8,128)(2,1)}) %all-gather.7.cloned.1.call-update) | async-done | bytes 4194320 | tf_op jit(solution)/shard_map/all_gather | solution.py:202
  342.0 5.5 collective-permute-done.20
  357.4 6.9 collective-permute-done.23.norm_ref.left_1
  364.2 19.2 %shard_map.239 = (bf16[1024,1024]{1,0:T(8,128)(2,1)}, bf16[1024,1024]{1,0:T(8,128)(2,1)}, bf16[1024,2048]{1,0:T(8,128)(2,1)}) custom-call(bf16[1024,2048]{1,0:T(8,128)(2,1)} %collective-permute-done.23.norm_ref.left_1, bf16[1024,2048]{1,0:T(8,128)(2,1)} %collective-permute-done.22.top_ref.refs_1_, bf16[2048,1024]{1,0:T(8,128)(2,1)} %bitcast.231, ...), custom_call_target="tpu_custom_call" | custom-call | flops 12884901888 | bytes 25165824 | tf_op jit(solution)/shard_map/pallas_call | solution.py:356
  383.6 19.1 %shard_map.240 = (bf16[1024,1024]{1,0:T(8,128)(2,1)}, bf16[1024,1024]{1,0:T(8,128)(2,1)}, bf16[1024,2048]{1,0:T(8,128)(2,1)}) custom-call(bf16[1024,2048]{1,0:T(8,128)(2,1)} %constant_dynamic-update-slice_fusion.norm_ref.left_0, bf16[1024,2048]{1,0:T(8,128)(2,1)} %pad_maximum_fusion.1.top_ref.refs_0_, bf16[2048,1024]{1,0:T(8,128)(2,1)} %bitcast.232, ...), custom_call_target="tpu_custom_call" | custom-call | flops 12884901888 | bytes 25165824 | tf_op jit(solution)/shard_map/pallas_call | solution.py:356
  410.6 14.3 %shard_map.241 = bf16[1024,2048]{1,0:T(8,128)(2,1)} custom-call(bf16[1024,1024]{1,0:T(8,128)(2,1)} %get-tuple-element.238.left_0, bf16[1024,1024]{1,0:T(8,128)(2,1)} %get-tuple-element.237.left_1, bf16[1024,2048]{1,0:T(8,128)(2,1)} %pad_maximum_fusion.1.top_ref.refs_0_, bf16[1024,2048]{1,0:T(8,128)(2,1)} %collective-permute-done.22.top_ref.refs_1_), custom_call_target="tpu_custom_call" | custom-call | flops 8589934592 | bytes 16777216 | tf_op jit(solution)/shard_map/pallas_call | solution.py:403
  428.5 14.5 %shard_map.242 = bf16[4,8,64,1024]{3,2,1,0:T(8,128)(2,1)} custom-call(bf16[1024,2048]{1,0:T(8,128)(2,1)} %constant_dynamic-update-slice_fusion.norm_ref.left_0, bf16[1024,2048]{1,0:T(8,128)(2,1)} %collective-permute-done.23.norm_ref.left_1, bf16[1024,1024]{1,0:T(8,128)(2,1)} %get-tuple-element.288.refs_0_, bf16[1024,1024]{1,0:T(8,128)(2,1)} %get-tuple-element.289.refs_1_), custom_call_target="tpu_custom_call" | custom-call | flops 8589934592 | bytes 16777216 | tf_op jit(solution)/shard_map/pallas_call | solution.py:403
  443.0 8.3 %collective-permute-done.25 = bf16[256,2048]{1,0:T(8,128)(2,1)} collective-permute-done((bf16[256,2048]{1,0:T(8,128)(2,1)}, bf16[256,2048]{1,0:T(8,128)(2,1)}, u32[]{:S(2)}, u32[]{:S(2)}) %collective-permute-start.25) | collective-permute-done | bytes 1048608 | tf_op jit(solution)/shard_map/ppermute | solution.py:47
  451.3 21.4 %collective-permute-done.26 = bf16[256,2048]{1,0:T(8,128)(2,1)} collective-permute-done((bf16[256,2048]{1,0:T(8,128)(2,1)}, bf16[256,2048]{1,0:T(8,128)(2,1)}, u32[]{:S(2)}, u32[]{:S(2)}) %collective-permute-start.26) | collective-permute-done | bytes 1048608 | tf_op jit(solution)/shard_map/ppermute | solution.py:47
  482.2 6.1 convolution_convert_fusion.3
  491.8 7.4 convolution_convert_fusion.2
  499.2 16.2 %collective-permute-done.30 = bf16[256,2048]{1,0:T(8,128)(2,1)S(1)} collective-permute-done((bf16[256,2048]{1,0:T(8,128)(2,1)}, bf16[256,2048]{1,0:T(8,128)(2,1)S(1)}, u32[]{:S(2)}, u32[]{:S(2)}) %collective-permute-start.30) | collective-permute-done | bytes 1048608 | tf_op jit(solution)/shard_map/ppermute | solution.py:47
  515.4 22.1 %collective-permute-done.29 = bf16[256,2048]{1,0:T(8,128)(2,1)} collective-permute-done((bf16[256,2048]{1,0:T(8,128)(2,1)}, bf16[256,2048]{1,0:T(8,128)(2,1)}, u32[]{:S(2)}, u32[]{:S(2)}) %collective-permute-start.29) | collective-permute-done | bytes 1048608 | tf_op jit(solution)/shard_map/ppermute | solution.py:47
  552.9 5.0 all-to-all-start.5
  562.4 8.8 %shard_map.243 = (bf16[1024,256]{1,0:T(8,128)(2,1)}, bf16[1024,256]{1,0:T(8,128)(2,1)}, bf16[1024,256]{1,0:T(8,128)(2,1)}) custom-call(s32[2]{0:T(128)} %pad_add_fusion.pos_ref, f32[2]{0:T(128)} %multiply_exponential_fusion.slope_ref, bf16[1024,768]{1,0:T(8,128)(2,1)} %add_convert_fusion.5.q_ref.k_ref.v_ref, ...), custom_call_target="tpu_custom_call" | custom-call | flops 4294967296 | bytes 7340032 | tf_op jit(solution)/shard_map/pallas_call | solution.py:319
  575.5 8.8 %shard_map.244 = (bf16[1024,256]{1,0:T(8,128)(2,1)}, bf16[1024,256]{1,0:T(8,128)(2,1)}, bf16[1024,256]{1,0:T(8,128)(2,1)}) custom-call(s32[2]{0:T(128)} %pad_add_fusion.pos_ref, f32[2]{0:T(128)} %multiply_exponential_fusion.slope_ref, bf16[1024,768]{1,0:T(8,128)(2,1)} %add_convert_fusion.4.q_ref.k_ref.v_ref, ...), custom_call_target="tpu_custom_call" | custom-call | flops 4294967296 | bytes 7340032 | tf_op jit(solution)/shard_map/pallas_call | solution.py:319
  584.3 12.5 %shard_map.245 = bf16[4,8,64,768]{3,2,1,0:T(8,128)(2,1)} custom-call(bf16[1024,2048]{1,0:T(8,128)(2,1)} %pad_maximum_fusion.left_0, bf16[1024,2048]{1,0:T(8,128)(2,1)} %collective-permute-done.11.left_1, bf16[1024,256]{1,0:T(8,128)(2,1)} %get-tuple-element.283.refs_0_, bf16[1024,256]{1,0:T(8,128)(2,1)} %get-tuple-element.284.refs_1_.refs_0_, ...), custom_call_target="tpu_custom_call" | custom-call | flops 6442450944 | bytes 14680064 | tf_op jit(solution)/shard_map/pallas_call | solution.py:403
  611.0 8.1 shard_map.246
  622.2 4.6 convert_reduce_fusion
  635.8 7.7 shard_map.247
  645.8 4.6 add_convert_fusion
  663.6 14.9 %collective-permute-done.34 = bf16[256,2048]{1,0:T(8,128)(2,1)S(1)} collective-permute-done((bf16[256,2048]{1,0:T(8,128)(2,1)}, bf16[256,2048]{1,0:T(8,128)(2,1)S(1)}, u32[]{:S(2)}, u32[]{:S(2)}) %collective-permute-start.34) | collective-permute-done | bytes 1048608 | tf_op jit(solution)/shard_map/ppermute | solution.py:47
  686.0 15.7 %reduce-scatter.8.cloned.1.call-done = bf16[512,1024]{1,0:T(8,128)(2,1)} async-done(((bf16[2048,1024]{1,0:T(8,128)(2,1)}), bf16[512,1024]{1,0:T(8,128)(2,1)}) %reduce-scatter.8.cloned.1.call-update) | async-done | bytes 1048592 | tf_op jit(solution)/shard_map/reduce_scatter | solution.py:181
  712.4 4.6 collective-permute-start.37
  726.4 9.6 %all-to-all-done.8 = bf16[8,64,768]{2,1,0:T(8,128)(2,1)S(1)} async-done(((bf16[8,64,768]{2,1,0:T(8,128)(2,1)}), bf16[8,64,768]{2,1,0:T(8,128)(2,1)S(1)}, u32[]{:S(2)}, u32[]{:S(2)}) %all-to-all-start.8) | async-done | bytes 786464 | tf_op jit(solution)/shard_map/all_to_all | solution.py:68
  754.6 9.2 %all_to_all.101 = f32[32,1,1]{2,1,0:T(1,128)S(1)} all-to-all(f32[32,1,1]{2,1,0:T(1,128)S(1)} %broadcast_in_dim.15), channel_id=1, replica_groups=mesh['o'=1,'chip'=4,'core'=2,'z'=4] {'o','chip','core','z'}, dimensions={0} | all-to-all | bytes 256 | tf_op jit(solution)/shard_map/all_to_all | solution.py:68
  786.2 5.5 shard_map.248
  791.7 7.6 shard_map.250
  799.3 6.4 shard_map.251
  (353 shorter events, 250.5 us)
Async XLA Ops:
  28.9 16.2 %all-to-all-start.1 = ((bf16[8,64,768]{2,1,0:T(8,128)(2,1)}), bf16[8,64,768]{2,1,0:T(8,128)(2,1)S(1)}, u32[]{:S(2)}, u32[]{:S(2)}) async-start(bf16[8,64,768]{2,1,0:T(8,128)(2,1)} %reshape.276), calls=%async_computation.1 | async-start | bytes 1572864 | tf_op jit(solution)/shard_map/all_to_all | solution.py:68
  32.6 134.1 %all-gather.9.cloned.1.call-start = ((), (), s32[]{:S(2)}) async-start(), calls=%async_computation.20 | async-start | bytes 5242880 | tf_op jit(solution)/shard_map/all_gather | solution.py:166
  35.2 21.6 %collective-permute-start.1 = (bf16[64,2048]{1,0:T(8,128)(2,1)}, bf16[64,2048]{1,0:T(8,128)(2,1)S(1)}, u32[]{:S(2)}, u32[]{:S(2)}) collective-permute-start(bf16[64,2048]{1,0:T(8,128)(2,1)} %get-tuple-element.463), channel_id=1, source_target_pairs={{0,2},{1,3},{2,0},{3,1},{4,6},{5,7},{6,4},{7,5},{8,10},{9,11},{10,... | collective-permute-start | bytes 786440 | tf_op jit(solution)/shard_map/ppermute | solution.py:55
  37.8 19.0 %collective-permute-start.2 = (bf16[64,2048]{1,0:T(8,128)(2,1)}, bf16[64,2048]{1,0:T(8,128)(2,1)S(1)}, u32[]{:S(2)}, u32[]{:S(2)}) collective-permute-start(bf16[64,2048]{1,0:T(8,128)(2,1)} %get-tuple-element.462), channel_id=1, source_target_pairs={{0,3},{1,2},{2,1},{3,0},{4,7},{5,6},{6,5},{7,4},{8,11},{9,10},{10,... | collective-permute-start | bytes 786440 | tf_op jit(solution)/shard_map/ppermute | solution.py:55
  56.8 40.6 %all-to-all-start.3 = ((bf16[4,64,2048]{2,1,0:T(8,128)(2,1)}), bf16[4,64,2048]{2,1,0:T(8,128)(2,1)}, u32[]{:S(2)}, u32[]{:S(2)}) async-start(bf16[4,64,2048]{2,1,0:T(8,128)(2,1)} %bitcast.14), calls=%async_computation.3 | async-start | bytes 2097152 | tf_op jit(solution)/shard_map/all_to_all | solution.py:68
  80.8 14.3 %collective-permute-start.6 = (bf16[12,2048]{1,0:T(8,128)(2,1)S(1)}, bf16[12,2048]{1,0:T(8,128)(2,1)S(1)}, u32[]{:S(2)}, u32[]{:S(2)}) collective-permute-start(bf16[12,2048]{1,0:T(8,128)(2,1)S(1)} %add.307), channel_id=1, source_target_pairs={{0,1},{1,0},{2,3},{3,2},{4,5},{5,4},{6,7},{7,6},{8,9},{9,8},{10,11... | collective-permute-start | bytes 147464 | tf_op jit(solution)/shard_map/ppermute | solution.py:55
  97.4 18.9 %all-to-all-start.2 = ((bf16[8,64,1024]{2,1,0:T(8,128)(2,1)}), bf16[8,64,1024]{2,1,0:T(8,128)(2,1)S(1)}, u32[]{:S(2)}, u32[]{:S(2)}) async-start(bf16[8,64,1024]{2,1,0:T(8,128)(2,1)} %copy.144), calls=%async_computation.2 | async-start | bytes 2097152 | tf_op jit(solution)/shard_map/all_to_all | solution.py:68
  117.5 54.8 %all-to-all-start.4 = ((bf16[4,64,2048]{2,1,0:T(8,128)(2,1)}), bf16[4,64,2048]{2,1,0:T(8,128)(2,1)S(1)}, u32[]{:S(2)}, u32[]{:S(2)}) async-start(bf16[4,64,2048]{2,1,0:T(8,128)(2,1)} %bitcast.18), calls=%async_computation.4 | async-start | bytes 2097152 | tf_op jit(solution)/shard_map/all_to_all | solution.py:68
  121.7 139.4 %all-gather.5.cloned.1.call-start = ((), (), s32[]{:S(2)}) async-start(), calls=%async_computation.15 | async-start | bytes 5242880 | tf_op jit(solution)/shard_map/all_gather | solution.py:570
  121.7 50.6 %collective-permute-start.8 = (bf16[256,2048]{1,0:T(8,128)(2,1)S(1)}, bf16[256,2048]{1,0:T(8,128)(2,1)}, u32[]{:S(2)}, u32[]{:S(2)}) collective-permute-start(bf16[256,2048]{1,0:T(8,128)(2,1)S(1)} %fusion.8), channel_id=1, source_target_pairs={{0,8},{8,0},{16,24},{24,16},{1,9},{9,1},{17,25},{25,17},{2,10},{10... | collective-permute-start | bytes 3145736 | tf_op jit(solution)/shard_map/ppermute | solution.py:47
  122.2 50.1 %collective-permute-start.9 = (bf16[256,2048]{1,0:T(8,128)(2,1)S(1)}, bf16[256,2048]{1,0:T(8,128)(2,1)}, u32[]{:S(2)}, u32[]{:S(2)}) collective-permute-start(bf16[256,2048]{1,0:T(8,128)(2,1)S(1)} %fusion.8), channel_id=1, source_target_pairs={{0,16},{8,24},{16,0},{24,8},{1,17},{9,25},{17,1},{25,9},{2,18},{10... | collective-permute-start | bytes 3145736 | tf_op jit(solution)/shard_map/ppermute | solution.py:47
  122.9 49.4 %collective-permute-start.10 = (bf16[256,2048]{1,0:T(8,128)(2,1)S(1)}, bf16[256,2048]{1,0:T(8,128)(2,1)}, u32[]{:S(2)}, u32[]{:S(2)}) collective-permute-start(bf16[256,2048]{1,0:T(8,128)(2,1)S(1)} %fusion.8), channel_id=1, source_target_pairs={{0,24},{8,16},{16,8},{24,0},{1,25},{9,17},{17,9},{25,1},{2,26},{10... | collective-permute-start | bytes 3145736 | tf_op jit(solution)/shard_map/ppermute | solution.py:47
  176.3 20.2 %collective-permute-start.11 = (bf16[1024,2048]{1,0:T(8,128)(2,1)}, bf16[1024,2048]{1,0:T(8,128)(2,1)}, u32[]{:S(2)}, u32[]{:S(2)}) collective-permute-start(bf16[1024,2048]{1,0:T(8,128)(2,1)} %pad_maximum_fusion.left_0), channel_id=1, source_target_pairs={{0,4},{4,0},{1,5},{5,1},{2,6},{6,2},{3,7},{7,3},{8,12},{12,8},{9,1... | collective-permute-start | bytes 12582920 | tf_op jit(solution)/shard_map/ppermute | solution.py:51
  178.3 31.5 %collective-permute-start.12 = (bf16[256,2048]{1,0:T(8,128)(2,1)S(1)}, bf16[256,2048]{1,0:T(8,128)(2,1)}, u32[]{:S(2)}, u32[]{:S(2)}) collective-permute-start(bf16[256,2048]{1,0:T(8,128)(2,1)S(1)} %pad_maximum_fusion.10), channel_id=1, source_target_pairs={{0,8},{8,0},{16,24},{24,16},{1,9},{9,1},{17,25},{25,17},{2,10},{10... | collective-permute-start | bytes 3145736 | tf_op jit(solution)/shard_map/ppermute | solution.py:47
  179.7 46.9 %collective-permute-start.13 = (bf16[256,2048]{1,0:T(8,128)(2,1)S(1)}, bf16[256,2048]{1,0:T(8,128)(2,1)}, u32[]{:S(2)}, u32[]{:S(2)}) collective-permute-start(bf16[256,2048]{1,0:T(8,128)(2,1)S(1)} %pad_maximum_fusion.10), channel_id=1, source_target_pairs={{0,16},{8,24},{16,0},{24,8},{1,17},{9,25},{17,1},{25,9},{2,18},{10... | collective-permute-start | bytes 3145736 | tf_op jit(solution)/shard_map/ppermute | solution.py:47
  181.4 46.2 %collective-permute-start.14 = (bf16[256,2048]{1,0:T(8,128)(2,1)S(1)}, bf16[256,2048]{1,0:T(8,128)(2,1)}, u32[]{:S(2)}, u32[]{:S(2)}) collective-permute-start(bf16[256,2048]{1,0:T(8,128)(2,1)S(1)} %pad_maximum_fusion.10), channel_id=1, source_target_pairs={{0,24},{8,16},{16,8},{24,0},{1,25},{9,17},{17,9},{25,1},{2,26},{10... | collective-permute-start | bytes 3145736 | tf_op jit(solution)/shard_map/ppermute | solution.py:47
  181.8 160.2 %all-gather.7.cloned.1.call-start = ((), (), s32[]{:S(2)}) async-start(), calls=%async_computation.16 | async-start | bytes 5242880 | tf_op jit(solution)/shard_map/all_gather | solution.py:202
  231.9 352.4 %reduce-scatter.4.cloned.1.call-start = ((), (), s32[]{:S(2)}) async-start(), calls=%async_computation.17 | async-start | bytes 5242880 | tf_op jit(solution)/shard_map/reduce_scatter | solution.py:209
  244.4 26.2 %collective-permute-start.16 = (bf16[256,2048]{1,0:T(8,128)(2,1)}, bf16[256,2048]{1,0:T(8,128)(2,1)S(1)}, u32[]{:S(2)}, u32[]{:S(2)}) collective-permute-start(bf16[256,2048]{1,0:T(8,128)(2,1)} %get-tuple-element.439), channel_id=1, source_target_pairs={{0,8},{8,0},{16,24},{24,16},{1,9},{9,1},{17,25},{25,17},{2,10},{10... | collective-permute-start | bytes 3145736 | tf_op jit(solution)/shard_map/ppermute | solution.py:47
  245.8 46.2 %collective-permute-start.17 = (bf16[256,2048]{1,0:T(8,128)(2,1)}, bf16[256,2048]{1,0:T(8,128)(2,1)S(1)}, u32[]{:S(2)}, u32[]{:S(2)}) collective-permute-start(bf16[256,2048]{1,0:T(8,128)(2,1)} %get-tuple-element.438), channel_id=1, source_target_pairs={{0,16},{8,24},{16,0},{24,8},{1,17},{9,25},{17,1},{25,9},{2,18},{10... | collective-permute-start | bytes 3145736 | tf_op jit(solution)/shard_map/ppermute | solution.py:47
  246.7 46.8 %collective-permute-start.18 = (bf16[256,2048]{1,0:T(8,128)(2,1)}, bf16[256,2048]{1,0:T(8,128)(2,1)}, u32[]{:S(2)}, u32[]{:S(2)}) collective-permute-start(bf16[256,2048]{1,0:T(8,128)(2,1)} %get-tuple-element.437), channel_id=1, source_target_pairs={{0,24},{8,16},{16,8},{24,0},{1,25},{9,17},{17,9},{25,1},{2,26},{10... | collective-permute-start | bytes 3145736 | tf_op jit(solution)/shard_map/ppermute | solution.py:47
  293.5 54.0 %collective-permute-start.22 = (bf16[1024,2048]{1,0:T(8,128)(2,1)}, bf16[1024,2048]{1,0:T(8,128)(2,1)}, u32[]{:S(2)}, u32[]{:S(2)}) collective-permute-start(bf16[1024,2048]{1,0:T(8,128)(2,1)} %pad_maximum_fusion.1.top_ref.refs_0_), channel_id=1, source_target_pairs={{0,4},{4,0},{1,5},{5,1},{2,6},{6,2},{3,7},{7,3},{8,12},{12,8},{9,1... | collective-permute-start | bytes 12582920 | tf_op jit(solution)/shard_map/ppermute | solution.py:51
  298.8 43.2 %collective-permute-start.19 = (bf16[256,2048]{1,0:T(8,128)(2,1)}, bf16[256,2048]{1,0:T(8,128)(2,1)}, u32[]{:S(2)}, u32[]{:S(2)}) collective-permute-start(bf16[256,2048]{1,0:T(8,128)(2,1)} %add_convert_fusion.7), channel_id=1, source_target_pairs={{0,8},{8,0},{16,24},{24,16},{1,9},{9,1},{17,25},{25,17},{2,10},{10... | collective-permute-start | bytes 3145736 | tf_op jit(solution)/shard_map/ppermute | solution.py:47
  299.6 47.9 %collective-permute-start.20 = (bf16[256,2048]{1,0:T(8,128)(2,1)}, bf16[256,2048]{1,0:T(8,128)(2,1)}, u32[]{:S(2)}, u32[]{:S(2)}) collective-permute-start(bf16[256,2048]{1,0:T(8,128)(2,1)} %add_convert_fusion.7), channel_id=1, source_target_pairs={{0,16},{8,24},{16,0},{24,8},{1,17},{9,25},{17,1},{25,9},{2,18},{10... | collective-permute-start | bytes 3145736 | tf_op jit(solution)/shard_map/ppermute | solution.py:47
  301.9 45.6 %collective-permute-start.21 = (bf16[256,2048]{1,0:T(8,128)(2,1)}, bf16[256,2048]{1,0:T(8,128)(2,1)}, u32[]{:S(2)}, u32[]{:S(2)}) collective-permute-start(bf16[256,2048]{1,0:T(8,128)(2,1)} %add_convert_fusion.7), channel_id=1, source_target_pairs={{0,24},{8,16},{16,8},{24,0},{1,25},{9,17},{17,9},{25,1},{2,26},{10... | collective-permute-start | bytes 3145736 | tf_op jit(solution)/shard_map/ppermute | solution.py:47
  383.4 19.2 %collective-permute-start.24 = (bf16[1024,2048]{1,0:T(8,128)(2,1)}, bf16[1024,2048]{1,0:T(8,128)(2,1)S(1)}, u32[]{:S(2)}, u32[]{:S(2)}) collective-permute-start(bf16[1024,2048]{1,0:T(8,128)(2,1)} %get-tuple-element.219), channel_id=1, source_target_pairs={{0,4},{4,0},{1,5},{5,1},{2,6},{6,2},{3,7},{7,3},{8,12},{12,8},{9,1... | collective-permute-start | bytes 12582920 | tf_op jit(solution)/shard_map/ppermute | solution.py:51
  424.9 194.2 %reduce-scatter.6.cloned.1.call-start = ((), (), s32[]{:S(2)}) async-start(), calls=%async_computation.18 | async-start | bytes 5242880 | tf_op jit(solution)/shard_map/reduce_scatter | solution.py:192
  424.9 26.4 %collective-permute-start.25 = (bf16[256,2048]{1,0:T(8,128)(2,1)}, bf16[256,2048]{1,0:T(8,128)(2,1)}, u32[]{:S(2)}, u32[]{:S(2)}) collective-permute-start(bf16[256,2048]{1,0:T(8,128)(2,1)} %get-tuple-element.223), channel_id=1, source_target_pairs={{0,8},{8,0},{16,24},{24,16},{1,9},{9,1},{17,25},{25,17},{2,10},{10... | collective-permute-start | bytes 3145736 | tf_op jit(solution)/shard_map/ppermute | solution.py:47
  426.4 46.3 %collective-permute-start.26 = (bf16[256,2048]{1,0:T(8,128)(2,1)}, bf16[256,2048]{1,0:T(8,128)(2,1)}, u32[]{:S(2)}, u32[]{:S(2)}) collective-permute-start(bf16[256,2048]{1,0:T(8,128)(2,1)} %get-tuple-element.224), channel_id=1, source_target_pairs={{0,16},{8,24},{16,0},{24,8},{1,17},{9,25},{17,1},{25,9},{2,18},{10... | collective-permute-start | bytes 3145736 | tf_op jit(solution)/shard_map/ppermute | solution.py:47
  427.2 47.1 %collective-permute-start.27 = (bf16[256,2048]{1,0:T(8,128)(2,1)}, bf16[256,2048]{1,0:T(8,128)(2,1)}, u32[]{:S(2)}, u32[]{:S(2)}) collective-permute-start(bf16[256,2048]{1,0:T(8,128)(2,1)} %get-tuple-element.225), channel_id=1, source_target_pairs={{0,24},{8,16},{16,8},{24,0},{1,25},{9,17},{17,9},{25,1},{2,26},{10... | collective-permute-start | bytes 3145736 | tf_op jit(solution)/shard_map/ppermute | solution.py:47
  488.3 52.8 %collective-permute-start.31 = (bf16[1024,2048]{1,0:T(8,128)(2,1)}, bf16[1024,2048]{1,0:T(8,128)(2,1)}, u32[]{:S(2)}, u32[]{:S(2)}) collective-permute-start(bf16[1024,2048]{1,0:T(8,128)(2,1)} %convolution_convert_fusion.3), channel_id=1, source_target_pairs={{0,4},{4,0},{1,5},{5,1},{2,6},{6,2},{3,7},{7,3},{8,12},{12,8},{9,1... | collective-permute-start | bytes 12582920 | tf_op jit(solution)/shard_map/ppermute | solution.py:51
  488.3 27.1 %collective-permute-start.30 = (bf16[256,2048]{1,0:T(8,128)(2,1)}, bf16[256,2048]{1,0:T(8,128)(2,1)S(1)}, u32[]{:S(2)}, u32[]{:S(2)}) collective-permute-start(bf16[256,2048]{1,0:T(8,128)(2,1)} %get-tuple-element.287), channel_id=1, source_target_pairs={{0,24},{8,16},{16,8},{24,0},{1,25},{9,17},{17,9},{25,1},{2,26},{10... | collective-permute-start | bytes 3145736 | tf_op jit(solution)/shard_map/ppermute | solution.py:47
  490.0 47.5 %collective-permute-start.29 = (bf16[256,2048]{1,0:T(8,128)(2,1)}, bf16[256,2048]{1,0:T(8,128)(2,1)}, u32[]{:S(2)}, u32[]{:S(2)}) collective-permute-start(bf16[256,2048]{1,0:T(8,128)(2,1)} %get-tuple-element.287), channel_id=1, source_target_pairs={{0,16},{8,24},{16,0},{24,8},{1,17},{9,25},{17,1},{25,9},{2,18},{10... | collective-permute-start | bytes 3145736 | tf_op jit(solution)/shard_map/ppermute | solution.py:47
  490.5 47.0 %collective-permute-start.28 = (bf16[256,2048]{1,0:T(8,128)(2,1)}, bf16[256,2048]{1,0:T(8,128)(2,1)}, u32[]{:S(2)}, u32[]{:S(2)}) collective-permute-start(bf16[256,2048]{1,0:T(8,128)(2,1)} %get-tuple-element.287), channel_id=1, source_target_pairs={{0,8},{8,0},{16,24},{24,16},{1,9},{9,1},{17,25},{25,17},{2,10},{10... | collective-permute-start | bytes 3145736 | tf_op jit(solution)/shard_map/ppermute | solution.py:47
  547.7 23.5 %collective-permute-start.32 = (bf16[1024,2048]{1,0:T(8,128)(2,1)}, bf16[1024,2048]{1,0:T(8,128)(2,1)}, u32[]{:S(2)}, u32[]{:S(2)}) collective-permute-start(bf16[1024,2048]{1,0:T(8,128)(2,1)} %pad_maximum_fusion.2), channel_id=1, source_target_pairs={{0,4},{4,0},{1,5},{5,1},{2,6},{6,2},{3,7},{7,3},{8,12},{12,8},{9,1... | collective-permute-start | bytes 12582920 | tf_op jit(solution)/shard_map/ppermute | solution.py:51
  552.9 53.3 %all-to-all-start.5 = ((bf16[4,256,2048]{2,1,0:T(8,128)(2,1)}), bf16[4,256,2048]{2,1,0:T(8,128)(2,1)}, u32[]{:S(2)}, u32[]{:S(2)}) async-start(bf16[4,256,2048]{2,1,0:T(8,128)(2,1)} %bitcast.219), calls=%async_computation.6 | async-start | bytes 8388608 | tf_op jit(solution)/shard_map/all_to_all | solution.py:68
  557.9 143.8 %reduce-scatter.8.cloned.1.call-start = ((), (), s32[]{:S(2)}) async-start(), calls=%async_computation.19 | async-start | bytes 5242880 | tf_op jit(solution)/shard_map/reduce_scatter | solution.py:181
  619.1 26.7 %collective-permute-start.33 = (bf16[1024,2048]{1,0:T(8,128)(2,1)}, bf16[1024,2048]{1,0:T(8,128)(2,1)}, u32[]{:S(2)}, u32[]{:S(2)}) collective-permute-start(bf16[1024,2048]{1,0:T(8,128)(2,1)} %shard_map.246), channel_id=1, source_target_pairs={{0,4},{4,0},{1,5},{5,1},{2,6},{6,2},{3,7},{7,3},{8,12},{12,8},{9,1... | collective-permute-start | bytes 12582920 | tf_op jit(solution)/shard_map/ppermute | solution.py:51
  626.8 19.0 %all-to-all-start.6 = ((bf16[8,64,1024]{2,1,0:T(8,128)(2,1)}), bf16[8,64,1024]{2,1,0:T(8,128)(2,1)S(1)}, u32[]{:S(2)}, u32[]{:S(2)}) async-start(bf16[8,64,1024]{2,1,0:T(8,128)(2,1)} %bitcast.253), calls=%async_computation.8 | async-start | bytes 2097152 | tf_op jit(solution)/shard_map/all_to_all | solution.py:68
  652.1 26.3 %collective-permute-start.34 = (bf16[256,2048]{1,0:T(8,128)(2,1)}, bf16[256,2048]{1,0:T(8,128)(2,1)S(1)}, u32[]{:S(2)}, u32[]{:S(2)}) collective-permute-start(bf16[256,2048]{1,0:T(8,128)(2,1)} %get-tuple-element.430), channel_id=1, source_target_pairs={{0,8},{8,0},{16,24},{24,16},{1,9},{9,1},{17,25},{25,17},{2,10},{10... | collective-permute-start | bytes 3145736 | tf_op jit(solution)/shard_map/ppermute | solution.py:47
  653.7 52.8 %all-to-all-start.7 = ((bf16[4,64,2048]{2,1,0:T(8,128)(2,1)}), bf16[4,64,2048]{2,1,0:T(8,128)(2,1)S(1)}, u32[]{:S(2)}, u32[]{:S(2)}) async-start(bf16[4,64,2048]{2,1,0:T(8,128)(2,1)} %bitcast.75), calls=%async_computation.10 | async-start | bytes 2097152 | tf_op jit(solution)/shard_map/all_to_all | solution.py:68
  657.3 49.3 %collective-permute-start.35 = (bf16[256,2048]{1,0:T(8,128)(2,1)}, bf16[256,2048]{1,0:T(8,128)(2,1)}, u32[]{:S(2)}, u32[]{:S(2)}) collective-permute-start(bf16[256,2048]{1,0:T(8,128)(2,1)} %get-tuple-element.429), channel_id=1, source_target_pairs={{0,16},{8,24},{16,0},{24,8},{1,17},{9,25},{17,1},{25,9},{2,18},{10... | collective-permute-start | bytes 3145736 | tf_op jit(solution)/shard_map/ppermute | solution.py:47
  658.0 48.6 %collective-permute-start.36 = (bf16[256,2048]{1,0:T(8,128)(2,1)}, bf16[256,2048]{1,0:T(8,128)(2,1)}, u32[]{:S(2)}, u32[]{:S(2)}) collective-permute-start(bf16[256,2048]{1,0:T(8,128)(2,1)} %get-tuple-element.428), channel_id=1, source_target_pairs={{0,24},{8,16},{16,8},{24,0},{1,25},{9,17},{17,9},{25,1},{2,26},{10... | collective-permute-start | bytes 3145736 | tf_op jit(solution)/shard_map/ppermute | solution.py:47
  712.4 52.7 %collective-permute-start.37 = (bf16[64,2048]{1,0:T(8,128)(2,1)}, bf16[64,2048]{1,0:T(8,128)(2,1)}, u32[]{:S(2)}, u32[]{:S(2)}) collective-permute-start(bf16[64,2048]{1,0:T(8,128)(2,1)} %get-tuple-element.448), channel_id=1, source_target_pairs={{0,1},{1,0},{2,3},{3,2},{4,5},{5,4},{6,7},{7,6},{8,9},{9,8},{10,11... | collective-permute-start | bytes 786440 | tf_op jit(solution)/shard_map/ppermute | solution.py:55
  717.1 48.1 %collective-permute-start.38 = (bf16[64,2048]{1,0:T(8,128)(2,1)}, bf16[64,2048]{1,0:T(8,128)(2,1)}, u32[]{:S(2)}, u32[]{:S(2)}) collective-permute-start(bf16[64,2048]{1,0:T(8,128)(2,1)} %get-tuple-element.447), channel_id=1, source_target_pairs={{0,2},{1,3},{2,0},{3,1},{4,6},{5,7},{6,4},{7,5},{8,10},{9,11},{10,... | collective-permute-start | bytes 786440 | tf_op jit(solution)/shard_map/ppermute | solution.py:55
  717.1 48.1 %collective-permute-start.39 = (bf16[64,2048]{1,0:T(8,128)(2,1)}, bf16[64,2048]{1,0:T(8,128)(2,1)}, u32[]{:S(2)}, u32[]{:S(2)}) collective-permute-start(bf16[64,2048]{1,0:T(8,128)(2,1)} %get-tuple-element.446), channel_id=1, source_target_pairs={{0,3},{1,2},{2,1},{3,0},{4,7},{5,6},{6,5},{7,4},{8,11},{9,10},{10,... | collective-permute-start | bytes 786440 | tf_op jit(solution)/shard_map/ppermute | solution.py:55
  719.6 16.4 %all-to-all-start.8 = ((bf16[8,64,768]{2,1,0:T(8,128)(2,1)}), bf16[8,64,768]{2,1,0:T(8,128)(2,1)S(1)}, u32[]{:S(2)}, u32[]{:S(2)}) async-start(bf16[8,64,768]{2,1,0:T(8,128)(2,1)} %bitcast.247), calls=%async_computation.11 | async-start | bytes 1572864 | tf_op jit(solution)/shard_map/all_to_all | solution.py:68
  768.2 40.1 %all-to-all-start.11 = ((bf16[4,64,4096]{2,1,0:T(8,128)(2,1)}), bf16[4,64,4096]{2,1,0:T(8,128)(2,1)S(1)}, u32[]{:S(2)}, u32[]{:S(2)}) async-start(bf16[4,64,4096]{2,1,0:T(8,128)(2,1)} %bitcast.223), calls=%async_computation.14 | async-start | bytes 4194304 | tf_op jit(solution)/shard_map/all_to_all | solution.py:68
  (55 other events, 936.0 us)
Sparse Core Ops, SparseCore 0:
  56.9 109.7 all-gather.8
  182.0 79.0 all-gather.4
  262.7 79.2 all-gather.6
  425.0 74.2 reduce-scatter.3
  501.5 77.2 reduce-scatter.5
  611.1 90.5 reduce-scatter.7

commit v4 on v3

--- a/solution.py
+++ b/solution.py
@@ -632,22 +632,20 @@
     grad_out = (dot_tn(held[0], grad_attn[0]) + dot_tn(held[1], grad_attn[1])).astype(BF16)
     grads, grad_out, mlp_parts = together(grads, grad_out, mlp_parts)
     term_other = terms(grads[1], w_qkv)
-    result = (residual + sum_parts(mlp_parts) + vecs[7]).astype(BF16)
     held, term_other, reduced_up = together(grads[0], term_other, reduced_up)
-    owned_up = trade_rows(reduced_up)
-    owned_up, result = together(owned_up, result)
-    result = trade(in_z_order(result), "z")
     term_own = terms(held, w_qkv)
     pieces = core_pieces(term_own, term_other)
     reduced_qkv, owned_out = scatter_pair(
         grad_qkv_weight, grad_out, qkv_weight.shape[0], p
     )
+    pieces, mlp_parts, reduced_up = together(pieces, mlp_parts, reduced_up)
     pieces = chip_exchange(pieces)
+    owned_up = trade_rows(reduced_up)
+    result = (residual + sum_parts(mlp_parts) + vecs[7]).astype(BF16)
     grads, grad_pre, pieces[1] = together(grads, grad_pre, pieces[1])
-    pieces, owned_up, reduced_qkv, result = together(pieces, owned_up, reduced_qkv, result)
+    pieces, result = together(pieces, result)
     grad_normed = add_up(pieces)
     through, gain_one_grad, shift_one_grad = norm_backward(grad_normed, hat_one, factor_one, vecs[0])
-    owned_qkv = trade_rows(reduced_qkv)
     bias_grads = [column_sum(grads[0][i]) + column_sum(grads[1][i]) for i in (0, 2)]
     up_bias_grad = column_sum(grad_pre[0]) + column_sum(grad_pre[1])
     wide = lambda v: lax.dynamic_update_slice(jnp.zeros((width,), F32), v, (p * part,))
@@ -673,7 +671,8 @@
         axis=0,
     )
     vec_parts = vector_grad.reshape(vectors.shape[0], devices, -1).transpose(1, 0, 2)
-    vec_parts, owned_qkv = together(vec_parts, owned_qkv)
+    vec_parts, reduced_qkv, owned_up = together(vec_parts, reduced_qkv, owned_up)
+    owned_qkv = trade_rows(reduced_qkv)
     owned_vec = jnp.sum(trade(vec_parts, AXES), axis=0)
 
     grad_qkv_rows = owned_qkv.reshape(GROUP, -1, 3, part).transpose(1, 2, 0, 3).reshape(qkv_weight.shape)
@@ -681,10 +680,7 @@
     squares = jnp.broadcast_to(sum(squares), (devices, 1))
     grad_norm = jnp.sqrt(jnp.sum(trade(squares, AXES)))
     back = (grad_residual + through).astype(BF16)
-    back = from_planes(back)
-    back, grad_norm = together(back, grad_norm)
-    result, back = together(result, by_chip(back))
-    both = trade(jnp.concatenate([result, back], axis=1), "chip")
+    result, back = from_planes(result), from_planes(back)
     clip_factor = jnp.minimum(1.0, hyper[4] / (grad_norm + 1e-06))
     step_float = step.astype(F32)
     fix_first = 1.0 / (1.0 - hyper[2] ** step_float)
@@ -693,6 +689,9 @@
     listed = jnp.stack(scalars)
     new_qkv, new_qkv_moments = adam_update(qkv_weight, qkv_moments, grad_qkv_rows, listed)
     out_step, new_out_moments = adam_update(out_weight, out_moments, owned_out, listed, as_step=True)
+    result, back, new_qkv, out_step, listed = together(result, back, new_qkv, out_step, listed)
+    result, back = together(by_chip(result), by_chip(back))
+    both = trade(jnp.concatenate([result, back], axis=1), "chip")
     new_up, new_up_moments = adam_update(up_weight, up_moments, owned_up, listed)
     new_down, new_down_moments = adam_update(down_weight, down_moments, owned_down, listed)
     both, new_qkv, out_step, new_up, new_down = together(both, new_qkv, out_step, new_up, new_down)

time: 827 us -> 824 us (level)
  blocking collectives: 28.6 us -> 19.4 us
    ppermute x21, waiting for transfers between devices: 140 us -> 164 us  [swap_chips(): return lax.ppermute(value, 'chip', [(q, q ^ k) for q in range(CHIPS)])]
    reduce_scatter x1, waiting for transfers between devices: 15.7 us -> 0.02 us  [scatter_pair(): mine = lax.psum_scatter(both, 'z', scatter_dimension=0, tiled=True)]
    all_to_all x2 -> x1, blocking collectives: 28.6 us -> 19.4 us  [trade(): return lax.all_to_all(value, axes, 0, 0, tiled=True)]
    ppermute x11 -> x14, starting transfers between devices: 21.3 us -> 23.1 us  [swap(): lax.ppermute(value, axis, [(i, i ^ k) for i in range(lax.axis_size(axis))])]
    ppermute x11 -> x14, waiting for transfers between devices: 38.5 us -> 38.5 us  [swap(): lax.ppermute(value, axis, [(i, i ^ k) for i in range(lax.axis_size(axis))])]
  transfers between devices with their start and end apart: 56 -> 59, of which waited for: 32 -> 32; matrix products, arithmetic and copies ran while one was open for 20% -> 20% of each run, Pallas kernels for 14% -> 14%
where the time goes in v4:
time: 824 us; the launch traced here: 815 us
  waiting for transfers between devices  337 us (41%)
  Pallas kernels  149 us (18%)
  other arithmetic  93 us (11%)
  starting transfers between devices  88.3 us (11%)
  local copies, waits for them, and re-layouts  53.7 us (7%)
  matrix products  49.1 us (6%)
  between operations  25.2 us (3%)
  blocking collectives  19.4 us (2%)
    ppermute x21, waiting for transfers between devices, swap_chips(): return lax.ppermute(value, 'chip', [(q, q ^ k) for q in range(CHIPS)])  164 us
    all_gather x1, waiting for transfers between devices, gather_pair(): full = lax.all_gather(pair[0], 'z', axis=0, tiled=False)  41.5 us
    pallas_call x3, Pallas kernels, weight_grad(): pl.pallas_call(partial(weight_kernel, len(rights)), grid=(width // tile,)...  41.3 us
    all_to_all x10, starting transfers between devices, trade(): return lax.all_to_all(value, axes, 0, 0, tiled=True)  39.7 us
    ppermute x14, waiting for transfers between devices, swap(): lax.ppermute(value, axis, [(i, i ^ k) for i in range(lax.axis_size(axis))])  38.5 us
    pallas_call x2, Pallas kernels, feed(): pl.pallas_call(feed_kernel, grid=(rows // tile,), in_specs=[wide, wide, w...  38.3 us
    all_gather x1, waiting for transfers between devices, gather_rows(): return lax.all_gather(weight, 'z', axis=0, tiled=True)  37.2 us
    all_to_all x10, waiting for transfers between devices, trade(): return lax.all_to_all(value, axes, 0, 0, tiled=True)  36.4 us
  transfers between devices with their start and end apart: 59, of which 32 were waited for; matrix products, arithmetic and copies ran while one was open for 20% of the time, Pallas kernels for 14%

profile of v4, /device:TPU:0, one launch (start us, length us, event | category | flops | bytes accessed | tf_op | source)
XLA Modules:
  0.0 814.8 jit_solution(18100679465692396762)
XLA Ops:
  7.2 19.4 %all_to_all.88 = bf16[4,64,2048]{2,1,0:T(8,128)(2,1)S(1)} all-to-all(bf16[4,64,2048]{2,1,0:T(8,128)(2,1)} %bitcast.251), channel_id=1, replica_groups=mesh['o'=1,'chip'=4,'core'=2,'z'=4] {'chip'}, dimensions={0} | all-to-all | bytes 2097152 | tf_op jit(solution)/shard_map/all_to_all | solution.py:68
  38.1 7.1 all-to-all-done.1
  47.4 9.3 %collective-permute-done.1 = bf16[64,2048]{1,0:T(8,128)(2,1)S(1)} collective-permute-done((bf16[64,2048]{1,0:T(8,128)(2,1)}, bf16[64,2048]{1,0:T(8,128)(2,1)S(1)}, u32[]{:S(2)}, u32[]{:S(2)}) %collective-permute-start.1) | collective-permute-done | bytes 262176 | tf_op jit(solution)/shard_map/ppermute | solution.py:55
  63.3 11.6 %collective-permute-done.3 = bf16[12,2048]{1,0:T(8,128)(2,1)S(1)} collective-permute-done((bf16[12,2048]{1,0:T(8,128)(2,1)S(1)}, bf16[12,2048]{1,0:T(8,128)(2,1)S(1)}, u32[]{:S(2)}, u32[]{:S(2)}) %collective-permute-start.3) | collective-permute-done | bytes 49184 | tf_op jit(solution)/shard_map/ppermute | solution.py:55
  80.8 6.2 collective-permute-start.6
  87.0 8.2 %collective-permute-done.6 = bf16[12,2048]{1,0:T(8,128)(2,1)S(1)} collective-permute-done((bf16[12,2048]{1,0:T(8,128)(2,1)S(1)}, bf16[12,2048]{1,0:T(8,128)(2,1)S(1)}, u32[]{:S(2)}, u32[]{:S(2)}) %collective-permute-start.6) | collective-permute-done | bytes 49184 | tf_op jit(solution)/shard_map/ppermute | solution.py:55
  105.8 10.5 %all-to-all-done.2 = bf16[8,64,1024]{2,1,0:T(8,128)(2,1)S(1)} async-done(((bf16[8,64,1024]{2,1,0:T(8,128)(2,1)}), bf16[8,64,1024]{2,1,0:T(8,128)(2,1)S(1)}, u32[]{:S(2)}, u32[]{:S(2)}) %all-to-all-start.2) | async-done | bytes 1048608 | tf_op jit(solution)/shard_map/all_to_all | solution.py:68
  125.2 41.5 %all-gather.9.cloned.1.call-done = bf16[2048,1024]{1,0:T(8,128)(2,1)} async-done(((bf16[512,1024]{1,0:T(8,128)(2,1)}), bf16[2048,1024]{1,0:T(8,128)(2,1)}) %all-gather.9.cloned.1.call-update) | async-done | bytes 4194320 | tf_op jit(solution)/shard_map/all_gather | solution.py:166
  182.1 7.7 add_convert_fusion.5.q_ref.k_ref.v_ref
  189.9 6.7 shard_map.237
  196.6 6.8 add_convert_fusion.4.q_ref.k_ref.v_ref
  203.4 6.5 shard_map.238
  209.8 16.8 %collective-permute-done.13 = bf16[256,2048]{1,0:T(8,128)(2,1)} collective-permute-done((bf16[256,2048]{1,0:T(8,128)(2,1)S(1)}, bf16[256,2048]{1,0:T(8,128)(2,1)}, u32[]{:S(2)}, u32[]{:S(2)}) %collective-permute-start.13) | collective-permute-done | bytes 1048608 | tf_op jit(solution)/shard_map/ppermute | solution.py:47
  227.6 4.3 convolution_convert_fusion.1
  233.3 6.1 collective-permute-done.15
  254.8 6.3 all-gather.5.cloned.1.call-done
  261.1 9.5 %collective-permute-done.16 = bf16[256,2048]{1,0:T(8,128)(2,1)S(1)} collective-permute-done((bf16[256,2048]{1,0:T(8,128)(2,1)}, bf16[256,2048]{1,0:T(8,128)(2,1)S(1)}, u32[]{:S(2)}, u32[]{:S(2)}) %collective-permute-start.16) | collective-permute-done | bytes 1048608 | tf_op jit(solution)/shard_map/ppermute | solution.py:47
  270.7 21.3 %collective-permute-done.17 = bf16[256,2048]{1,0:T(8,128)(2,1)S(1)} collective-permute-done((bf16[256,2048]{1,0:T(8,128)(2,1)}, bf16[256,2048]{1,0:T(8,128)(2,1)S(1)}, u32[]{:S(2)}, u32[]{:S(2)}) %collective-permute-start.17) | collective-permute-done | bytes 1048608 | tf_op jit(solution)/shard_map/ppermute | solution.py:47
  304.8 37.2 %all-gather.7.cloned.1.call-done.down_ref = bf16[1024,2048]{1,0:T(8,128)(2,1)} async-done(((bf16[256,2048]{1,0:T(8,128)(2,1)}), bf16[1024,2048]{1,0:T(8,128)(2,1)}) %all-gather.7.cloned.1.call-update) | async-done | bytes 4194320 | tf_op jit(solution)/shard_map/all_gather | solution.py:202
  342.0 5.5 collective-permute-done.20
  357.4 6.9 collective-permute-done.23.norm_ref.left_1
  364.3 19.2 %shard_map.239 = (bf16[1024,1024]{1,0:T(8,128)(2,1)}, bf16[1024,1024]{1,0:T(8,128)(2,1)}, bf16[1024,2048]{1,0:T(8,128)(2,1)}) custom-call(bf16[1024,2048]{1,0:T(8,128)(2,1)} %collective-permute-done.23.norm_ref.left_1, bf16[1024,2048]{1,0:T(8,128)(2,1)} %collective-permute-done.22.top_ref.refs_1_, bf16[2048,1024]{1,0:T(8,128)(2,1)} %bitcast.231, ...), custom_call_target="tpu_custom_call" | custom-call | flops 12884901888 | bytes 25165824 | tf_op jit(solution)/shard_map/pallas_call | solution.py:356
  383.6 19.1 %shard_map.240 = (bf16[1024,1024]{1,0:T(8,128)(2,1)}, bf16[1024,1024]{1,0:T(8,128)(2,1)}, bf16[1024,2048]{1,0:T(8,128)(2,1)}) custom-call(bf16[1024,2048]{1,0:T(8,128)(2,1)} %constant_dynamic-update-slice_fusion.norm_ref.left_0, bf16[1024,2048]{1,0:T(8,128)(2,1)} %pad_maximum_fusion.1.top_ref.refs_0_, bf16[2048,1024]{1,0:T(8,128)(2,1)} %bitcast.232, ...), custom_call_target="tpu_custom_call" | custom-call | flops 12884901888 | bytes 25165824 | tf_op jit(solution)/shard_map/pallas_call | solution.py:356
  410.6 14.4 %shard_map.241 = bf16[1024,2048]{1,0:T(8,128)(2,1)} custom-call(bf16[1024,1024]{1,0:T(8,128)(2,1)} %get-tuple-element.247.left_0, bf16[1024,1024]{1,0:T(8,128)(2,1)} %get-tuple-element.246.left_1, bf16[1024,2048]{1,0:T(8,128)(2,1)} %pad_maximum_fusion.1.top_ref.refs_0_, bf16[1024,2048]{1,0:T(8,128)(2,1)} %collective-permute-done.22.top_ref.refs_1_), custom_call_target="tpu_custom_call" | custom-call | flops 8589934592 | bytes 16777216 | tf_op jit(solution)/shard_map/pallas_call | solution.py:403
  428.6 14.5 %shard_map.242 = bf16[4,8,64,1024]{3,2,1,0:T(8,128)(2,1)} custom-call(bf16[1024,2048]{1,0:T(8,128)(2,1)} %constant_dynamic-update-slice_fusion.norm_ref.left_0, bf16[1024,2048]{1,0:T(8,128)(2,1)} %collective-permute-done.23.norm_ref.left_1, bf16[1024,1024]{1,0:T(8,128)(2,1)} %get-tuple-element.298.refs_0_, bf16[1024,1024]{1,0:T(8,128)(2,1)} %get-tuple-element.299.refs_1_), custom_call_target="tpu_custom_call" | custom-call | flops 8589934592 | bytes 16777216 | tf_op jit(solution)/shard_map/pallas_call | solution.py:403
  443.1 8.3 %collective-permute-done.25 = bf16[256,2048]{1,0:T(8,128)(2,1)} collective-permute-done((bf16[256,2048]{1,0:T(8,128)(2,1)}, bf16[256,2048]{1,0:T(8,128)(2,1)}, u32[]{:S(2)}, u32[]{:S(2)}) %collective-permute-start.25) | collective-permute-done | bytes 1048608 | tf_op jit(solution)/shard_map/ppermute | solution.py:47
  451.4 21.4 %collective-permute-done.26 = bf16[256,2048]{1,0:T(8,128)(2,1)} collective-permute-done((bf16[256,2048]{1,0:T(8,128)(2,1)}, bf16[256,2048]{1,0:T(8,128)(2,1)}, u32[]{:S(2)}, u32[]{:S(2)}) %collective-permute-start.26) | collective-permute-done | bytes 1048608 | tf_op jit(solution)/shard_map/ppermute | solution.py:47
  482.2 6.1 convolution_convert_fusion.3
  491.9 7.4 convolution_convert_fusion.2
  499.3 16.2 %collective-permute-done.30 = bf16[256,2048]{1,0:T(8,128)(2,1)S(1)} collective-permute-done((bf16[256,2048]{1,0:T(8,128)(2,1)}, bf16[256,2048]{1,0:T(8,128)(2,1)S(1)}, u32[]{:S(2)}, u32[]{:S(2)}) %collective-permute-start.30) | collective-permute-done | bytes 1048608 | tf_op jit(solution)/shard_map/ppermute | solution.py:47
  515.4 22.1 %collective-permute-done.29 = bf16[256,2048]{1,0:T(8,128)(2,1)} collective-permute-done((bf16[256,2048]{1,0:T(8,128)(2,1)}, bf16[256,2048]{1,0:T(8,128)(2,1)}, u32[]{:S(2)}, u32[]{:S(2)}) %collective-permute-start.29) | collective-permute-done | bytes 1048608 | tf_op jit(solution)/shard_map/ppermute | solution.py:47
  552.9 5.0 all-to-all-start.5
  562.5 8.8 %shard_map.243 = (bf16[1024,256]{1,0:T(8,128)(2,1)}, bf16[1024,256]{1,0:T(8,128)(2,1)}, bf16[1024,256]{1,0:T(8,128)(2,1)}) custom-call(s32[2]{0:T(128)} %pad_add_fusion.pos_ref, f32[2]{0:T(128)} %multiply_exponential_fusion.slope_ref, bf16[1024,768]{1,0:T(8,128)(2,1)} %add_convert_fusion.5.q_ref.k_ref.v_ref, ...), custom_call_target="tpu_custom_call" | custom-call | flops 4294967296 | bytes 7340032 | tf_op jit(solution)/shard_map/pallas_call | solution.py:319
  575.6 8.8 %shard_map.244 = (bf16[1024,256]{1,0:T(8,128)(2,1)}, bf16[1024,256]{1,0:T(8,128)(2,1)}, bf16[1024,256]{1,0:T(8,128)(2,1)}) custom-call(s32[2]{0:T(128)} %pad_add_fusion.pos_ref, f32[2]{0:T(128)} %multiply_exponential_fusion.slope_ref, bf16[1024,768]{1,0:T(8,128)(2,1)} %add_convert_fusion.4.q_ref.k_ref.v_ref, ...), custom_call_target="tpu_custom_call" | custom-call | flops 4294967296 | bytes 7340032 | tf_op jit(solution)/shard_map/pallas_call | solution.py:319
  584.3 12.5 %shard_map.245 = bf16[4,8,64,768]{3,2,1,0:T(8,128)(2,1)} custom-call(bf16[1024,2048]{1,0:T(8,128)(2,1)} %pad_maximum_fusion.left_0, bf16[1024,2048]{1,0:T(8,128)(2,1)} %collective-permute-done.11.left_1, bf16[1024,256]{1,0:T(8,128)(2,1)} %get-tuple-element.293.refs_0_, bf16[1024,256]{1,0:T(8,128)(2,1)} %get-tuple-element.294.refs_1_.refs_0_, ...), custom_call_target="tpu_custom_call" | custom-call | flops 6442450944 | bytes 14680064 | tf_op jit(solution)/shard_map/pallas_call | solution.py:403
  606.2 8.0 shard_map.246
  625.9 7.7 shard_map.247
  654.9 14.2 %collective-permute-done.34 = bf16[256,2048]{1,0:T(8,128)(2,1)} collective-permute-done((bf16[256,2048]{1,0:T(8,128)(2,1)}, bf16[256,2048]{1,0:T(8,128)(2,1)}, u32[]{:S(2)}, u32[]{:S(2)}) %collective-permute-start.34) | collective-permute-done | bytes 1048608 | tf_op jit(solution)/shard_map/ppermute | solution.py:47
  669.1 24.0 %collective-permute-done.35 = bf16[256,2048]{1,0:T(8,128)(2,1)} collective-permute-done((bf16[256,2048]{1,0:T(8,128)(2,1)}, bf16[256,2048]{1,0:T(8,128)(2,1)}, u32[]{:S(2)}, u32[]{:S(2)}) %collective-permute-start.35) | collective-permute-done | bytes 1048608 | tf_op jit(solution)/shard_map/ppermute | solution.py:47
  698.4 4.4 fusion.14
  713.6 4.8 all-to-all-start.8
  721.4 4.9 all-to-all-done.8
  726.4 4.4 all-to-all-start.7
  756.6 4.5 all-to-all-done.9
  767.5 5.5 shard_map.248
  783.9 7.6 shard_map.250
  791.5 6.4 shard_map.251
  800.3 4.8 all-to-all-done.10
  (358 shorter events, 248.9 us)
Async XLA Ops:
  32.6 134.1 %all-gather.9.cloned.1.call-start = ((), (), s32[]{:S(2)}) async-start(), calls=%async_computation.19 | async-start | bytes 5242880 | tf_op jit(solution)/shard_map/all_gather | solution.py:166
  35.2 21.6 %collective-permute-start.1 = (bf16[64,2048]{1,0:T(8,128)(2,1)}, bf16[64,2048]{1,0:T(8,128)(2,1)S(1)}, u32[]{:S(2)}, u32[]{:S(2)}) collective-permute-start(bf16[64,2048]{1,0:T(8,128)(2,1)} %get-tuple-element.485), channel_id=1, source_target_pairs={{0,2},{1,3},{2,0},{3,1},{4,6},{5,7},{6,4},{7,5},{8,10},{9,11},{10,... | collective-permute-start | bytes 786440 | tf_op jit(solution)/shard_map/ppermute | solution.py:55
  37.8 19.0 %collective-permute-start.2 = (bf16[64,2048]{1,0:T(8,128)(2,1)}, bf16[64,2048]{1,0:T(8,128)(2,1)S(1)}, u32[]{:S(2)}, u32[]{:S(2)}) collective-permute-start(bf16[64,2048]{1,0:T(8,128)(2,1)} %get-tuple-element.484), channel_id=1, source_target_pairs={{0,3},{1,2},{2,1},{3,0},{4,7},{5,6},{6,5},{7,4},{8,11},{9,10},{10,... | collective-permute-start | bytes 786440 | tf_op jit(solution)/shard_map/ppermute | solution.py:55
  56.8 40.6 %all-to-all-start.3 = ((bf16[4,64,2048]{2,1,0:T(8,128)(2,1)}), bf16[4,64,2048]{2,1,0:T(8,128)(2,1)}, u32[]{:S(2)}, u32[]{:S(2)}) async-start(bf16[4,64,2048]{2,1,0:T(8,128)(2,1)} %bitcast.14), calls=%async_computation.3 | async-start | bytes 2097152 | tf_op jit(solution)/shard_map/all_to_all | solution.py:68
  97.4 18.9 %all-to-all-start.2 = ((bf16[8,64,1024]{2,1,0:T(8,128)(2,1)}), bf16[8,64,1024]{2,1,0:T(8,128)(2,1)S(1)}, u32[]{:S(2)}, u32[]{:S(2)}) async-start(bf16[8,64,1024]{2,1,0:T(8,128)(2,1)} %copy.144), calls=%async_computation.2 | async-start | bytes 2097152 | tf_op jit(solution)/shard_map/all_to_all | solution.py:68
  117.5 54.8 %all-to-all-start.4 = ((bf16[4,64,2048]{2,1,0:T(8,128)(2,1)}), bf16[4,64,2048]{2,1,0:T(8,128)(2,1)S(1)}, u32[]{:S(2)}, u32[]{:S(2)}) async-start(bf16[4,64,2048]{2,1,0:T(8,128)(2,1)} %bitcast.18), calls=%async_computation.4 | async-start | bytes 2097152 | tf_op jit(solution)/shard_map/all_to_all | solution.py:68
  121.7 139.4 %all-gather.5.cloned.1.call-start = ((), (), s32[]{:S(2)}) async-start(), calls=%async_computation.14 | async-start | bytes 5242880 | tf_op jit(solution)/shard_map/all_gather | solution.py:570
  121.7 50.6 %collective-permute-start.8 = (bf16[256,2048]{1,0:T(8,128)(2,1)S(1)}, bf16[256,2048]{1,0:T(8,128)(2,1)}, u32[]{:S(2)}, u32[]{:S(2)}) collective-permute-start(bf16[256,2048]{1,0:T(8,128)(2,1)S(1)} %fusion.8), channel_id=1, source_target_pairs={{0,8},{8,0},{16,24},{24,16},{1,9},{9,1},{17,25},{25,17},{2,10},{10... | collective-permute-start | bytes 3145736 | tf_op jit(solution)/shard_map/ppermute | solution.py:47
  122.2 50.1 %collective-permute-start.9 = (bf16[256,2048]{1,0:T(8,128)(2,1)S(1)}, bf16[256,2048]{1,0:T(8,128)(2,1)}, u32[]{:S(2)}, u32[]{:S(2)}) collective-permute-start(bf16[256,2048]{1,0:T(8,128)(2,1)S(1)} %fusion.8), channel_id=1, source_target_pairs={{0,16},{8,24},{16,0},{24,8},{1,17},{9,25},{17,1},{25,9},{2,18},{10... | collective-permute-start | bytes 3145736 | tf_op jit(solution)/shard_map/ppermute | solution.py:47
  122.9 49.5 %collective-permute-start.10 = (bf16[256,2048]{1,0:T(8,128)(2,1)S(1)}, bf16[256,2048]{1,0:T(8,128)(2,1)}, u32[]{:S(2)}, u32[]{:S(2)}) collective-permute-start(bf16[256,2048]{1,0:T(8,128)(2,1)S(1)} %fusion.8), channel_id=1, source_target_pairs={{0,24},{8,16},{16,8},{24,0},{1,25},{9,17},{17,9},{25,1},{2,26},{10... | collective-permute-start | bytes 3145736 | tf_op jit(solution)/shard_map/ppermute | solution.py:47
  176.3 20.2 %collective-permute-start.11 = (bf16[1024,2048]{1,0:T(8,128)(2,1)}, bf16[1024,2048]{1,0:T(8,128)(2,1)}, u32[]{:S(2)}, u32[]{:S(2)}) collective-permute-start(bf16[1024,2048]{1,0:T(8,128)(2,1)} %pad_maximum_fusion.left_0), channel_id=1, source_target_pairs={{0,4},{4,0},{1,5},{5,1},{2,6},{6,2},{3,7},{7,3},{8,12},{12,8},{9,1... | collective-permute-start | bytes 12582920 | tf_op jit(solution)/shard_map/ppermute | solution.py:51
  178.3 31.5 %collective-permute-start.12 = (bf16[256,2048]{1,0:T(8,128)(2,1)S(1)}, bf16[256,2048]{1,0:T(8,128)(2,1)}, u32[]{:S(2)}, u32[]{:S(2)}) collective-permute-start(bf16[256,2048]{1,0:T(8,128)(2,1)S(1)} %pad_maximum_fusion.10), channel_id=1, source_target_pairs={{0,8},{8,0},{16,24},{24,16},{1,9},{9,1},{17,25},{25,17},{2,10},{10... | collective-permute-start | bytes 3145736 | tf_op jit(solution)/shard_map/ppermute | solution.py:47
  179.8 46.9 %collective-permute-start.13 = (bf16[256,2048]{1,0:T(8,128)(2,1)S(1)}, bf16[256,2048]{1,0:T(8,128)(2,1)}, u32[]{:S(2)}, u32[]{:S(2)}) collective-permute-start(bf16[256,2048]{1,0:T(8,128)(2,1)S(1)} %pad_maximum_fusion.10), channel_id=1, source_target_pairs={{0,16},{8,24},{16,0},{24,8},{1,17},{9,25},{17,1},{25,9},{2,18},{10... | collective-permute-start | bytes 3145736 | tf_op jit(solution)/shard_map/ppermute | solution.py:47
  181.4 46.2 %collective-permute-start.14 = (bf16[256,2048]{1,0:T(8,128)(2,1)S(1)}, bf16[256,2048]{1,0:T(8,128)(2,1)}, u32[]{:S(2)}, u32[]{:S(2)}) collective-permute-start(bf16[256,2048]{1,0:T(8,128)(2,1)S(1)} %pad_maximum_fusion.10), channel_id=1, source_target_pairs={{0,24},{8,16},{16,8},{24,0},{1,25},{9,17},{17,9},{25,1},{2,26},{10... | collective-permute-start | bytes 3145736 | tf_op jit(solution)/shard_map/ppermute | solution.py:47
  181.9 160.1 %all-gather.7.cloned.1.call-start = ((), (), s32[]{:S(2)}) async-start(), calls=%async_computation.15 | async-start | bytes 5242880 | tf_op jit(solution)/shard_map/all_gather | solution.py:202
  232.0 352.4 %reduce-scatter.4.cloned.1.call-start = ((), (), s32[]{:S(2)}) async-start(), calls=%async_computation.16 | async-start | bytes 5242880 | tf_op jit(solution)/shard_map/reduce_scatter | solution.py:209
  244.4 26.2 %collective-permute-start.16 = (bf16[256,2048]{1,0:T(8,128)(2,1)}, bf16[256,2048]{1,0:T(8,128)(2,1)S(1)}, u32[]{:S(2)}, u32[]{:S(2)}) collective-permute-start(bf16[256,2048]{1,0:T(8,128)(2,1)} %get-tuple-element.457), channel_id=1, source_target_pairs={{0,8},{8,0},{16,24},{24,16},{1,9},{9,1},{17,25},{25,17},{2,10},{10... | collective-permute-start | bytes 3145736 | tf_op jit(solution)/shard_map/ppermute | solution.py:47
  245.8 46.2 %collective-permute-start.17 = (bf16[256,2048]{1,0:T(8,128)(2,1)}, bf16[256,2048]{1,0:T(8,128)(2,1)S(1)}, u32[]{:S(2)}, u32[]{:S(2)}) collective-permute-start(bf16[256,2048]{1,0:T(8,128)(2,1)} %get-tuple-element.456), channel_id=1, source_target_pairs={{0,16},{8,24},{16,0},{24,8},{1,17},{9,25},{17,1},{25,9},{2,18},{10... | collective-permute-start | bytes 3145736 | tf_op jit(solution)/shard_map/ppermute | solution.py:47
  246.7 46.8 %collective-permute-start.18 = (bf16[256,2048]{1,0:T(8,128)(2,1)}, bf16[256,2048]{1,0:T(8,128)(2,1)}, u32[]{:S(2)}, u32[]{:S(2)}) collective-permute-start(bf16[256,2048]{1,0:T(8,128)(2,1)} %get-tuple-element.455), channel_id=1, source_target_pairs={{0,24},{8,16},{16,8},{24,0},{1,25},{9,17},{17,9},{25,1},{2,26},{10... | collective-permute-start | bytes 3145736 | tf_op jit(solution)/shard_map/ppermute | solution.py:47
  293.5 54.1 %collective-permute-start.22 = (bf16[1024,2048]{1,0:T(8,128)(2,1)}, bf16[1024,2048]{1,0:T(8,128)(2,1)}, u32[]{:S(2)}, u32[]{:S(2)}) collective-permute-start(bf16[1024,2048]{1,0:T(8,128)(2,1)} %pad_maximum_fusion.1.top_ref.refs_0_), channel_id=1, source_target_pairs={{0,4},{4,0},{1,5},{5,1},{2,6},{6,2},{3,7},{7,3},{8,12},{12,8},{9,1... | collective-permute-start | bytes 12582920 | tf_op jit(solution)/shard_map/ppermute | solution.py:51
  298.8 43.2 %collective-permute-start.19 = (bf16[256,2048]{1,0:T(8,128)(2,1)}, bf16[256,2048]{1,0:T(8,128)(2,1)}, u32[]{:S(2)}, u32[]{:S(2)}) collective-permute-start(bf16[256,2048]{1,0:T(8,128)(2,1)} %add_convert_fusion.7), channel_id=1, source_target_pairs={{0,8},{8,0},{16,24},{24,16},{1,9},{9,1},{17,25},{25,17},{2,10},{10... | collective-permute-start | bytes 3145736 | tf_op jit(solution)/shard_map/ppermute | solution.py:47
  299.6 47.9 %collective-permute-start.20 = (bf16[256,2048]{1,0:T(8,128)(2,1)}, bf16[256,2048]{1,0:T(8,128)(2,1)}, u32[]{:S(2)}, u32[]{:S(2)}) collective-permute-start(bf16[256,2048]{1,0:T(8,128)(2,1)} %add_convert_fusion.7), channel_id=1, source_target_pairs={{0,16},{8,24},{16,0},{24,8},{1,17},{9,25},{17,1},{25,9},{2,18},{10... | collective-permute-start | bytes 3145736 | tf_op jit(solution)/shard_map/ppermute | solution.py:47
  302.0 45.6 %collective-permute-start.21 = (bf16[256,2048]{1,0:T(8,128)(2,1)}, bf16[256,2048]{1,0:T(8,128)(2,1)}, u32[]{:S(2)}, u32[]{:S(2)}) collective-permute-start(bf16[256,2048]{1,0:T(8,128)(2,1)} %add_convert_fusion.7), channel_id=1, source_target_pairs={{0,24},{8,16},{16,8},{24,0},{1,25},{9,17},{17,9},{25,1},{2,26},{10... | collective-permute-start | bytes 3145736 | tf_op jit(solution)/shard_map/ppermute | solution.py:47
  383.4 19.2 %collective-permute-start.24 = (bf16[1024,2048]{1,0:T(8,128)(2,1)}, bf16[1024,2048]{1,0:T(8,128)(2,1)S(1)}, u32[]{:S(2)}, u32[]{:S(2)}) collective-permute-start(bf16[1024,2048]{1,0:T(8,128)(2,1)} %get-tuple-element.228), channel_id=1, source_target_pairs={{0,4},{4,0},{1,5},{5,1},{2,6},{6,2},{3,7},{7,3},{8,12},{12,8},{9,1... | collective-permute-start | bytes 12582920 | tf_op jit(solution)/shard_map/ppermute | solution.py:51
  425.0 189.3 %reduce-scatter.6.cloned.1.call-start = ((), (), s32[]{:S(2)}) async-start(), calls=%async_computation.17 | async-start | bytes 5242880 | tf_op jit(solution)/shard_map/reduce_scatter | solution.py:192
  425.0 26.4 %collective-permute-start.25 = (bf16[256,2048]{1,0:T(8,128)(2,1)}, bf16[256,2048]{1,0:T(8,128)(2,1)}, u32[]{:S(2)}, u32[]{:S(2)}) collective-permute-start(bf16[256,2048]{1,0:T(8,128)(2,1)} %get-tuple-element.232), channel_id=1, source_target_pairs={{0,8},{8,0},{16,24},{24,16},{1,9},{9,1},{17,25},{25,17},{2,10},{10... | collective-permute-start | bytes 3145736 | tf_op jit(solution)/shard_map/ppermute | solution.py:47
  426.4 46.4 %collective-permute-start.26 = (bf16[256,2048]{1,0:T(8,128)(2,1)}, bf16[256,2048]{1,0:T(8,128)(2,1)}, u32[]{:S(2)}, u32[]{:S(2)}) collective-permute-start(bf16[256,2048]{1,0:T(8,128)(2,1)} %get-tuple-element.233), channel_id=1, source_target_pairs={{0,16},{8,24},{16,0},{24,8},{1,17},{9,25},{17,1},{25,9},{2,18},{10... | collective-permute-start | bytes 3145736 | tf_op jit(solution)/shard_map/ppermute | solution.py:47
  427.3 47.1 %collective-permute-start.27 = (bf16[256,2048]{1,0:T(8,128)(2,1)}, bf16[256,2048]{1,0:T(8,128)(2,1)}, u32[]{:S(2)}, u32[]{:S(2)}) collective-permute-start(bf16[256,2048]{1,0:T(8,128)(2,1)} %get-tuple-element.234), channel_id=1, source_target_pairs={{0,24},{8,16},{16,8},{24,0},{1,25},{9,17},{17,9},{25,1},{2,26},{10... | collective-permute-start | bytes 3145736 | tf_op jit(solution)/shard_map/ppermute | solution.py:47
  488.3 52.8 %collective-permute-start.31 = (bf16[1024,2048]{1,0:T(8,128)(2,1)}, bf16[1024,2048]{1,0:T(8,128)(2,1)}, u32[]{:S(2)}, u32[]{:S(2)}) collective-permute-start(bf16[1024,2048]{1,0:T(8,128)(2,1)} %convolution_convert_fusion.3), channel_id=1, source_target_pairs={{0,4},{4,0},{1,5},{5,1},{2,6},{6,2},{3,7},{7,3},{8,12},{12,8},{9,1... | collective-permute-start | bytes 12582920 | tf_op jit(solution)/shard_map/ppermute | solution.py:51
  488.3 27.1 %collective-permute-start.30 = (bf16[256,2048]{1,0:T(8,128)(2,1)}, bf16[256,2048]{1,0:T(8,128)(2,1)S(1)}, u32[]{:S(2)}, u32[]{:S(2)}) collective-permute-start(bf16[256,2048]{1,0:T(8,128)(2,1)} %get-tuple-element.297), channel_id=1, source_target_pairs={{0,24},{8,16},{16,8},{24,0},{1,25},{9,17},{17,9},{25,1},{2,26},{10... | collective-permute-start | bytes 3145736 | tf_op jit(solution)/shard_map/ppermute | solution.py:47
  490.1 47.5 %collective-permute-start.29 = (bf16[256,2048]{1,0:T(8,128)(2,1)}, bf16[256,2048]{1,0:T(8,128)(2,1)}, u32[]{:S(2)}, u32[]{:S(2)}) collective-permute-start(bf16[256,2048]{1,0:T(8,128)(2,1)} %get-tuple-element.297), channel_id=1, source_target_pairs={{0,16},{8,24},{16,0},{24,8},{1,17},{9,25},{17,1},{25,9},{2,18},{10... | collective-permute-start | bytes 3145736 | tf_op jit(solution)/shard_map/ppermute | solution.py:47
  490.6 47.0 %collective-permute-start.28 = (bf16[256,2048]{1,0:T(8,128)(2,1)}, bf16[256,2048]{1,0:T(8,128)(2,1)}, u32[]{:S(2)}, u32[]{:S(2)}) collective-permute-start(bf16[256,2048]{1,0:T(8,128)(2,1)} %get-tuple-element.297), channel_id=1, source_target_pairs={{0,8},{8,0},{16,24},{24,16},{1,9},{9,1},{17,25},{25,17},{2,10},{10... | collective-permute-start | bytes 3145736 | tf_op jit(solution)/shard_map/ppermute | solution.py:47
  547.8 23.5 %collective-permute-start.32 = (bf16[1024,2048]{1,0:T(8,128)(2,1)}, bf16[1024,2048]{1,0:T(8,128)(2,1)}, u32[]{:S(2)}, u32[]{:S(2)}) collective-permute-start(bf16[1024,2048]{1,0:T(8,128)(2,1)} %pad_maximum_fusion.2), channel_id=1, source_target_pairs={{0,4},{4,0},{1,5},{5,1},{2,6},{6,2},{3,7},{7,3},{8,12},{12,8},{9,1... | collective-permute-start | bytes 12582920 | tf_op jit(solution)/shard_map/ppermute | solution.py:51
  552.9 53.3 %all-to-all-start.5 = ((bf16[4,256,2048]{2,1,0:T(8,128)(2,1)}), bf16[4,256,2048]{2,1,0:T(8,128)(2,1)}, u32[]{:S(2)}, u32[]{:S(2)}) async-start(bf16[4,256,2048]{2,1,0:T(8,128)(2,1)} %bitcast.220), calls=%async_computation.6 | async-start | bytes 8388608 | tf_op jit(solution)/shard_map/all_to_all | solution.py:68
  557.9 152.6 %reduce-scatter.8.cloned.1.call-start = ((), (), s32[]{:S(2)}) async-start(), calls=%async_computation.18 | async-start | bytes 5242880 | tf_op jit(solution)/shard_map/reduce_scatter | solution.py:181
  614.3 19.3 %collective-permute-start.33 = (bf16[1024,2048]{1,0:T(8,128)(2,1)}, bf16[1024,2048]{1,0:T(8,128)(2,1)}, u32[]{:S(2)}, u32[]{:S(2)}) collective-permute-start(bf16[1024,2048]{1,0:T(8,128)(2,1)} %shard_map.246), channel_id=1, source_target_pairs={{0,4},{4,0},{1,5},{5,1},{2,6},{6,2},{3,7},{7,3},{8,12},{12,8},{9,1... | collective-permute-start | bytes 12582920 | tf_op jit(solution)/shard_map/ppermute | solution.py:51
  642.8 26.3 %collective-permute-start.34 = (bf16[256,2048]{1,0:T(8,128)(2,1)}, bf16[256,2048]{1,0:T(8,128)(2,1)}, u32[]{:S(2)}, u32[]{:S(2)}) collective-permute-start(bf16[256,2048]{1,0:T(8,128)(2,1)} %get-tuple-element.283), channel_id=1, source_target_pairs={{0,8},{8,0},{16,24},{24,16},{1,9},{9,1},{17,25},{25,17},{2,10},{10... | collective-permute-start | bytes 3145736 | tf_op jit(solution)/shard_map/ppermute | solution.py:47
  644.3 48.8 %collective-permute-start.35 = (bf16[256,2048]{1,0:T(8,128)(2,1)}, bf16[256,2048]{1,0:T(8,128)(2,1)}, u32[]{:S(2)}, u32[]{:S(2)}) collective-permute-start(bf16[256,2048]{1,0:T(8,128)(2,1)} %get-tuple-element.285), channel_id=1, source_target_pairs={{0,16},{8,24},{16,0},{24,8},{1,17},{9,25},{17,1},{25,9},{2,18},{10... | collective-permute-start | bytes 3145736 | tf_op jit(solution)/shard_map/ppermute | solution.py:47
  644.8 48.3 %collective-permute-start.36 = (bf16[256,2048]{1,0:T(8,128)(2,1)}, bf16[256,2048]{1,0:T(8,128)(2,1)}, u32[]{:S(2)}, u32[]{:S(2)}) collective-permute-start(bf16[256,2048]{1,0:T(8,128)(2,1)} %get-tuple-element.286), channel_id=1, source_target_pairs={{0,24},{8,16},{16,8},{24,0},{1,25},{9,17},{17,9},{25,1},{2,26},{10... | collective-permute-start | bytes 3145736 | tf_op jit(solution)/shard_map/ppermute | solution.py:47
  647.5 65.2 %all-to-all-start.6 = ((bf16[8,64,1024]{2,1,0:T(8,128)(2,1)}), bf16[8,64,1024]{2,1,0:T(8,128)(2,1)S(1)}, u32[]{:S(2)}, u32[]{:S(2)}) async-start(bf16[8,64,1024]{2,1,0:T(8,128)(2,1)} %bitcast.252), calls=%async_computation.9 | async-start | bytes 2097152 | tf_op jit(solution)/shard_map/all_to_all | solution.py:68
  694.0 43.7 %collective-permute-start.37 = (bf16[64,2048]{1,0:T(8,128)(2,1)}, bf16[64,2048]{1,0:T(8,128)(2,1)}, u32[]{:S(2)}, u32[]{:S(2)}) collective-permute-start(bf16[64,2048]{1,0:T(8,128)(2,1)} %get-tuple-element.478), channel_id=1, source_target_pairs={{0,1},{1,0},{2,3},{3,2},{4,5},{5,4},{6,7},{7,6},{8,9},{9,8},{10,11... | collective-permute-start | bytes 786440 | tf_op jit(solution)/shard_map/ppermute | solution.py:55
  694.0 78.9 %collective-permute-start.38 = (bf16[64,2048]{1,0:T(8,128)(2,1)}, bf16[64,2048]{1,0:T(8,128)(2,1)}, u32[]{:S(2)}, u32[]{:S(2)}) collective-permute-start(bf16[64,2048]{1,0:T(8,128)(2,1)} %get-tuple-element.477), channel_id=1, source_target_pairs={{0,2},{1,3},{2,0},{3,1},{4,6},{5,7},{6,4},{7,5},{8,10},{9,11},{10,... | collective-permute-start | bytes 786440 | tf_op jit(solution)/shard_map/ppermute | solution.py:55
  695.3 77.6 %collective-permute-start.39 = (bf16[64,2048]{1,0:T(8,128)(2,1)}, bf16[64,2048]{1,0:T(8,128)(2,1)}, u32[]{:S(2)}, u32[]{:S(2)}) collective-permute-start(bf16[64,2048]{1,0:T(8,128)(2,1)} %get-tuple-element.476), channel_id=1, source_target_pairs={{0,3},{1,2},{2,1},{3,0},{4,7},{5,6},{6,5},{7,4},{8,11},{9,10},{10,... | collective-permute-start | bytes 786440 | tf_op jit(solution)/shard_map/ppermute | solution.py:55
  726.4 17.0 %all-to-all-start.7 = ((bf16[8,64,768]{2,1,0:T(8,128)(2,1)}), bf16[8,64,768]{2,1,0:T(8,128)(2,1)}, u32[]{:S(2)}, u32[]{:S(2)}) async-start(bf16[8,64,768]{2,1,0:T(8,128)(2,1)} %bitcast.246), calls=%async_computation.10 | async-start | bytes 1572864 | tf_op jit(solution)/shard_map/all_to_all | solution.py:68
  731.8 41.2 %collective-permute-start.40 = (bf16[64,2048]{1,0:T(8,128)(2,1)}, bf16[64,2048]{1,0:T(8,128)(2,1)S(1)}, u32[]{:S(2)}, u32[]{:S(2)}) collective-permute-start(bf16[64,2048]{1,0:T(8,128)(2,1)} %get-tuple-element.474), channel_id=1, source_target_pairs={{0,1},{1,0},{2,3},{3,2},{4,5},{5,4},{6,7},{7,6},{8,9},{9,8},{10,11... | collective-permute-start | bytes 786440 | tf_op jit(solution)/shard_map/ppermute | solution.py:55
  731.8 41.2 %collective-permute-start.41 = (bf16[64,2048]{1,0:T(8,128)(2,1)}, bf16[64,2048]{1,0:T(8,128)(2,1)S(1)}, u32[]{:S(2)}, u32[]{:S(2)}) collective-permute-start(bf16[64,2048]{1,0:T(8,128)(2,1)} %get-tuple-element.473), channel_id=1, source_target_pairs={{0,2},{1,3},{2,0},{3,1},{4,6},{5,7},{6,4},{7,5},{8,10},{9,11},{10,... | collective-permute-start | bytes 786440 | tf_op jit(solution)/shard_map/ppermute | solution.py:55
  737.7 35.2 %collective-permute-start.42 = (bf16[64,2048]{1,0:T(8,128)(2,1)}, bf16[64,2048]{1,0:T(8,128)(2,1)S(1)}, u32[]{:S(2)}, u32[]{:S(2)}) collective-permute-start(bf16[64,2048]{1,0:T(8,128)(2,1)} %get-tuple-element.472), channel_id=1, source_target_pairs={{0,3},{1,2},{2,1},{3,0},{4,7},{5,6},{6,5},{7,4},{8,11},{9,10},{10,... | collective-permute-start | bytes 786440 | tf_op jit(solution)/shard_map/ppermute | solution.py:55
  776.4 28.8 %all-to-all-start.10 = ((bf16[4,64,4096]{2,1,0:T(8,128)(2,1)}), bf16[4,64,4096]{2,1,0:T(8,128)(2,1)S(1)}, u32[]{:S(2)}, u32[]{:S(2)}) async-start(bf16[4,64,4096]{2,1,0:T(8,128)(2,1)} %bitcast.224), calls=%async_computation.13 | async-start | bytes 4194304 | tf_op jit(solution)/shard_map/all_to_all | solution.py:68
  (57 other events, 1059.9 us)
Sparse Core Ops, SparseCore 0:
  56.9 109.7 all-gather.8
  182.0 79.0 all-gather.4
  262.7 79.2 all-gather.6
  425.1 74.2 reduce-scatter.3
  501.6 77.2 reduce-scatter.5
  619.3 74.1 reduce-scatter.7
